TPU v7x, 512 devices: a whole 4x4x16 slice. The times are simulated.
512 devices in a mesh: dom: 32 (over x_hi, z), pan: 16 (over y, x_lo, core).
Axes of the slice: x: 4 (x_hi: 2, x_lo: 2; x = x_hi * 2 + x_lo), y: 4, z: 16, core: 2. Of those that a mesh axis runs over, the one named last changes fastest.
Arguments:
- coupling_tiles: bfloat16 [512, 8, 256, 256], P(('dom', 'pan')), may hold values from -6 to 6
- coupling_cols: int32 [512, 8], P(('dom', 'pan')), may hold values from 0 to 255, as said below
- row_blocks: int32 [512], P(('dom', 'pan')), may hold values from 0 to 15, as said below
- factor_tiles: bfloat16 [8192, 256, 256], P(('dom', 'pan')), as said below
Outputs:
- refined_tiles: bfloat16 [512, 8, 256, 256], P(('dom', 'pan'))
Inputs may be any that keep to these rules, and one draw needn't show every extreme that they name: `coupling_cols`: A row on a device of pan index p names only blocks held by pan indices p - 1, p, p + 1 of the sibling, that is values from max(p - 1, 0) * 16 to (min(p + 1, 15) + 1) * 16 - 1; every device names blocks of both neighbouring pan indices where they exist. `row_blocks`: the rows of one device name distinct blocks. `factor_tiles`: each tile is upper triangular with a positive diagonal.
All inputs are finite; a program needn't handle non-finite values.
Results may differ from a plain program's by a relative error of at most 0.0053.
Values may be sent and summed in bfloat16 or wider, within the bound.
No kernel may reach another device: no remote copies, remote signals or barrier semaphores. Data moves between devices by JAX's collectives and lax.ppermute only.
A program may use at most 64 MiB of HBM per device.

v0:
```python
import jax
import jax.numpy as jnp
from jax import lax
from jax.sharding import PartitionSpec as P


def swapped(value, axis, apart):
    mask = 2**apart
    pairs = [(source, source ^ mask) for source in range(lax.axis_size(axis))]
    return lax.ppermute(value, axis, pairs)


def with_halo(cells, sides, width):
    for axis, dim in sides:
        count = lax.axis_size(axis)
        ends = count - 1
        head = lax.slice_in_dim(cells, 0, width, axis=dim)
        tail = lax.slice_in_dim(cells, cells.shape[dim] - width, cells.shape[dim], axis=dim)
        cells = jnp.concatenate(
            [
                lax.ppermute(tail, axis, [(i, (i + 1) % count) for i in range(ends)]),
                cells,
                lax.ppermute(head, axis, [((i + 1) % count, i) for i in range(ends)]),
            ],
            axis=dim,
        )
    return cells


def on_device(coupling_tiles, coupling_cols, row_blocks, factor_tiles):
    z_row = jnp.take(factor_tiles, row_blocks, axis=0)
    left = jnp.einsum(
        "rab,rkac->rkbc", z_row, coupling_tiles, preferred_element_type=jnp.float32
    ).astype(jnp.bfloat16)
    top_bit = lax.axis_size("dom").bit_length() - 2
    local_count = factor_tiles.shape[0]
    partner = swapped(factor_tiles, "dom", top_bit)
    nearby = with_halo(partner, (("pan", 0),), local_count)
    first_block = (lax.axis_index("pan") - 1) * local_count
    picked = jnp.take(nearby, coupling_cols - first_block, axis=0)
    inner = jnp.einsum("rkab,rkbc->rkac", left, picked, preferred_element_type=jnp.float32).astype(
        jnp.bfloat16
    )
    product = jnp.einsum("rab,rkbc->rkac", z_row, inner, preferred_element_type=jnp.float32)
    return (-0.5 * product).astype(jnp.bfloat16)


def solution(mesh):
    return jax.shard_map(
        on_device,
        mesh=mesh,
        in_specs=(
            P(("dom", "pan"), None, None, None),
            P(("dom", "pan"), None),
            P(("dom", "pan")),
            P(("dom", "pan"), None, None),
        ),
        out_specs=P(("dom", "pan"), None, None, None),
        check_vma=False,
    )
```

profile of v0, /device:TPU:504, one launch (start us, length us, event | category | flops | bytes accessed | tf_op | source)
XLA Modules:
  0.0 112.7 jit_solution(11953740863518863932)
XLA Ops:
  0.0 0.0 copy-start
  0.0 5.1 %collective-permute-start = (bf16[16,256,256]{2,1,0:T(8,128)(2,1)}, bf16[16,256,256]{2,1,0:T(8,128)(2,1)S(1)}, u32[]{:S(2)}, u32[]{:S(2)}) collective-permute-start(bf16[16,256,256]{2,1,0:T(8,128)(2,1)} %param.7), channel_id=1, source_target_pairs={{0,256},{16,272},{32,288},{48,304},{64,320},{80,336},{96,352},{112... | collective-permute-start | bytes 6291464 | tf_op jit(solution)/shard_map/ppermute | solution.py:10
  5.1 46.0 %collective-permute-done = bf16[16,256,256]{2,1,0:T(8,128)(2,1)S(1)} collective-permute-done((bf16[16,256,256]{2,1,0:T(8,128)(2,1)}, bf16[16,256,256]{2,1,0:T(8,128)(2,1)S(1)}, u32[]{:S(2)}, u32[]{:S(2)}) %collective-permute-start) | collective-permute-done | bytes 2097184 | tf_op jit(solution)/shard_map/ppermute | solution.py:10
  51.1 2.1 %collective-permute-start.2 = (bf16[16,256,256]{2,1,0:T(8,128)(2,1)S(1)}, bf16[16,256,256]{2,1,0:T(8,128)(2,1)}, u32[]{:S(2)}, u32[]{:S(2)}) collective-permute-start(bf16[16,256,256]{2,1,0:T(8,128)(2,1)S(1)} %collective-permute-done), channel_id=1, source_target_pairs={{1,0},{2,1},{3,2},{4,3},{5,4},{6,5},{7,6},{8,7},{9,8},{10,9},{11,1... | collective-permute-start | bytes 6291464 | tf_op jit(solution)/shard_map/ppermute | solution.py:23
  53.2 2.2 %collective-permute-start.1 = (bf16[16,256,256]{2,1,0:T(8,128)(2,1)S(1)}, bf16[16,256,256]{2,1,0:T(8,128)(2,1)}, u32[]{:S(2)}, u32[]{:S(2)}) collective-permute-start(bf16[16,256,256]{2,1,0:T(8,128)(2,1)S(1)} %collective-permute-done), channel_id=1, source_target_pairs={{0,1},{1,2},{2,3},{3,4},{4,5},{5,6},{6,7},{7,8},{8,9},{9,10},{10,1... | collective-permute-start | bytes 6291464 | tf_op jit(solution)/shard_map/ppermute | solution.py:21
  56.1 0.9 constant_dynamic-slice_fusion
  57.0 0.1 copy.10
  57.1 0.7 and_bitcast_fusion
  57.8 38.8 %collective-permute-done.2 = bf16[16,256,256]{2,1,0:T(8,128)(2,1)} collective-permute-done((bf16[16,256,256]{2,1,0:T(8,128)(2,1)S(1)}, bf16[16,256,256]{2,1,0:T(8,128)(2,1)}, u32[]{:S(2)}, u32[]{:S(2)}) %collective-permute-start.2) | collective-permute-done | bytes 2097184 | tf_op jit(solution)/shard_map/ppermute | solution.py:23
  96.6 4.7 %collective-permute-done.1 = bf16[16,256,256]{2,1,0:T(8,128)(2,1)} collective-permute-done((bf16[16,256,256]{2,1,0:T(8,128)(2,1)S(1)}, bf16[16,256,256]{2,1,0:T(8,128)(2,1)}, u32[]{:S(2)}, u32[]{:S(2)}) %collective-permute-start.1) | collective-permute-done | bytes 2097184 | tf_op jit(solution)/shard_map/ppermute | solution.py:21
  101.3 5.5 %pad_maximum_fusion = bf16[48,256,256]{2,1,0:T(8,128)(2,1)} fusion(bf16[16,256,256]{2,1,0:T(8,128)(2,1)} %collective-permute-done.2, bf16[16,256,256]{2,1,0:T(8,128)(2,1)S(1)} %collective-permute-done, bf16[16,256,256]{2,1,0:T(8,128)(2,1)} %collective-permute-done.1), kind=kLoop, calls=%fused_computation.1 | loop fusion | flops 6291456 | bytes 12582912 | tf_op jit(solution)/shard_map/concatenate | solution.py:19
  106.7 3.4 %gather_fusion = bf16[8,256,256]{2,1,0:T(8,128)(2,1)S(1)} fusion(bf16[48,256,256]{2,1,0:T(8,128)(2,1)} %pad_maximum_fusion, s32[1024]{0:T(1024)S(1)} %pad_clamp_fusion), kind=kCustom, calls=%fused_computation | custom fusion | bytes 2097184 | tf_op jit(solution)/shard_map/jit(_take)/gather | solution.py:40
  110.1 0.0 copy-done
  110.2 0.8 convolution_convert_fusion
  110.9 0.4 fusion.1
  111.4 1.3 %copy.7 = bf16[1,8,256,256]{3,2,1,0:T(8,128)(2,1)} copy(bf16[1,8,256,256]{2,3,1,0:T(8,128)(2,1)S(1)} %fusion.1) | data formatting | bytes 2097152 | tf_op jit(solution)/shard_map/convert_element_type | solution.py:45
  (1 shorter events, 0.0 us)
Async XLA Ops:
  0.0 110.1 %copy-start = (bf16[1,8,256,256]{3,2,1,0:T(8,128)(2,1)S(1)}, bf16[1,8,256,256]{3,2,1,0:T(8,128)(2,1)}, u32[]{:S(2)}) copy-start(bf16[1,8,256,256]{3,2,1,0:T(8,128)(2,1)} %param.4) | copy-start | bytes 3145732
  0.0 51.1 %collective-permute-start = (bf16[16,256,256]{2,1,0:T(8,128)(2,1)}, bf16[16,256,256]{2,1,0:T(8,128)(2,1)S(1)}, u32[]{:S(2)}, u32[]{:S(2)}) collective-permute-start(bf16[16,256,256]{2,1,0:T(8,128)(2,1)} %param.7), channel_id=1, source_target_pairs={{0,256},{16,272},{32,288},{48,304},{64,320},{80,336},{96,352},{112... | collective-permute-start | bytes 6291464 | tf_op jit(solution)/shard_map/ppermute | solution.py:10
  51.1 45.5 %collective-permute-start.2 = (bf16[16,256,256]{2,1,0:T(8,128)(2,1)S(1)}, bf16[16,256,256]{2,1,0:T(8,128)(2,1)}, u32[]{:S(2)}, u32[]{:S(2)}) collective-permute-start(bf16[16,256,256]{2,1,0:T(8,128)(2,1)S(1)} %collective-permute-done), channel_id=1, source_target_pairs={{1,0},{2,1},{3,2},{4,3},{5,4},{6,5},{7,6},{8,7},{9,8},{10,9},{11,1... | collective-permute-start | bytes 6291464 | tf_op jit(solution)/shard_map/ppermute | solution.py:23
  53.2 48.0 %collective-permute-start.1 = (bf16[16,256,256]{2,1,0:T(8,128)(2,1)S(1)}, bf16[16,256,256]{2,1,0:T(8,128)(2,1)}, u32[]{:S(2)}, u32[]{:S(2)}) collective-permute-start(bf16[16,256,256]{2,1,0:T(8,128)(2,1)S(1)} %collective-permute-done), channel_id=1, source_target_pairs={{0,1},{1,2},{2,3},{3,4},{4,5},{5,6},{6,7},{7,8},{8,9},{9,10},{10,1... | collective-permute-start | bytes 6291464 | tf_op jit(solution)/shard_map/ppermute | solution.py:21
where the time goes:
time: 113 us
  waiting for transfers between devices  89.5 us (79%)
  starting transfers between devices  9.37 us (8%)
  other arithmetic  6.16 us (5%)
  local copies, waits for them, and re-layouts  5.73 us (5%)
  matrix products  1.21 us (1%)
    ppermute x1, waiting for transfers between devices, swapped(): return lax.ppermute(value, axis, pairs)  46 us
    ppermute x1, waiting for transfers between devices, with_halo(): lax.ppermute(head, axis, [((i + 1) % count, i) for i in range(ends)])  38.8 us
    concatenate x1, other arithmetic, with_halo(): jnp.concatenate([lax.ppermute(tail, axis, [(i, (i + 1) % count) for i in...  5.49 us
    ppermute x1, starting transfers between devices, swapped(): return lax.ppermute(value, axis, pairs)  5.05 us
    ppermute x1, waiting for transfers between devices, with_halo(): lax.ppermute(tail, axis, [(i, (i + 1) % count) for i in range(ends)])  4.68 us
    gather x1, local copies, waits for them, and re-layouts, on_device(): picked = jnp.take(nearby, coupling_cols - first_block, axis=0)  3.4 us
  transfers between devices with their start and end apart: 3, of which 3 were waited for; matrix products, arithmetic and copies ran while one was open for 1% of the time, Pallas kernels for 0%

commit v1 on v0

v1 whole, which is shorter than its diff:
```python
import functools

import jax
import jax.numpy as jnp
from jax import lax
from jax.experimental import pallas as pl
from jax.experimental.pallas import tpu as pltpu
from jax.sharding import PartitionSpec as P


def other_panel(panel, panels):
    there = panel + 2 * (panel % 2) - 1
    return there if 0 <= there < panels else panel


def slots_of(cols_ref, panel, blocks, put):
    count = cols_ref.shape[1]
    near_used = jnp.int32(0)
    far_used = jnp.int32(0)
    for k in range(count):
        col = cols_ref[0, k]
        near = (lax.div(col, 2 * blocks) == lax.div(panel, 2)) & (near_used < count - 1)
        put(k, col, near, jnp.where(near, near_used, far_used))
        near_used = near_used + near.astype(jnp.int32)
        far_used = far_used + 1 - near.astype(jnp.int32)


def pack_kernel(panels, near_cols, far_cols, own, mate, near_out, far_out, source, tiles, sems):
    blocks, width, _ = own.shape
    half = width // 2
    slots = tiles.shape[0] // 2
    me = lax.axis_index("pan")
    odd = lax.rem(me, 2)
    there = me + 2 * odd - 1
    there = jnp.where((there < 0) | (there >= panels), me, there)
    for slot in range(2 * slots):
        source[slot] = jnp.int32(0)

    def local(col):
        return lax.rem(col, blocks) + jnp.where(lax.div(col, blocks) == me, 0, blocks)

    def put_near(k, col, near, slot):
        @pl.when(near)
        def _():
            source[slot] = local(col)

    def put_far(k, col, near, slot):
        @pl.when(jnp.logical_not(near))
        def _():
            source[slots + slot] = local(col)

    slots_of(near_cols, me, blocks, put_near)
    slots_of(far_cols, there, blocks, put_far)

    for slot in range(2 * slots):
        index = source[slot]

        @pl.when(index < blocks)
        def _():
            pltpu.make_async_copy(own.at[index], tiles.at[slot], sems.at[slot]).start()

        @pl.when(index >= blocks)
        def _():
            pltpu.make_async_copy(mate.at[index - blocks], tiles.at[slot], sems.at[slot]).start()

    rows = lax.broadcasted_iota(jnp.int32, (half, half), 0)
    lanes = lax.broadcasted_iota(jnp.int32, (half, half), 1)
    line = lax.broadcasted_iota(jnp.int32, (16, half), 0)
    for out, first in ((near_out, 0), (far_out, slots)):
        diagonals = jnp.zeros((16, half), jnp.float32)
        for slot in range(slots):
            pltpu.make_async_copy(own.at[0], tiles.at[first + slot], sems.at[first + slot]).wait()
            upper = tiles[first + slot, :half, :half].astype(jnp.float32)
            lower = tiles[first + slot, half:, half:].astype(jnp.float32)
            base = slot * width
            out[base : base + half, :] = jnp.where(rows <= lanes, upper, lower.T).astype(jnp.bfloat16)
            out[base + half : base + width, :] = tiles[first + slot, :half, half:]
            diagonal = jnp.sum(jnp.where(rows == lanes, lower, 0.0), axis=0, keepdims=True)
            diagonals = jnp.where(line == slot, diagonal, diagonals)
        out[slots * width :, :] = diagonals.astype(jnp.bfloat16)


def left_kernel(block, factors, tiles, left, z_row, sem):
    copy = pltpu.make_async_copy(factors.at[block[0]], z_row, sem)
    copy.start()
    copy.wait()
    turned = z_row[...].astype(jnp.float32).T.astype(jnp.bfloat16)
    for k in range(tiles.shape[1]):
        left[k] = jnp.dot(turned, tiles[0, k], preferred_element_type=jnp.float32).astype(jnp.bfloat16)


def right_kernel(blocks, cols, near, far, left, z_row, out, z_col):
    slots = left.shape[0] - 1
    width = z_row.shape[0]
    half = width // 2
    me = lax.axis_index("pan")
    rows = lax.broadcasted_iota(jnp.int32, (half, half), 0)
    lanes = lax.broadcasted_iota(jnp.int32, (half, half), 1)
    line = lax.broadcasted_iota(jnp.int32, (16, half), 0)
    z_col[half:, :half] = jnp.zeros((half, half), jnp.bfloat16)

    def one(k, col, is_near, slot):
        def unpack(source):
            base = pl.multiple_of(slot * width, width)
            packed = source[pl.ds(base, half), :].astype(jnp.float32)
            diagonals = source[slots * width :, :].astype(jnp.float32)
            diagonal = jnp.sum(jnp.where(line == slot, diagonals, 0.0), axis=0, keepdims=True)
            z_col[:half, :half] = jnp.where(rows <= lanes, packed, 0.0).astype(jnp.bfloat16)
            z_col[:half, half:] = source[pl.ds(base + half, half), :]
            lower = jnp.where(rows < lanes, packed.T, jnp.where(rows == lanes, diagonal, 0.0))
            z_col[half:, half:] = lower.astype(jnp.bfloat16)

        @pl.when(is_near)
        def _():
            unpack(near)

        @pl.when(jnp.logical_not(is_near))
        def _():
            unpack(far)

        inner = jnp.dot(left[k], z_col[...], preferred_element_type=jnp.float32).astype(jnp.bfloat16)
        product = jnp.dot(z_row[...], inner, preferred_element_type=jnp.float32)
        out[0, k] = (-0.5 * product).astype(jnp.bfloat16)

    slots_of(cols, me, blocks, one)


VMEM = pl.BlockSpec(memory_space=pltpu.VMEM)
SMEM = pl.BlockSpec(memory_space=pltpu.SMEM)
ANY = pl.BlockSpec(memory_space=pl.ANY)


def on_device(coupling_tiles, coupling_cols, row_blocks, factor_tiles):
    doms, panels = lax.axis_size("dom"), lax.axis_size("pan")
    blocks, width, _ = factor_tiles.shape
    _, count, _, _ = coupling_tiles.shape
    half, slots = width // 2, count - 1
    limit = pltpu.CompilerParams(vmem_limit_bytes=24 * 2**20)

    def flat(dom, panel):
        return dom * panels + panel

    straight = [(dom, dom ^ (doms // 2)) for dom in range(doms)]
    across = [
        (flat(dom, panel), flat(dom ^ (doms // 2), other_panel(panel, panels)))
        for dom in range(doms)
        for panel in range(panels)
    ]
    near_cols = lax.ppermute(coupling_cols, "dom", straight)
    far_cols = lax.ppermute(coupling_cols, ("dom", "pan"), across)
    mate = lax.ppermute(factor_tiles, "pan", [(panel, panel ^ 1) for panel in range(panels)])

    message = jax.ShapeDtypeStruct((slots * width + 16, half), jnp.bfloat16)
    near, far = pl.pallas_call(
        functools.partial(pack_kernel, panels),
        out_shape=(message, message),
        in_specs=[SMEM, SMEM, ANY, ANY],
        out_specs=(VMEM, VMEM),
        scratch_shapes=[
            pltpu.SMEM((2 * slots,), jnp.int32),
            pltpu.VMEM((2 * slots, width, width), jnp.bfloat16),
            pltpu.SemaphoreType.DMA((2 * slots,)),
        ],
        compiler_params=limit,
        name="pack",
    )(near_cols, far_cols, factor_tiles, mate)
    far = lax.ppermute(far, ("dom", "pan"), across)
    near = lax.ppermute(near, "dom", straight)

    square = jax.ShapeDtypeStruct((width, width), jnp.bfloat16)
    left, z_row = pl.pallas_call(
        left_kernel,
        out_shape=(jax.ShapeDtypeStruct((count, width, width), jnp.bfloat16), square),
        in_specs=[SMEM, ANY, VMEM],
        out_specs=(VMEM, VMEM),
        scratch_shapes=[pltpu.SemaphoreType.DMA],
        compiler_params=limit,
        cost_estimate=pl.CostEstimate(
            flops=2 * count * width**3, bytes_accessed=4 * count * width**2, transcendentals=0
        ),
        name="left",
    )(row_blocks, factor_tiles, coupling_tiles)

    return pl.pallas_call(
        functools.partial(right_kernel, blocks),
        out_shape=jax.ShapeDtypeStruct(coupling_tiles.shape, jnp.bfloat16),
        in_specs=[SMEM, VMEM, VMEM, VMEM, VMEM],
        out_specs=VMEM,
        scratch_shapes=[pltpu.VMEM((width, width), jnp.bfloat16)],
        compiler_params=limit,
        name="right",
    )(coupling_cols, near, far, left, z_row)


def solution(mesh):
    return jax.shard_map(
        on_device,
        mesh=mesh,
        in_specs=(
            P(("dom", "pan"), None, None, None),
            P(("dom", "pan"), None),
            P(("dom", "pan")),
            P(("dom", "pan"), None, None),
        ),
        out_specs=P(("dom", "pan"), None, None, None),
        check_vma=False,
    )
```

time: 113 us -> 59.8 us (0.53)
  the two profiles are of different devices: /device:TPU:504 before, /device:TPU:1 now
where the time goes in v1:
time: 59.8 us; the launch traced here: 59.5 us
  waiting for transfers between devices  27 us (45%)
  starting transfers between devices  19.1 us (32%)
  Pallas kernels  11 us (18%)
  local copies, waits for them, and re-layouts  1.61 us (3%)
  between operations  0.73 us (1%)
    ppermute x1, waiting for transfers between devices, on_device(): far = lax.ppermute(far, ('dom', 'pan'), across)  15.9 us
    ppermute x1, starting transfers between devices, on_device(): lax.ppermute(factor_tiles, 'pan', [(panel, panel ^ 1) for panel in range(...  8.77 us
    ppermute x1, waiting for transfers between devices, on_device(): near = lax.ppermute(near, 'dom', straight)  6.8 us
    pallas_call x1, Pallas kernels, on_device(): pl.pallas_call(functools.partial(right_kernel, blocks), out_shape=jax.Sha...  5.53 us
    pallas_call x1, Pallas kernels, on_device(): pl.pallas_call(functools.partial(pack_kernel, panels), out_shape=(message...  4.84 us
    ppermute x1, starting transfers between devices, on_device(): near = lax.ppermute(near, 'dom', straight)  3.66 us
    ppermute x1, starting transfers between devices, on_device(): far = lax.ppermute(far, ('dom', 'pan'), across)  2.87 us
    ppermute x1, waiting for transfers between devices, on_device(): far_cols = lax.ppermute(coupling_cols, ('dom', 'pan'), across)  2.21 us
  transfers between devices with their start and end apart: 5, of which 4 were waited for; matrix products, arithmetic and copies ran while one was open for 0% of the time, Pallas kernels for 1%

profile of v1, /device:TPU:1, one launch (start us, length us, event | category | flops | bytes accessed | tf_op | source)
XLA Modules:
  0.0 59.5 jit_solution(15766889890132516162)
XLA Ops:
  0.0 8.8 %collective-permute-start.2 = (bf16[16,256,256]{2,1,0:T(8,128)(2,1)}, bf16[16,256,256]{2,1,0:T(8,128)(2,1)S(1)}, u32[]{:S(2)}, u32[]{:S(2)}) collective-permute-start(bf16[16,256,256]{2,1,0:T(8,128)(2,1)} %factors.1), channel_id=1, source_target_pairs={{0,1},{1,0},{2,3},{3,2},{4,5},{5,4},{6,7},{7,6},{8,9},{9,8},{10,11... | collective-permute-start | bytes 6291464 | tf_op jit(solution)/shard_map/ppermute | solution.py:151
  8.8 1.9 %collective-permute-start = (s32[1,8]{1,0:T(1,128)}, s32[1,8]{1,0:T(1,128)S(1)}, u32[]{:S(2)}, u32[]{:S(2)}) collective-permute-start(s32[1,8]{1,0:T(1,128)} %cols.1), channel_id=1, source_target_pairs={{0,256},{16,272},{32,288},{48,304},{64,320},{80,336},{96,352},{112... | collective-permute-start | bytes 104 | tf_op jit(solution)/shard_map/ppermute | solution.py:149
  10.7 1.9 %collective-permute-start.1 = (s32[1,8]{1,0:T(1,128)}, s32[1,8]{1,0:T(1,128)S(1)}, u32[]{:S(2)}, u32[]{:S(2)}) collective-permute-start(s32[1,8]{1,0:T(1,128)} %cols.1), channel_id=1, source_target_pairs={{0,256},{1,258},{2,257},{3,260},{4,259},{5,262},{6,261},{7,264},{8... | collective-permute-start | bytes 104 | tf_op jit(solution)/shard_map/ppermute | solution.py:150
  12.6 2.1 %collective-permute-done.near_cols = s32[1,8]{1,0:T(1,128)S(1)} collective-permute-done((s32[1,8]{1,0:T(1,128)}, s32[1,8]{1,0:T(1,128)S(1)}, u32[]{:S(2)}, u32[]{:S(2)}) %collective-permute-start) | collective-permute-done | bytes 64 | tf_op jit(solution)/shard_map/ppermute | solution.py:149
  14.7 2.2 %collective-permute-done.1.far_cols = s32[1,8]{1,0:T(1,128)S(1)} collective-permute-done((s32[1,8]{1,0:T(1,128)}, s32[1,8]{1,0:T(1,128)S(1)}, u32[]{:S(2)}, u32[]{:S(2)}) %collective-permute-start.1) | collective-permute-done | bytes 64 | tf_op jit(solution)/shard_map/ppermute | solution.py:150
  16.9 0.0 collective-permute-done.2.mate
  16.9 0.0 copy-start
  16.9 1.6 %copy-done = bf16[16,256,256]{2,1,0:T(8,128)(2,1)S(1)} copy-done((bf16[16,256,256]{2,1,0:T(8,128)(2,1)S(1)}, bf16[16,256,256]{2,1,0:T(8,128)(2,1)}, u32[]{:S(2)}) %copy-start) | copy-done | bytes 2097176
  18.5 0.0 copy-start.1
  18.5 0.0 copy-start.2
  18.5 4.8 %pack.1 = (bf16[1808,128]{1,0:T(8,128)(2,1)S(1)}, bf16[1808,128]{1,0:T(8,128)(2,1)S(1)}) custom-call(s32[1,8]{1,0:T(1,128)S(1)} %collective-permute-done.near_cols, s32[1,8]{1,0:T(1,128)S(1)} %collective-permute-done.1.far_cols, bf16[16,256,256]{2,1,0:T(8,128)(2,1)S(1)} %copy-done, bf16[16,256,256]{2,1,0:T(8,128)(2,1)S(1)} %collective-permute-done.2.mate), custom_call_target="tpu_custom_call" | custom-call | tf_op jit(solution)/shard_map/pack/pallas_call | solution.py:154
  23.4 0.0 copy-start.3
  23.4 3.7 %collective-permute-start.3 = (bf16[1808,128]{1,0:T(8,128)(2,1)S(1)}, bf16[1808,128]{1,0:T(8,128)(2,1)S(1)}, u32[]{:S(2)}, u32[]{:S(2)}) collective-permute-start(bf16[1808,128]{1,0:T(8,128)(2,1)S(1)} %get-tuple-element.9), channel_id=1, source_target_pairs={{0,256},{16,272},{32,288},{48,304},{64,320},{80,336},{96,352},{112... | collective-permute-start | bytes 1388552 | tf_op jit(solution)/shard_map/ppermute | solution.py:168
  27.0 2.9 %collective-permute-start.4 = (bf16[1808,128]{1,0:T(8,128)(2,1)S(1)}, bf16[1808,128]{1,0:T(8,128)(2,1)S(1)}, u32[]{:S(2)}, u32[]{:S(2)}) collective-permute-start(bf16[1808,128]{1,0:T(8,128)(2,1)S(1)} %get-tuple-element.10), channel_id=1, source_target_pairs={{0,256},{1,258},{2,257},{3,260},{4,259},{5,262},{6,261},{7,264},{8... | collective-permute-start | bytes 1388552 | tf_op jit(solution)/shard_map/ppermute | solution.py:167
  30.6 0.0 copy-done.1
  30.6 0.0 copy-done.2
  30.6 0.7 %left.1 = (bf16[8,256,256]{2,1,0:T(8,128)(2,1)S(1)}, bf16[256,256]{1,0:T(8,128)(2,1)S(1)}) custom-call(s32[1]{0:T(128)S(6)} %copy.5.block, bf16[16,256,256]{2,1,0:T(8,128)(2,1)S(1)} %copy-done.1, bf16[1,8,256,256]{3,2,1,0:T(8,128)(2,1)S(1)} %copy-done.2), custom_call_target="tpu_custom_call" | custom-call | flops 268435456 | bytes 2097152 | tf_op jit(solution)/shard_map/left/pallas_call | solution.py:171
  31.3 6.8 %collective-permute-done.3.near = bf16[1808,128]{1,0:T(8,128)(2,1)S(1)} collective-permute-done((bf16[1808,128]{1,0:T(8,128)(2,1)S(1)}, bf16[1808,128]{1,0:T(8,128)(2,1)S(1)}, u32[]{:S(2)}, u32[]{:S(2)}) %collective-permute-start.3) | collective-permute-done | bytes 462880 | tf_op jit(solution)/shard_map/ppermute | solution.py:168
  38.1 15.9 %collective-permute-done.4.far = bf16[1808,128]{1,0:T(8,128)(2,1)S(1)} collective-permute-done((bf16[1808,128]{1,0:T(8,128)(2,1)S(1)}, bf16[1808,128]{1,0:T(8,128)(2,1)S(1)}, u32[]{:S(2)}, u32[]{:S(2)}) %collective-permute-start.4) | collective-permute-done | bytes 462880 | tf_op jit(solution)/shard_map/ppermute | solution.py:167
  54.0 0.0 copy-done.3
  54.0 5.5 %right.1 = bf16[1,8,256,256]{3,2,1,0:T(8,128)(2,1)} custom-call(s32[1,8]{1,0:T(1,128)S(1)} %copy-done.3, bf16[1808,128]{1,0:T(8,128)(2,1)S(1)} %collective-permute-done.3.near, bf16[1808,128]{1,0:T(8,128)(2,1)S(1)} %collective-permute-done.4.far, bf16[8,256,256]{2,1,0:T(8,128)(2,1)S(1)} %get-tuple-element.11.left, bf16[256,256]{1,0:T(8,128)(2,1)S(1)} %get-tuple-element.12.z_row), custom_call_target="tpu_custom_call" | custom-call | tf_op jit(solution)/shard_map/right/pallas_call | solution.py:184
Async XLA Ops:
  0.0 16.9 %collective-permute-start.2 = (bf16[16,256,256]{2,1,0:T(8,128)(2,1)}, bf16[16,256,256]{2,1,0:T(8,128)(2,1)S(1)}, u32[]{:S(2)}, u32[]{:S(2)}) collective-permute-start(bf16[16,256,256]{2,1,0:T(8,128)(2,1)} %factors.1), channel_id=1, source_target_pairs={{0,1},{1,0},{2,3},{3,2},{4,5},{5,4},{6,7},{7,6},{8,9},{9,8},{10,11... | collective-permute-start | bytes 6291464 | tf_op jit(solution)/shard_map/ppermute | solution.py:151
  8.8 5.9 %collective-permute-start = (s32[1,8]{1,0:T(1,128)}, s32[1,8]{1,0:T(1,128)S(1)}, u32[]{:S(2)}, u32[]{:S(2)}) collective-permute-start(s32[1,8]{1,0:T(1,128)} %cols.1), channel_id=1, source_target_pairs={{0,256},{16,272},{32,288},{48,304},{64,320},{80,336},{96,352},{112... | collective-permute-start | bytes 104 | tf_op jit(solution)/shard_map/ppermute | solution.py:149
  10.7 6.2 %collective-permute-start.1 = (s32[1,8]{1,0:T(1,128)}, s32[1,8]{1,0:T(1,128)S(1)}, u32[]{:S(2)}, u32[]{:S(2)}) collective-permute-start(s32[1,8]{1,0:T(1,128)} %cols.1), channel_id=1, source_target_pairs={{0,256},{1,258},{2,257},{3,260},{4,259},{5,262},{6,261},{7,264},{8... | collective-permute-start | bytes 104 | tf_op jit(solution)/shard_map/ppermute | solution.py:150
  16.9 1.6 %copy-start = (bf16[16,256,256]{2,1,0:T(8,128)(2,1)S(1)}, bf16[16,256,256]{2,1,0:T(8,128)(2,1)}, u32[]{:S(2)}) copy-start(bf16[16,256,256]{2,1,0:T(8,128)(2,1)} %factors.1) | copy-start | bytes 6291460
  18.5 12.1 %copy-start.1 = (bf16[16,256,256]{2,1,0:T(8,128)(2,1)S(1)}, bf16[16,256,256]{2,1,0:T(8,128)(2,1)}, u32[]{:S(2)}) copy-start(bf16[16,256,256]{2,1,0:T(8,128)(2,1)} %factors.1) | copy-start | bytes 6291460
  18.5 12.1 %copy-start.2 = (bf16[1,8,256,256]{3,2,1,0:T(8,128)(2,1)S(1)}, bf16[1,8,256,256]{3,2,1,0:T(8,128)(2,1)}, u32[]{:S(2)}) copy-start(bf16[1,8,256,256]{3,2,1,0:T(8,128)(2,1)} %tiles.1) | copy-start | bytes 3145732
  23.4 30.6 %copy-start.3 = (s32[1,8]{1,0:T(1,128)S(1)}, s32[1,8]{1,0:T(1,128)}, u32[]{:S(2)}) copy-start(s32[1,8]{1,0:T(1,128)} %cols.1) | copy-start | bytes 100
  23.4 14.7 %collective-permute-start.3 = (bf16[1808,128]{1,0:T(8,128)(2,1)S(1)}, bf16[1808,128]{1,0:T(8,128)(2,1)S(1)}, u32[]{:S(2)}, u32[]{:S(2)}) collective-permute-start(bf16[1808,128]{1,0:T(8,128)(2,1)S(1)} %get-tuple-element.9), channel_id=1, source_target_pairs={{0,256},{16,272},{32,288},{48,304},{64,320},{80,336},{96,352},{112... | collective-permute-start | bytes 1388552 | tf_op jit(solution)/shard_map/ppermute | solution.py:168
  27.0 26.9 %collective-permute-start.4 = (bf16[1808,128]{1,0:T(8,128)(2,1)S(1)}, bf16[1808,128]{1,0:T(8,128)(2,1)S(1)}, u32[]{:S(2)}, u32[]{:S(2)}) collective-permute-start(bf16[1808,128]{1,0:T(8,128)(2,1)S(1)} %get-tuple-element.10), channel_id=1, source_target_pairs={{0,256},{1,258},{2,257},{3,260},{4,259},{5,262},{6,261},{7,264},{8... | collective-permute-start | bytes 1388552 | tf_op jit(solution)/shard_map/ppermute | solution.py:167

commit v2 on v0

v2 whole, which is shorter than its diff:
```python
import functools

import jax
import jax.numpy as jnp
from jax import lax
from jax.experimental import pallas as pl
from jax.experimental.pallas import tpu as pltpu
from jax.sharding import PartitionSpec as P

FAR_CHUNKS = (4, 3)
EDGE_SLOT = 4


def other_panel(panel, panels):
    there = panel + 2 * (panel % 2) - 1
    return there if 0 <= there < panels else panel


def slots_of(cols_ref, panel, panels, blocks, put):
    count = cols_ref.shape[1]
    edge = (panel == 0) | (panel == panels - 1)
    near_used = jnp.int32(0)
    far_used = jnp.where(edge, EDGE_SLOT, 0).astype(jnp.int32)
    for k in range(count):
        col = cols_ref[0, k]
        near = (lax.div(col, 2 * blocks) == lax.div(panel, 2)) & (near_used < count - 1)
        put(k, col, near, jnp.where(near, near_used, far_used))
        near_used = near_used + near.astype(jnp.int32)
        far_used = far_used + 1 - near.astype(jnp.int32)


def iotas(half):
    rows = lax.broadcasted_iota(jnp.int32, (half, half), 0)
    lanes = lax.broadcasted_iota(jnp.int32, (half, half), 1)
    return rows, lanes


def load_kernel(block, factors, own, z_row, sem, row_sem):
    copy = pltpu.make_async_copy(factors, own, sem)
    copy.start()
    row_copy = pltpu.make_async_copy(factors.at[block[0]], z_row, row_sem)
    row_copy.start()
    row_copy.wait()
    copy.wait()


def left_kernel(z_row, tiles, left):
    turned = z_row[...].astype(jnp.float32).T.astype(jnp.bfloat16)
    for k in range(tiles.shape[1]):
        left[k] = jnp.dot(turned, tiles[0, k], preferred_element_type=jnp.float32).astype(jnp.bfloat16)


def send_kernel(near_wanted, panels, firsts, cols, own, mate, *rest):
    outs, source = rest[:-1], rest[-1]
    blocks, width, _ = own.shape
    half = width // 2
    me = lax.axis_index("pan")
    there = me + 2 * lax.rem(me, 2) - 1
    asker = me if near_wanted else jnp.where((there < 0) | (there >= panels), me, there)
    total = source.shape[0] - 1
    for slot in range(total):
        source[slot] = jnp.int32(0)

    def put(k, col, near, slot):
        local = lax.rem(col, blocks) + jnp.where(lax.div(col, blocks) == me, 0, blocks)
        source[jnp.where(near == near_wanted, slot, total)] = local

    slots_of(cols, asker, panels, blocks, put)

    rows, lanes = iotas(half)
    line = lax.broadcasted_iota(jnp.int32, (16, half), 0)
    for out, first, last in zip(outs, firsts[:-1], firsts[1:]):
        found = jnp.zeros((16, half), jnp.float32)
        for slot in range(first, last):
            index = source[slot]
            mine = index < blocks
            block = jnp.where(mine, index, index - blocks)

            def part(rows_of, lanes_of):
                return jnp.where(mine, own[block, rows_of, lanes_of], mate[block, rows_of, lanes_of])

            head, tail = slice(0, half), slice(half, width)
            upper = part(head, head).astype(jnp.float32)
            lower = part(tail, tail).astype(jnp.float32)
            base = (slot - first) * width
            triangle = jnp.where(rows <= lanes, upper, lower.T)
            out[base : base + half, :] = triangle.astype(jnp.bfloat16)
            out[base + half : base + width, :] = part(head, tail)
            diagonal = jnp.sum(jnp.where(rows == lanes, lower, 0.0), axis=0, keepdims=True)
            found = jnp.where(line == slot - first, diagonal, found)
        out[(last - first) * width :, :] = found.astype(jnp.bfloat16)


def right_kernel(near_wanted, panels, blocks, first, cols, message, left, z_row, *rest):
    out, results, places, sems = rest[-4:]
    slots, width, _ = results.shape
    half = width // 2
    me = lax.axis_index("pan")
    for slot in range(slots):
        places[slot] = jnp.int32(-1)

    def put(k, col, near, slot):
        here = (near == near_wanted) & (slot >= first) & (slot < first + slots)
        places[jnp.where(here, slot - first, slots)] = jnp.int32(k)

    slots_of(cols, me, panels, blocks, put)

    rows, lanes = iotas(half)
    diagonals = message[slots * width :, :].astype(jnp.float32)
    for slot in range(slots):
        k = places[slot]
        base = slot * width
        triangle = message[base : base + half, :].astype(jnp.float32)
        upper = jnp.where(rows <= lanes, triangle, 0.0).astype(jnp.bfloat16)
        lower = jnp.where(rows < lanes, triangle.T, jnp.where(rows == lanes, diagonals[slot : slot + 1, :], 0.0))
        lower = lower.astype(jnp.bfloat16)
        corner = message[base + half : base + width, :]
        z_col = jnp.concatenate(
            [
                jnp.concatenate([upper, corner], axis=1),
                jnp.concatenate([jnp.zeros_like(lower), lower], axis=1),
            ],
            axis=0,
        )
        inner = jnp.dot(left[jnp.maximum(k, 0)], z_col, preferred_element_type=jnp.float32)
        product = jnp.dot(z_row[...], inner.astype(jnp.bfloat16), preferred_element_type=jnp.float32)
        results[slot] = (-0.5 * product).astype(jnp.bfloat16)

        @pl.when(k >= 0)
        def _():
            pltpu.make_async_copy(results.at[slot], out.at[0, k], sems.at[slot]).start()

    for slot in range(slots):

        @pl.when(places[slot] >= 0)
        def _():
            pltpu.make_async_copy(results.at[slot], out.at[0, 0], sems.at[slot]).wait()


VMEM = pl.BlockSpec(memory_space=pltpu.VMEM)
SMEM = pl.BlockSpec(memory_space=pltpu.SMEM)
HBM = pl.BlockSpec(memory_space=pltpu.HBM)


def on_device(coupling_tiles, coupling_cols, row_blocks, factor_tiles):
    doms, panels = lax.axis_size("dom"), lax.axis_size("pan")
    blocks, width, _ = factor_tiles.shape
    _, count, _, _ = coupling_tiles.shape
    half, slots = width // 2, count - 1
    limit = pltpu.CompilerParams(vmem_limit_bytes=32 * 2**20)
    bf16 = lambda *shape: jax.ShapeDtypeStruct(shape, jnp.bfloat16)

    def flat(dom, panel):
        return dom * panels + panel

    straight = [(dom, dom ^ (doms // 2)) for dom in range(doms)]
    ends = (0, panels - 1)

    def across(with_ends):
        return [
            (flat(dom, panel), flat(dom ^ (doms // 2), other_panel(panel, panels)))
            for dom in range(doms)
            for panel in range(panels)
            if with_ends or panel not in ends
        ]

    mate = lax.ppermute(factor_tiles, "pan", [(panel, panel ^ 1) for panel in range(panels)])
    near_cols = lax.ppermute(coupling_cols, "dom", straight)
    far_cols = lax.ppermute(coupling_cols, ("dom", "pan"), across(True))

    own, z_row = pl.pallas_call(
        load_kernel,
        out_shape=(bf16(blocks, width, width), bf16(width, width)),
        in_specs=[SMEM, HBM],
        out_specs=(VMEM,) * 2,
        scratch_shapes=[pltpu.SemaphoreType.DMA] * 2,
        compiler_params=limit,
        name="load",
    )(row_blocks, factor_tiles)

    def filled(near_wanted, sizes, cols):
        firsts = [sum(sizes[:i]) for i in range(len(sizes) + 1)]
        return pl.pallas_call(
            functools.partial(send_kernel, near_wanted, panels, firsts),
            out_shape=tuple(bf16(size * width + 16, half) for size in sizes),
            in_specs=[SMEM, VMEM, VMEM],
            out_specs=(VMEM,) * len(sizes),
            scratch_shapes=[pltpu.SMEM((slots + 1,), jnp.int32)],
            compiler_params=limit,
            name="fill_near" if near_wanted else "fill_far",
        )(cols, own, mate)

    (near,) = filled(True, (slots,), near_cols)
    near, far_cols = lax.optimization_barrier((near, far_cols))
    near = lax.ppermute(near, "dom", straight)
    far = filled(False, FAR_CHUNKS, far_cols)
    first = 0
    messages = [(True, 0, slots, near)]
    for size, message in zip(FAR_CHUNKS, far):
        with_ends = first <= EDGE_SLOT < first + size
        message = lax.ppermute(message, ("dom", "pan"), across(with_ends))
        messages.append((False, first, size, message))
        first += size

    left = pl.pallas_call(
        left_kernel,
        out_shape=bf16(count, width, width),
        in_specs=[VMEM, VMEM],
        out_specs=VMEM,
        compiler_params=limit,
        name="left",
    )(z_row, coupling_tiles)

    out = None
    for near_wanted, first, size, message in messages:
        out = pl.pallas_call(
            functools.partial(right_kernel, near_wanted, panels, blocks, first),
            out_shape=bf16(*coupling_tiles.shape),
            in_specs=[SMEM, VMEM, VMEM, VMEM] + ([] if out is None else [HBM]),
            out_specs=HBM,
            scratch_shapes=[
                pltpu.VMEM((size, width, width), jnp.bfloat16),
                pltpu.SMEM((size + 1,), jnp.int32),
                pltpu.SemaphoreType.DMA((size,)),
            ],
            input_output_aliases={} if out is None else {4: 0},
            compiler_params=limit,
            name="right_near" if near_wanted else "right_far",
        )(coupling_cols, message, left, z_row, *(() if out is None else (out,)))
    return out


def solution(mesh):
    return jax.shard_map(
        on_device,
        mesh=mesh,
        in_specs=(
            P(("dom", "pan"), None, None, None),
            P(("dom", "pan"), None),
            P(("dom", "pan")),
            P(("dom", "pan"), None, None),
        ),
        out_specs=P(("dom", "pan"), None, None, None),
        check_vma=False,
    )
```

time: 113 us -> 47.6 us (0.42)
  the two profiles are of different devices: /device:TPU:504 before, /device:TPU:1 now
where the time goes in v2:
time: 47.6 us; the launch traced here: 47.3 us
  starting transfers between devices  23.5 us (49%)
  waiting for transfers between devices  13.4 us (28%)
  Pallas kernels  7.94 us (17%)
  local copies, waits for them, and re-layouts  1.6 us (3%)
  between operations  0.78 us (2%)
    ppermute x2, waiting for transfers between devices, on_device(): message = lax.ppermute(message, ('dom', 'pan'), across(with_ends))  10.7 us
    ppermute x1, starting transfers between devices, on_device(): lax.ppermute(factor_tiles, 'pan', [(panel, panel ^ 1) for panel in range(...  8.77 us
    ppermute x2, starting transfers between devices, on_device(): message = lax.ppermute(message, ('dom', 'pan'), across(with_ends))  7.33 us
    pallas_call x3, Pallas kernels, on_device(): pl.pallas_call(functools.partial(right_kernel, near_wanted, panels, block...  5.48 us
    ppermute x1, starting transfers between devices, on_device(): near = lax.ppermute(near, 'dom', straight)  3.59 us
    ppermute x1, starting transfers between devices, on_device(): far_cols = lax.ppermute(coupling_cols, ('dom', 'pan'), across(True))  1.92 us
    ppermute x1, starting transfers between devices, on_device(): near_cols = lax.ppermute(coupling_cols, 'dom', straight)  1.92 us
    pallas_call x2, Pallas kernels, filled(): pl.pallas_call(functools.partial(send_kernel, near_wanted, panels, firsts...  1.66 us
  transfers between devices with their start and end apart: 6, of which 4 were waited for; matrix products, arithmetic and copies ran while one was open for 0% of the time, Pallas kernels for 13%

profile of v2, /device:TPU:1, one launch (start us, length us, event | category | flops | bytes accessed | tf_op | source)
XLA Modules:
  0.0 47.3 jit_solution(2735110507114644671)
XLA Ops:
  0.0 8.8 %collective-permute-start.1 = (bf16[16,256,256]{2,1,0:T(8,128)(2,1)}, bf16[16,256,256]{2,1,0:T(8,128)(2,1)S(1)}, u32[]{:S(2)}, u32[]{:S(2)}) collective-permute-start(bf16[16,256,256]{2,1,0:T(8,128)(2,1)} %factors.1), channel_id=1, source_target_pairs={{0,1},{1,0},{2,3},{3,2},{4,5},{5,4},{6,7},{7,6},{8,9},{9,8},{10,11... | collective-permute-start | bytes 6291464 | tf_op jit(solution)/shard_map/ppermute | solution.py:167
  8.8 1.9 %collective-permute-start.2 = (s32[1,8]{1,0:T(1,128)}, s32[1,8]{1,0:T(1,128)S(1)}, u32[]{:S(2)}, u32[]{:S(2)}) collective-permute-start(s32[1,8]{1,0:T(1,128)} %cols.5), channel_id=1, source_target_pairs={{0,256},{1,258},{2,257},{3,260},{4,259},{5,262},{6,261},{7,264},{8... | collective-permute-start | bytes 104 | tf_op jit(solution)/shard_map/ppermute | solution.py:169
  10.7 1.9 %collective-permute-start = (s32[1,8]{1,0:T(1,128)}, s32[1,8]{1,0:T(1,128)S(1)}, u32[]{:S(2)}, u32[]{:S(2)}) collective-permute-start(s32[1,8]{1,0:T(1,128)} %cols.5), channel_id=1, source_target_pairs={{0,256},{16,272},{32,288},{48,304},{64,320},{80,336},{96,352},{112... | collective-permute-start | bytes 104 | tf_op jit(solution)/shard_map/ppermute | solution.py:168
  13.3 0.0 copy-start
  13.3 1.6 %copy-done = bf16[16,256,256]{2,1,0:T(8,128)(2,1)S(1)} copy-done((bf16[16,256,256]{2,1,0:T(8,128)(2,1)S(1)}, bf16[16,256,256]{2,1,0:T(8,128)(2,1)}, u32[]{:S(2)}) %copy-start) | copy-done | bytes 2097176
  14.9 0.3 load.1
  15.2 1.4 %collective-permute-done.cols = s32[1,8]{1,0:T(1,128)S(1)} collective-permute-done((s32[1,8]{1,0:T(1,128)}, s32[1,8]{1,0:T(1,128)S(1)}, u32[]{:S(2)}, u32[]{:S(2)}) %collective-permute-start) | collective-permute-done | bytes 64 | tf_op jit(solution)/shard_map/ppermute | solution.py:168
  16.6 0.0 collective-permute-done.1.mate
  16.6 0.8 %fill_near.1 = bf16[1808,128]{1,0:T(8,128)(2,1)S(1)} custom-call(s32[1,8]{1,0:T(1,128)S(1)} %collective-permute-done.cols, bf16[16,256,256]{2,1,0:T(8,128)(2,1)S(1)} %get-tuple-element.11.own, bf16[16,256,256]{2,1,0:T(8,128)(2,1)S(1)} %collective-permute-done.1.mate), custom_call_target="tpu_custom_call" | custom-call | tf_op jit(solution)/shard_map/fill_near/pallas_call | solution.py:183
  17.5 0.0 copy-start.1
  17.5 0.0 collective-permute-done.2.cols
  17.5 3.6 %collective-permute-start.5 = (bf16[1808,128]{1,0:T(8,128)(2,1)S(1)}, bf16[1808,128]{1,0:T(8,128)(2,1)S(1)}, u32[]{:S(2)}, u32[]{:S(2)}) collective-permute-start(bf16[1808,128]{1,0:T(8,128)(2,1)S(1)} %fill_near.1), channel_id=1, source_target_pairs={{0,256},{16,272},{32,288},{48,304},{64,320},{80,336},{96,352},{112... | collective-permute-start | bytes 1388552 | tf_op jit(solution)/shard_map/ppermute | solution.py:195
  21.1 0.8 %fill_far.1 = (bf16[1040,128]{1,0:T(8,128)(2,1)S(1)}, bf16[784,128]{1,0:T(8,128)(2,1)S(1)}) custom-call(s32[1,8]{1,0:T(1,128)S(1)} %collective-permute-done.2.cols, bf16[16,256,256]{2,1,0:T(8,128)(2,1)S(1)} %get-tuple-element.11.own, bf16[16,256,256]{2,1,0:T(8,128)(2,1)S(1)} %collective-permute-done.1.mate), custom_call_target="tpu_custom_call" | custom-call | tf_op jit(solution)/shard_map/fill_far/pallas_call | solution.py:183
  21.9 0.0 copy-start.2
  21.9 5.4 %collective-permute-start.4 = (bf16[1040,128]{1,0:T(8,128)(2,1)S(1)}, bf16[1040,128]{1,0:T(8,128)(2,1)S(1)}, u32[]{:S(2)}, u32[]{:S(2)}) collective-permute-start(bf16[1040,128]{1,0:T(8,128)(2,1)S(1)} %get-tuple-element.15), channel_id=1, source_target_pairs={{1,258},{2,257},{3,260},{4,259},{5,262},{6,261},{7,264},{8,263},{9... | collective-permute-start | bytes 798728 | tf_op jit(solution)/shard_map/ppermute | solution.py:201
  27.4 1.9 %collective-permute-start.3 = (bf16[784,128]{1,0:T(8,128)(2,1)S(1)}, bf16[784,128]{1,0:T(8,128)(2,1)S(1)}, u32[]{:S(2)}, u32[]{:S(2)}) collective-permute-start(bf16[784,128]{1,0:T(8,128)(2,1)S(1)} %get-tuple-element.13), channel_id=1, source_target_pairs={{0,256},{1,258},{2,257},{3,260},{4,259},{5,262},{6,261},{7,264},{8... | collective-permute-start | bytes 602120 | tf_op jit(solution)/shard_map/ppermute | solution.py:201
  29.3 0.0 copy-done.1
  29.3 0.5 %left.1 = bf16[8,256,256]{2,1,0:T(8,128)(2,1)S(1)} custom-call(bf16[256,256]{1,0:T(8,128)(2,1)S(1)} %get-tuple-element.14.z_row, bf16[1,8,256,256]{3,2,1,0:T(8,128)(2,1)S(1)} %copy-done.1), custom_call_target="tpu_custom_call" | custom-call | tf_op jit(solution)/shard_map/left/pallas_call | solution.py:205
  29.8 1.3 %collective-permute-done.5.message = bf16[1808,128]{1,0:T(8,128)(2,1)S(1)} collective-permute-done((bf16[1808,128]{1,0:T(8,128)(2,1)S(1)}, bf16[1808,128]{1,0:T(8,128)(2,1)S(1)}, u32[]{:S(2)}, u32[]{:S(2)}) %collective-permute-start.5) | collective-permute-done | bytes 462880 | tf_op jit(solution)/shard_map/ppermute | solution.py:195
  31.1 0.0 copy-done.2
  31.1 1.8 %right_near.1.rest_0_ = bf16[1,8,256,256]{3,2,1,0:T(8,128)(2,1)} custom-call(s32[1,8]{1,0:T(1,128)S(1)} %copy-done.2, bf16[1808,128]{1,0:T(8,128)(2,1)S(1)} %collective-permute-done.5.message, bf16[8,256,256]{2,1,0:T(8,128)(2,1)S(1)} %left.1, bf16[256,256]{1,0:T(8,128)(2,1)S(1)} %get-tuple-element.14.z_row), custom_call_target="tpu_custom_call" | custom-call | tf_op jit(solution)/shard_map/right_near/pallas_call | solution.py:216
  32.9 8.4 %collective-permute-done.4.message = bf16[1040,128]{1,0:T(8,128)(2,1)S(1)} collective-permute-done((bf16[1040,128]{1,0:T(8,128)(2,1)S(1)}, bf16[1040,128]{1,0:T(8,128)(2,1)S(1)}, u32[]{:S(2)}, u32[]{:S(2)}) %collective-permute-start.4) | collective-permute-done | bytes 266272 | tf_op jit(solution)/shard_map/ppermute | solution.py:201
  41.3 1.9 %right_far.2.rest_0_ = bf16[1,8,256,256]{3,2,1,0:T(8,128)(2,1)} custom-call(s32[1,8]{1,0:T(1,128)S(1)} %copy-done.2, bf16[1040,128]{1,0:T(8,128)(2,1)S(1)} %collective-permute-done.4.message, bf16[8,256,256]{2,1,0:T(8,128)(2,1)S(1)} %left.1, bf16[256,256]{1,0:T(8,128)(2,1)S(1)} %get-tuple-element.14.z_row, ...), custom_call_target="tpu_custom_call", output_to_operand_aliasing={{}: (4, {})} | custom-call | tf_op jit(solution)/shard_map/right_far/pallas_call | solution.py:216
  43.2 2.3 %collective-permute-done.3.message = bf16[784,128]{1,0:T(8,128)(2,1)S(1)} collective-permute-done((bf16[784,128]{1,0:T(8,128)(2,1)S(1)}, bf16[784,128]{1,0:T(8,128)(2,1)S(1)}, u32[]{:S(2)}, u32[]{:S(2)}) %collective-permute-start.3) | collective-permute-done | bytes 200736 | tf_op jit(solution)/shard_map/ppermute | solution.py:201
  45.5 1.8 %right_far.3 = bf16[1,8,256,256]{3,2,1,0:T(8,128)(2,1)} custom-call(s32[1,8]{1,0:T(1,128)S(1)} %copy-done.2, bf16[784,128]{1,0:T(8,128)(2,1)S(1)} %collective-permute-done.3.message, bf16[8,256,256]{2,1,0:T(8,128)(2,1)S(1)} %left.1, bf16[256,256]{1,0:T(8,128)(2,1)S(1)} %get-tuple-element.14.z_row, ...), custom_call_target="tpu_custom_call", output_to_operand_aliasing={{}: (4, {})} | custom-call | tf_op jit(solution)/shard_map/right_far/pallas_call | solution.py:216
Async XLA Ops:
  0.0 16.6 %collective-permute-start.1 = (bf16[16,256,256]{2,1,0:T(8,128)(2,1)}, bf16[16,256,256]{2,1,0:T(8,128)(2,1)S(1)}, u32[]{:S(2)}, u32[]{:S(2)}) collective-permute-start(bf16[16,256,256]{2,1,0:T(8,128)(2,1)} %factors.1), channel_id=1, source_target_pairs={{0,1},{1,0},{2,3},{3,2},{4,5},{5,4},{6,7},{7,6},{8,9},{9,8},{10,11... | collective-permute-start | bytes 6291464 | tf_op jit(solution)/shard_map/ppermute | solution.py:167
  8.8 8.7 %collective-permute-start.2 = (s32[1,8]{1,0:T(1,128)}, s32[1,8]{1,0:T(1,128)S(1)}, u32[]{:S(2)}, u32[]{:S(2)}) collective-permute-start(s32[1,8]{1,0:T(1,128)} %cols.5), channel_id=1, source_target_pairs={{0,256},{1,258},{2,257},{3,260},{4,259},{5,262},{6,261},{7,264},{8... | collective-permute-start | bytes 104 | tf_op jit(solution)/shard_map/ppermute | solution.py:169
  10.7 5.9 %collective-permute-start = (s32[1,8]{1,0:T(1,128)}, s32[1,8]{1,0:T(1,128)S(1)}, u32[]{:S(2)}, u32[]{:S(2)}) collective-permute-start(s32[1,8]{1,0:T(1,128)} %cols.5), channel_id=1, source_target_pairs={{0,256},{16,272},{32,288},{48,304},{64,320},{80,336},{96,352},{112... | collective-permute-start | bytes 104 | tf_op jit(solution)/shard_map/ppermute | solution.py:168
  13.3 1.6 %copy-start = (bf16[16,256,256]{2,1,0:T(8,128)(2,1)S(1)}, bf16[16,256,256]{2,1,0:T(8,128)(2,1)}, u32[]{:S(2)}) copy-start(bf16[16,256,256]{2,1,0:T(8,128)(2,1)} %factors.1) | copy-start | bytes 6291460
  17.5 11.8 %copy-start.1 = (bf16[1,8,256,256]{3,2,1,0:T(8,128)(2,1)S(1)}, bf16[1,8,256,256]{3,2,1,0:T(8,128)(2,1)}, u32[]{:S(2)}) copy-start(bf16[1,8,256,256]{3,2,1,0:T(8,128)(2,1)} %tiles.1) | copy-start | bytes 3145732
  17.5 13.6 %collective-permute-start.5 = (bf16[1808,128]{1,0:T(8,128)(2,1)S(1)}, bf16[1808,128]{1,0:T(8,128)(2,1)S(1)}, u32[]{:S(2)}, u32[]{:S(2)}) collective-permute-start(bf16[1808,128]{1,0:T(8,128)(2,1)S(1)} %fill_near.1), channel_id=1, source_target_pairs={{0,256},{16,272},{32,288},{48,304},{64,320},{80,336},{96,352},{112... | collective-permute-start | bytes 1388552 | tf_op jit(solution)/shard_map/ppermute | solution.py:195
  21.9 9.1 %copy-start.2 = (s32[1,8]{1,0:T(1,128)S(1)}, s32[1,8]{1,0:T(1,128)}, u32[]{:S(2)}) copy-start(s32[1,8]{1,0:T(1,128)} %cols.5) | copy-start | bytes 100
  21.9 19.4 %collective-permute-start.4 = (bf16[1040,128]{1,0:T(8,128)(2,1)S(1)}, bf16[1040,128]{1,0:T(8,128)(2,1)S(1)}, u32[]{:S(2)}, u32[]{:S(2)}) collective-permute-start(bf16[1040,128]{1,0:T(8,128)(2,1)S(1)} %get-tuple-element.15), channel_id=1, source_target_pairs={{1,258},{2,257},{3,260},{4,259},{5,262},{6,261},{7,264},{8,263},{9... | collective-permute-start | bytes 798728 | tf_op jit(solution)/shard_map/ppermute | solution.py:201
  27.4 18.1 %collective-permute-start.3 = (bf16[784,128]{1,0:T(8,128)(2,1)S(1)}, bf16[784,128]{1,0:T(8,128)(2,1)S(1)}, u32[]{:S(2)}, u32[]{:S(2)}) collective-permute-start(bf16[784,128]{1,0:T(8,128)(2,1)S(1)} %get-tuple-element.13), channel_id=1, source_target_pairs={{0,256},{1,258},{2,257},{3,260},{4,259},{5,262},{6,261},{7,264},{8... | collective-permute-start | bytes 602120 | tf_op jit(solution)/shard_map/ppermute | solution.py:201

commit v3 on v2

v3 whole, which is shorter than its diff:
```python
import functools

import jax
import jax.numpy as jnp
from jax import lax
from jax.experimental import pallas as pl
from jax.experimental.pallas import tpu as pltpu
from jax.sharding import PartitionSpec as P

NEAR, FAR, LAST = 5, 4, 3
IN_NEAR, IN_FAR, IN_LAST = range(3)


def other_panel(panel, panels):
    return panel + 2 * (panel % 2) - 1


def slots_of(cols_ref, panel, blocks, put):
    near_used = jnp.int32(0)
    far_used = jnp.int32(0)
    for k in range(cols_ref.shape[1]):
        col = cols_ref[0, k]
        near = lax.div(col, 2 * blocks) == lax.div(panel, 2)
        used = jnp.where(near, near_used, far_used)
        room = jnp.where(near, NEAR, FAR)
        direct = used < room
        message = jnp.where(direct, jnp.where(near, IN_NEAR, IN_FAR), IN_LAST)
        put(k, col, message, jnp.where(direct, used, used - room))
        near_used = near_used + near.astype(jnp.int32)
        far_used = far_used + 1 - near.astype(jnp.int32)


def iotas(half):
    rows = lax.broadcasted_iota(jnp.int32, (half, half), 0)
    lanes = lax.broadcasted_iota(jnp.int32, (half, half), 1)
    return rows, lanes


def load_kernel(block, factors, own, z_row, sem, row_sem):
    copy = pltpu.make_async_copy(factors, own, sem)
    copy.start()
    row_copy = pltpu.make_async_copy(factors.at[block[0]], z_row, row_sem)
    row_copy.start()
    row_copy.wait()
    copy.wait()


def left_kernel(z_row, tiles, left):
    turned = z_row[...].astype(jnp.float32).T.astype(jnp.bfloat16)
    for k in range(tiles.shape[1]):
        left[k] = jnp.dot(turned, tiles[0, k], preferred_element_type=jnp.float32).astype(jnp.bfloat16)


def write_slot(out, slot, found, tile_part, width):
    half = width // 2
    rows, lanes = iotas(half)
    line = lax.broadcasted_iota(jnp.int32, (16, half), 0)
    head, tail = slice(0, half), slice(half, width)
    upper = tile_part(head, head).astype(jnp.float32)
    lower = tile_part(tail, tail).astype(jnp.float32)
    base = slot * width
    out[base : base + half, :] = jnp.where(rows <= lanes, upper, lower.T).astype(jnp.bfloat16)
    out[base + half : base + width, :] = tile_part(head, tail)
    diagonal = jnp.sum(jnp.where(rows == lanes, lower, 0.0), axis=0, keepdims=True)
    return jnp.where(line == slot, diagonal, found)


def chosen(index, own, mate):
    blocks = own.shape[0]
    mine = index < blocks
    block = jnp.where(mine, index, jnp.where(index < 2 * blocks, index - blocks, 0))
    return lambda rows, lanes: jnp.where(mine, own[block, rows, lanes], mate[block, rows, lanes])


def near_kernel(cols, own, mate, out, source):
    blocks, width, _ = own.shape
    me = lax.axis_index("pan")
    for slot in range(NEAR):
        source[slot] = jnp.int32(0)

    def put(k, col, message, slot):
        local = lax.rem(col, blocks) + jnp.where(lax.div(col, blocks) == me, 0, blocks)
        source[jnp.where(message == IN_NEAR, slot, NEAR)] = local

    slots_of(cols, me, blocks, put)
    found = jnp.zeros((16, width // 2), jnp.float32)
    for slot in range(NEAR):
        found = write_slot(out, slot, found, chosen(source[slot], own, mate), width)
    out[NEAR * width :, :] = found.astype(jnp.bfloat16)


def far_kernel(cols, own, far_out, relay_out, source):
    blocks, width, _ = own.shape
    relayed = relay_out.shape[0] // width
    total = FAR + relayed
    me = lax.axis_index("pan")
    there = me + 2 * lax.rem(me, 2) - 1
    for slot in range(total):
        source[slot] = jnp.int32(0)

    def put(k, col, message, slot):
        far = lax.div(col, blocks) == me
        place = jnp.where(message == IN_FAR, slot, FAR + slot)
        source[jnp.where(far, jnp.minimum(place, total), total)] = lax.rem(col, blocks)

    slots_of(cols, there, blocks, put)
    for out, first, size in ((far_out, 0, FAR), (relay_out, FAR, relayed)):
        found = jnp.zeros((16, width // 2), jnp.float32)
        for slot in range(size):
            found = write_slot(out, slot, found, chosen(source[first + slot], own, own), width)
        out[size * width :, :] = found.astype(jnp.bfloat16)


def last_kernel(cols, own, mate, relay, out, source):
    blocks, width, _ = own.shape
    half = width // 2
    relayed = relay.shape[0] // width
    me = lax.axis_index("pan")
    for slot in range(LAST):
        source[slot] = jnp.int32(0)

    def put(k, col, message, slot):
        local = lax.rem(col, blocks) + jnp.where(lax.div(col, blocks) == me, 0, blocks)
        near = lax.div(col, 2 * blocks) == lax.div(me, 2)
        source[jnp.where(message == IN_LAST, slot, LAST)] = jnp.where(near, local, 2 * blocks)

    slots_of(cols, me, blocks, put)
    line = lax.broadcasted_iota(jnp.int32, (16, half), 0)
    found = jnp.zeros((16, half), jnp.float32)
    for slot in range(LAST):
        found = write_slot(out, slot, found, chosen(source[slot], own, mate), width)
    for slot in range(min(LAST, relayed)):
        base = slot * width
        theirs = source[slot] >= 2 * blocks
        out[base : base + width, :] = jnp.where(theirs, relay[base : base + width, :], out[base : base + width, :])
        found = jnp.where((line == slot) & theirs, relay[relayed * width :, :].astype(jnp.float32), found)
    out[LAST * width :, :] = found.astype(jnp.bfloat16)


def right_kernel(wanted, blocks, cols, received, left, z_row, *rest):
    out, results, places, sems = rest[-4:]
    slots, width, _ = results.shape
    half = width // 2
    me = lax.axis_index("pan")
    for slot in range(slots):
        places[slot] = jnp.int32(-1)

    def put(k, col, message, slot):
        places[jnp.where(message == wanted, slot, slots)] = jnp.int32(k)

    slots_of(cols, me, blocks, put)

    rows, lanes = iotas(half)
    diagonals = received[slots * width :, :].astype(jnp.float32)
    for slot in range(slots):
        k = places[slot]
        base = slot * width
        triangle = received[base : base + half, :].astype(jnp.float32)
        upper = jnp.where(rows <= lanes, triangle, 0.0).astype(jnp.bfloat16)
        lower = jnp.where(rows < lanes, triangle.T, jnp.where(rows == lanes, diagonals[slot : slot + 1, :], 0.0))
        lower = lower.astype(jnp.bfloat16)
        corner = received[base + half : base + width, :]
        z_col = jnp.concatenate(
            [
                jnp.concatenate([upper, corner], axis=1),
                jnp.concatenate([jnp.zeros_like(lower), lower], axis=1),
            ],
            axis=0,
        )
        inner = jnp.dot(left[jnp.maximum(k, 0)], z_col, preferred_element_type=jnp.float32)
        product = jnp.dot(z_row[...], inner.astype(jnp.bfloat16), preferred_element_type=jnp.float32)
        results[slot] = (-0.5 * product).astype(jnp.bfloat16)

    for slot in range(slots):
        k = places[slot]

        @pl.when(k >= 0)
        def _():
            pltpu.make_async_copy(results.at[slot], out.at[0, k], sems.at[slot]).start()

    for slot in range(slots):

        @pl.when(places[slot] >= 0)
        def _():
            pltpu.make_async_copy(results.at[slot], out.at[0, 0], sems.at[slot]).wait()


RIGHT_COST = (2 * 10**9,) * 3
LEFT_COST = 1
TINY = pl.CostEstimate(flops=1, bytes_accessed=1, transcendentals=0)
VMEM = pl.BlockSpec(memory_space=pltpu.VMEM)
SMEM = pl.BlockSpec(memory_space=pltpu.SMEM)
HBM = pl.BlockSpec(memory_space=pltpu.HBM)


def on_device(coupling_tiles, coupling_cols, row_blocks, factor_tiles):
    doms, panels = lax.axis_size("dom"), lax.axis_size("pan")
    blocks, width, _ = factor_tiles.shape
    _, count, _, _ = coupling_tiles.shape
    half, slots = width // 2, count - 1
    limit = pltpu.CompilerParams(vmem_limit_bytes=32 * 2**20)
    bf16 = lambda *shape: jax.ShapeDtypeStruct(shape, jnp.bfloat16)

    def flat(dom, panel):
        return dom * panels + panel

    straight = [(dom, dom ^ (doms // 2)) for dom in range(doms)]
    ends = (0, panels - 1)

    across = [
        (flat(dom, panel), flat(dom ^ (doms // 2), other_panel(panel, panels)))
        for dom in range(doms)
        for panel in range(panels)
        if panel not in ends
    ]
    beside = [
        (flat(dom, panel), flat(dom, other_panel(panel, panels)))
        for dom in range(doms)
        for panel in range(panels)
        if panel not in ends
    ]

    far_cols = lax.ppermute(coupling_cols, ("dom", "pan"), across)
    near_cols = lax.ppermute(coupling_cols, "dom", straight)

    own, z_row = pl.pallas_call(
        load_kernel,
        out_shape=(bf16(blocks, width, width), bf16(width, width)),
        in_specs=[SMEM, HBM],
        out_specs=(VMEM,) * 2,
        scratch_shapes=[pltpu.SemaphoreType.DMA] * 2,
        compiler_params=limit,
        cost_estimate=TINY,
        name="load",
    )(row_blocks, factor_tiles)

    def fill(kernel, sizes, *operands):
        return pl.pallas_call(
            kernel,
            out_shape=tuple(bf16(size * width + 16, half) for size in sizes),
            in_specs=[SMEM] + [VMEM] * (len(operands) - 1),
            out_specs=(VMEM,) * len(sizes),
            scratch_shapes=[pltpu.SMEM((sum(sizes) + 1,), jnp.int32)],
            compiler_params=limit,
            cost_estimate=TINY,
            name=kernel.__name__,
        )(*operands)

    far, relay = fill(far_kernel, (FAR, slots - FAR), far_cols, own)
    far, relay, near_cols, given = lax.optimization_barrier((far, relay, near_cols, factor_tiles))
    far = lax.ppermute(far, ("dom", "pan"), across)
    mate = lax.ppermute(given, "pan", [(panel, panel ^ 1) for panel in range(panels)])
    relay = lax.ppermute(relay, ("dom", "pan"), beside)
    (near,) = fill(near_kernel, (NEAR,), near_cols, own, mate)
    near = lax.ppermute(near, "dom", straight)
    (last,) = fill(last_kernel, (LAST,), near_cols, own, mate, relay)
    last = lax.ppermute(last, "dom", straight)
    messages = [(IN_FAR, FAR, far), (IN_NEAR, NEAR, near), (IN_LAST, LAST, last)]

    left = pl.pallas_call(
        left_kernel,
        out_shape=bf16(count, width, width),
        in_specs=[VMEM, VMEM],
        out_specs=VMEM,
        compiler_params=limit,
        cost_estimate=pl.CostEstimate(flops=LEFT_COST, bytes_accessed=1, transcendentals=0),
        name="left",
    )(z_row, coupling_tiles)

    out = None
    for wanted, size, message in messages:
        out = pl.pallas_call(
            functools.partial(right_kernel, wanted, blocks),
            out_shape=bf16(*coupling_tiles.shape),
            in_specs=[SMEM, VMEM, VMEM, VMEM] + ([] if out is None else [HBM]),
            out_specs=HBM,
            scratch_shapes=[
                pltpu.VMEM((size, width, width), jnp.bfloat16),
                pltpu.SMEM((size + 1,), jnp.int32),
                pltpu.SemaphoreType.DMA((size,)),
            ],
            input_output_aliases={} if out is None else {4: 0},
            compiler_params=limit,
            cost_estimate=pl.CostEstimate(flops=RIGHT_COST[wanted], bytes_accessed=1, transcendentals=0),
            name=("right_near", "right_far", "right_last")[wanted],
        )(coupling_cols, message, left, z_row, *(() if out is None else (out,)))
    return out


def solution(mesh):
    return jax.shard_map(
        on_device,
        mesh=mesh,
        in_specs=(
            P(("dom", "pan"), None, None, None),
            P(("dom", "pan"), None),
            P(("dom", "pan")),
            P(("dom", "pan"), None, None),
        ),
        out_specs=P(("dom", "pan"), None, None, None),
        check_vma=False,
    )
```

time: 47.6 us -> 42.5 us (0.89)
  the two profiles are of different devices: /device:TPU:1 before, /device:TPU:200 now
where the time goes in v3:
time: 42.5 us; the launch traced here: 42.2 us
  starting transfers between devices  22.1 us (52%)
  Pallas kernels  9.12 us (21%)
  waiting for transfers between devices  8.58 us (20%)
  local copies, waits for them, and re-layouts  1.59 us (4%)
  between operations  0.8 us (2%)
    ppermute x1, waiting for transfers between devices, on_device(): far = lax.ppermute(far, ('dom', 'pan'), across)  5.97 us
    pallas_call x3, Pallas kernels, on_device(): pl.pallas_call(functools.partial(right_kernel, wanted, blocks), out_shape...  5.95 us
    ppermute x1, starting transfers between devices, on_device(): near = lax.ppermute(near, 'dom', straight)  4.37 us
    ppermute x1, starting transfers between devices, on_device(): far = lax.ppermute(far, ('dom', 'pan'), across)  4.07 us
    ppermute x1, starting transfers between devices, on_device(): far_cols = lax.ppermute(coupling_cols, ('dom', 'pan'), across)  3.98 us
    ppermute x1, starting transfers between devices, on_device(): near_cols = lax.ppermute(coupling_cols, 'dom', straight)  2.86 us
    ppermute x1, starting transfers between devices, on_device(): relay = lax.ppermute(relay, ('dom', 'pan'), beside)  2.6 us
    pallas_call x3, Pallas kernels, fill(): pl.pallas_call(kernel, out_shape=tuple((bf16(size * width + 16, half) for...  2.36 us
  transfers between devices with their start and end apart: 7, of which 3 were waited for; matrix products, arithmetic and copies ran while one was open for 0% of the time, Pallas kernels for 17%

profile of v3, /device:TPU:200, one launch (start us, length us, event | category | flops | bytes accessed | tf_op | source)
XLA Modules:
  0.0 42.2 jit_solution(14127896778013812891)
XLA Ops:
  0.0 4.0 %collective-permute-start = (s32[1,8]{1,0:T(1,128)}, s32[1,8]{1,0:T(1,128)S(1)}, u32[]{:S(2)}, u32[]{:S(2)}) collective-permute-start(s32[1,8]{1,0:T(1,128)} %cols.5), channel_id=1, source_target_pairs={{1,258},{2,257},{3,260},{4,259},{5,262},{6,261},{7,264},{8,263},{9... | collective-permute-start | bytes 104 | tf_op jit(solution)/shard_map/ppermute | solution.py:223
  4.0 2.9 %collective-permute-start.1 = (s32[1,8]{1,0:T(1,128)}, s32[1,8]{1,0:T(1,128)S(1)}, u32[]{:S(2)}, u32[]{:S(2)}) collective-permute-start(s32[1,8]{1,0:T(1,128)} %cols.5), channel_id=1, source_target_pairs={{0,256},{16,272},{32,288},{48,304},{64,320},{80,336},{96,352},{112... | collective-permute-start | bytes 104 | tf_op jit(solution)/shard_map/ppermute | solution.py:224
  7.5 0.0 copy-start
  7.5 1.6 %copy-done = bf16[16,256,256]{2,1,0:T(8,128)(2,1)S(1)} copy-done((bf16[16,256,256]{2,1,0:T(8,128)(2,1)S(1)}, bf16[16,256,256]{2,1,0:T(8,128)(2,1)}, u32[]{:S(2)}) %copy-start) | copy-done | bytes 2097176
  9.1 0.3 load.1
  9.4 0.0 collective-permute-done.cols
  9.4 0.8 %far_kernel.1 = (bf16[1040,128]{1,0:T(8,128)(2,1)S(1)}, bf16[784,128]{1,0:T(8,128)(2,1)S(1)}) custom-call(s32[1,8]{1,0:T(1,128)S(1)} %collective-permute-done.cols, bf16[16,256,256]{2,1,0:T(8,128)(2,1)S(1)} %get-tuple-element.13.own), custom_call_target="tpu_custom_call" | custom-call | flops 1 | bytes 1 | tf_op jit(solution)/shard_map/far_kernel/pallas_call | solution.py:238
  10.2 0.8 %collective-permute-done.1.cols = s32[1,8]{1,0:T(1,128)S(1)} collective-permute-done((s32[1,8]{1,0:T(1,128)}, s32[1,8]{1,0:T(1,128)S(1)}, u32[]{:S(2)}, u32[]{:S(2)}) %collective-permute-start.1) | collective-permute-done | bytes 64 | tf_op jit(solution)/shard_map/ppermute | solution.py:224
  11.1 0.0 copy-start.1
  11.1 2.0 %collective-permute-start.2 = (bf16[16,256,256]{2,1,0:T(8,128)(2,1)S(1)}, bf16[16,256,256]{2,1,0:T(8,128)(2,1)S(1)}, u32[]{:S(2)}, u32[]{:S(2)}) collective-permute-start(bf16[16,256,256]{2,1,0:T(8,128)(2,1)S(1)} %copy-done), channel_id=1, source_target_pairs={{0,1},{1,0},{2,3},{3,2},{4,5},{5,4},{6,7},{7,6},{8,9},{9,8},{10,11... | collective-permute-start | bytes 6291464 | tf_op jit(solution)/shard_map/ppermute | solution.py:252
  13.1 4.1 %collective-permute-start.6 = (bf16[1040,128]{1,0:T(8,128)(2,1)S(1)}, bf16[1040,128]{1,0:T(8,128)(2,1)S(1)}, u32[]{:S(2)}, u32[]{:S(2)}) collective-permute-start(bf16[1040,128]{1,0:T(8,128)(2,1)S(1)} %get-tuple-element.20), channel_id=1, source_target_pairs={{1,258},{2,257},{3,260},{4,259},{5,262},{6,261},{7,264},{8,263},{9... | collective-permute-start | bytes 798728 | tf_op jit(solution)/shard_map/ppermute | solution.py:251
  17.2 2.6 %collective-permute-start.3 = (bf16[784,128]{1,0:T(8,128)(2,1)S(1)}, bf16[784,128]{1,0:T(8,128)(2,1)S(1)}, u32[]{:S(2)}, u32[]{:S(2)}) collective-permute-start(bf16[784,128]{1,0:T(8,128)(2,1)S(1)} %get-tuple-element.18), channel_id=1, source_target_pairs={{1,2},{2,1},{3,4},{4,3},{5,6},{6,5},{7,8},{8,7},{9,10},{10,9},{11,... | collective-permute-start | bytes 602120 | tf_op jit(solution)/shard_map/ppermute | solution.py:253
  19.8 0.0 collective-permute-done.2.mate
  19.8 0.8 %near_kernel.1 = bf16[1296,128]{1,0:T(8,128)(2,1)S(1)} custom-call(s32[1,8]{1,0:T(1,128)S(1)} %collective-permute-done.1.cols, bf16[16,256,256]{2,1,0:T(8,128)(2,1)S(1)} %get-tuple-element.13.own, bf16[16,256,256]{2,1,0:T(8,128)(2,1)S(1)} %collective-permute-done.2.mate), custom_call_target="tpu_custom_call" | custom-call | flops 1 | bytes 1 | tf_op jit(solution)/shard_map/near_kernel/pallas_call | solution.py:238
  20.6 4.4 %collective-permute-start.5 = (bf16[1296,128]{1,0:T(8,128)(2,1)S(1)}, bf16[1296,128]{1,0:T(8,128)(2,1)S(1)}, u32[]{:S(2)}, u32[]{:S(2)}) collective-permute-start(bf16[1296,128]{1,0:T(8,128)(2,1)S(1)} %near_kernel.1), channel_id=1, source_target_pairs={{0,256},{16,272},{32,288},{48,304},{64,320},{80,336},{96,352},{112... | collective-permute-start | bytes 995336 | tf_op jit(solution)/shard_map/ppermute | solution.py:255
  25.0 0.0 copy-done.1
  25.0 0.5 %left.1 = bf16[8,256,256]{2,1,0:T(8,128)(2,1)S(1)} custom-call(bf16[256,256]{1,0:T(8,128)(2,1)S(1)} %get-tuple-element.19.z_row, bf16[1,8,256,256]{3,2,1,0:T(8,128)(2,1)S(1)} %copy-done.1), custom_call_target="tpu_custom_call" | custom-call | flops 1 | bytes 1 | tf_op jit(solution)/shard_map/left/pallas_call | solution.py:260
  25.5 0.0 copy-start.2
  25.5 1.8 %collective-permute-done.3.relay = bf16[784,128]{1,0:T(8,128)(2,1)S(1)} collective-permute-done((bf16[784,128]{1,0:T(8,128)(2,1)S(1)}, bf16[784,128]{1,0:T(8,128)(2,1)S(1)}, u32[]{:S(2)}, u32[]{:S(2)}) %collective-permute-start.3) | collective-permute-done | bytes 200736 | tf_op jit(solution)/shard_map/ppermute | solution.py:253
  27.3 0.8 %last_kernel.1 = bf16[784,128]{1,0:T(8,128)(2,1)S(1)} custom-call(s32[1,8]{1,0:T(1,128)S(1)} %collective-permute-done.1.cols, bf16[16,256,256]{2,1,0:T(8,128)(2,1)S(1)} %get-tuple-element.13.own, bf16[16,256,256]{2,1,0:T(8,128)(2,1)S(1)} %collective-permute-done.2.mate, bf16[784,128]{1,0:T(8,128)(2,1)S(1)} %collective-permute-done.3.relay), custom_call_target="tpu_custom_call" | custom-call | flops 1 | bytes 1 | tf_op jit(solution)/shard_map/last_kernel/pallas_call | solution.py:238
  28.1 2.2 %collective-permute-start.4 = (bf16[784,128]{1,0:T(8,128)(2,1)S(1)}, bf16[784,128]{1,0:T(8,128)(2,1)S(1)}, u32[]{:S(2)}, u32[]{:S(2)}) collective-permute-start(bf16[784,128]{1,0:T(8,128)(2,1)S(1)} %last_kernel.1), channel_id=1, source_target_pairs={{0,256},{16,272},{32,288},{48,304},{64,320},{80,336},{96,352},{112... | collective-permute-start | bytes 602120 | tf_op jit(solution)/shard_map/ppermute | solution.py:257
  30.3 6.0 %collective-permute-done.6.received = bf16[1040,128]{1,0:T(8,128)(2,1)S(1)} collective-permute-done((bf16[1040,128]{1,0:T(8,128)(2,1)S(1)}, bf16[1040,128]{1,0:T(8,128)(2,1)S(1)}, u32[]{:S(2)}, u32[]{:S(2)}) %collective-permute-start.6) | collective-permute-done | bytes 266272 | tf_op jit(solution)/shard_map/ppermute | solution.py:251
  36.2 0.0 copy-done.2
  36.2 2.0 %right_far.1.rest_0_ = bf16[1,8,256,256]{3,2,1,0:T(8,128)(2,1)} custom-call(s32[1,8]{1,0:T(1,128)S(1)} %copy-done.2, bf16[1040,128]{1,0:T(8,128)(2,1)S(1)} %collective-permute-done.6.received, bf16[8,256,256]{2,1,0:T(8,128)(2,1)S(1)} %left.1, bf16[256,256]{1,0:T(8,128)(2,1)S(1)} %get-tuple-element.19.z_row), custom_call_target="tpu_custom_call" | custom-call | flops 2000000000 | bytes 1 | tf_op jit(solution)/shard_map/right_far/pallas_call | solution.py:272
  38.2 0.0 collective-permute-done.5.received
  38.2 2.2 %right_near.1.rest_0_ = bf16[1,8,256,256]{3,2,1,0:T(8,128)(2,1)} custom-call(s32[1,8]{1,0:T(1,128)S(1)} %copy-done.2, bf16[1296,128]{1,0:T(8,128)(2,1)S(1)} %collective-permute-done.5.received, bf16[8,256,256]{2,1,0:T(8,128)(2,1)S(1)} %left.1, bf16[256,256]{1,0:T(8,128)(2,1)S(1)} %get-tuple-element.19.z_row, ...), custom_call_target="tpu_custom_call", output_to_operand_aliasing={{}: (4, {})} | custom-call | flops 2000000000 | bytes 1 | tf_op jit(solution)/shard_map/right_near/pallas_call | solution.py:272
  40.4 0.0 collective-permute-done.4.received
  40.4 1.8 %right_last.1 = bf16[1,8,256,256]{3,2,1,0:T(8,128)(2,1)} custom-call(s32[1,8]{1,0:T(1,128)S(1)} %copy-done.2, bf16[784,128]{1,0:T(8,128)(2,1)S(1)} %collective-permute-done.4.received, bf16[8,256,256]{2,1,0:T(8,128)(2,1)S(1)} %left.1, bf16[256,256]{1,0:T(8,128)(2,1)S(1)} %get-tuple-element.19.z_row, ...), custom_call_target="tpu_custom_call", output_to_operand_aliasing={{}: (4, {})} | custom-call | flops 2000000000 | bytes 1 | tf_op jit(solution)/shard_map/right_last/pallas_call | solution.py:272
Async XLA Ops:
  0.0 9.4 %collective-permute-start = (s32[1,8]{1,0:T(1,128)}, s32[1,8]{1,0:T(1,128)S(1)}, u32[]{:S(2)}, u32[]{:S(2)}) collective-permute-start(s32[1,8]{1,0:T(1,128)} %cols.5), channel_id=1, source_target_pairs={{1,258},{2,257},{3,260},{4,259},{5,262},{6,261},{7,264},{8,263},{9... | collective-permute-start | bytes 104 | tf_op jit(solution)/shard_map/ppermute | solution.py:223
  4.0 7.1 %collective-permute-start.1 = (s32[1,8]{1,0:T(1,128)}, s32[1,8]{1,0:T(1,128)S(1)}, u32[]{:S(2)}, u32[]{:S(2)}) collective-permute-start(s32[1,8]{1,0:T(1,128)} %cols.5), channel_id=1, source_target_pairs={{0,256},{16,272},{32,288},{48,304},{64,320},{80,336},{96,352},{112... | collective-permute-start | bytes 104 | tf_op jit(solution)/shard_map/ppermute | solution.py:224
  7.5 1.6 %copy-start = (bf16[16,256,256]{2,1,0:T(8,128)(2,1)S(1)}, bf16[16,256,256]{2,1,0:T(8,128)(2,1)}, u32[]{:S(2)}) copy-start(bf16[16,256,256]{2,1,0:T(8,128)(2,1)} %factors.1) | copy-start | bytes 6291460
  11.1 13.9 %copy-start.1 = (bf16[1,8,256,256]{3,2,1,0:T(8,128)(2,1)S(1)}, bf16[1,8,256,256]{3,2,1,0:T(8,128)(2,1)}, u32[]{:S(2)}) copy-start(bf16[1,8,256,256]{3,2,1,0:T(8,128)(2,1)} %tiles.1) | copy-start | bytes 3145732
  11.1 8.7 %collective-permute-start.2 = (bf16[16,256,256]{2,1,0:T(8,128)(2,1)S(1)}, bf16[16,256,256]{2,1,0:T(8,128)(2,1)S(1)}, u32[]{:S(2)}, u32[]{:S(2)}) collective-permute-start(bf16[16,256,256]{2,1,0:T(8,128)(2,1)S(1)} %copy-done), channel_id=1, source_target_pairs={{0,1},{1,0},{2,3},{3,2},{4,5},{5,4},{6,7},{7,6},{8,9},{9,8},{10,11... | collective-permute-start | bytes 6291464 | tf_op jit(solution)/shard_map/ppermute | solution.py:252
  13.1 23.1 %collective-permute-start.6 = (bf16[1040,128]{1,0:T(8,128)(2,1)S(1)}, bf16[1040,128]{1,0:T(8,128)(2,1)S(1)}, u32[]{:S(2)}, u32[]{:S(2)}) collective-permute-start(bf16[1040,128]{1,0:T(8,128)(2,1)S(1)} %get-tuple-element.20), channel_id=1, source_target_pairs={{1,258},{2,257},{3,260},{4,259},{5,262},{6,261},{7,264},{8,263},{9... | collective-permute-start | bytes 798728 | tf_op jit(solution)/shard_map/ppermute | solution.py:251
  17.2 10.1 %collective-permute-start.3 = (bf16[784,128]{1,0:T(8,128)(2,1)S(1)}, bf16[784,128]{1,0:T(8,128)(2,1)S(1)}, u32[]{:S(2)}, u32[]{:S(2)}) collective-permute-start(bf16[784,128]{1,0:T(8,128)(2,1)S(1)} %get-tuple-element.18), channel_id=1, source_target_pairs={{1,2},{2,1},{3,4},{4,3},{5,6},{6,5},{7,8},{8,7},{9,10},{10,9},{11,... | collective-permute-start | bytes 602120 | tf_op jit(solution)/shard_map/ppermute | solution.py:253
  20.6 17.6 %collective-permute-start.5 = (bf16[1296,128]{1,0:T(8,128)(2,1)S(1)}, bf16[1296,128]{1,0:T(8,128)(2,1)S(1)}, u32[]{:S(2)}, u32[]{:S(2)}) collective-permute-start(bf16[1296,128]{1,0:T(8,128)(2,1)S(1)} %near_kernel.1), channel_id=1, source_target_pairs={{0,256},{16,272},{32,288},{48,304},{64,320},{80,336},{96,352},{112... | collective-permute-start | bytes 995336 | tf_op jit(solution)/shard_map/ppermute | solution.py:255
  25.5 10.7 %copy-start.2 = (s32[1,8]{1,0:T(1,128)S(1)}, s32[1,8]{1,0:T(1,128)}, u32[]{:S(2)}) copy-start(s32[1,8]{1,0:T(1,128)} %cols.5) | copy-start | bytes 100
  28.1 12.3 %collective-permute-start.4 = (bf16[784,128]{1,0:T(8,128)(2,1)S(1)}, bf16[784,128]{1,0:T(8,128)(2,1)S(1)}, u32[]{:S(2)}, u32[]{:S(2)}) collective-permute-start(bf16[784,128]{1,0:T(8,128)(2,1)S(1)} %last_kernel.1), channel_id=1, source_target_pairs={{0,256},{16,272},{32,288},{48,304},{64,320},{80,336},{96,352},{112... | collective-permute-start | bytes 602120 | tf_op jit(solution)/shard_map/ppermute | solution.py:257

commit v4 on v2

--- a/solution.py
+++ b/solution.py
@@ -126,6 +126,9 @@
         product = jnp.dot(z_row[...], inner.astype(jnp.bfloat16), preferred_element_type=jnp.float32)
         results[slot] = (-0.5 * product).astype(jnp.bfloat16)
 
+    for slot in range(slots):
+        k = places[slot]
+
         @pl.when(k >= 0)
         def _():
             pltpu.make_async_copy(results.at[slot], out.at[0, k], sems.at[slot]).start()
@@ -137,6 +140,9 @@
             pltpu.make_async_copy(results.at[slot], out.at[0, 0], sems.at[slot]).wait()
 
 
+RIGHT_COST = 1
+TINY = pl.CostEstimate(flops=1, bytes_accessed=1, transcendentals=0)
+COST = pl.CostEstimate(flops=RIGHT_COST, bytes_accessed=1, transcendentals=0)
 VMEM = pl.BlockSpec(memory_space=pltpu.VMEM)
 SMEM = pl.BlockSpec(memory_space=pltpu.SMEM)
 HBM = pl.BlockSpec(memory_space=pltpu.HBM)
@@ -175,6 +181,7 @@
         out_specs=(VMEM,) * 2,
         scratch_shapes=[pltpu.SemaphoreType.DMA] * 2,
         compiler_params=limit,
+        cost_estimate=TINY,
         name="load",
     )(row_blocks, factor_tiles)
 
@@ -187,11 +194,11 @@
             out_specs=(VMEM,) * len(sizes),
             scratch_shapes=[pltpu.SMEM((slots + 1,), jnp.int32)],
             compiler_params=limit,
+            cost_estimate=TINY,
             name="fill_near" if near_wanted else "fill_far",
         )(cols, own, mate)
 
     (near,) = filled(True, (slots,), near_cols)
-    near, far_cols = lax.optimization_barrier((near, far_cols))
     near = lax.ppermute(near, "dom", straight)
     far = filled(False, FAR_CHUNKS, far_cols)
     first = 0
@@ -208,6 +215,7 @@
         in_specs=[VMEM, VMEM],
         out_specs=VMEM,
         compiler_params=limit,
+        cost_estimate=TINY,
         name="left",
     )(z_row, coupling_tiles)
 
@@ -225,6 +233,7 @@
             ],
             input_output_aliases={} if out is None else {4: 0},
             compiler_params=limit,
+            cost_estimate=COST,
             name="right_near" if near_wanted else "right_far",
         )(coupling_cols, message, left, z_row, *(() if out is None else (out,)))
     return out

time: 47.6 us -> 45.7 us (0.960)
  starting transfers between devices: 23.5 us -> 22.4 us
  waiting for transfers between devices: 13.4 us -> 12.7 us
    ppermute x2, waiting for transfers between devices: 10.7 us -> 6.23 us  [on_device(): message = lax.ppermute(message, ('dom', 'pan'), across(with_ends))]
    ppermute x1, waiting for transfers between devices: 0.01 us -> 4.44 us  [on_device(): far_cols = lax.ppermute(coupling_cols, ('dom', 'pan'), across(True))]
    ppermute x1, waiting for transfers between devices: 1.26 us -> 0.01 us  [on_device(): near = lax.ppermute(near, 'dom', straight)]
    ppermute x1, waiting for transfers between devices: 1.42 us -> 2.07 us  [on_device(): near_cols = lax.ppermute(coupling_cols, 'dom', straight)]
    ppermute x1, starting transfers between devices: 3.59 us -> 2.96 us  [on_device(): near = lax.ppermute(near, 'dom', straight)]
    ppermute x2, starting transfers between devices: 7.33 us -> 6.77 us  [on_device(): message = lax.ppermute(message, ('dom', 'pan'), across(with_ends))]
where the time goes in v4:
time: 45.7 us; the launch traced here: 45.4 us
  starting transfers between devices  22.4 us (49%)
  waiting for transfers between devices  12.7 us (28%)
  Pallas kernels  7.95 us (17%)
  local copies, waits for them, and re-layouts  1.59 us (3%)
  between operations  0.78 us (2%)
    ppermute x1, starting transfers between devices, on_device(): lax.ppermute(factor_tiles, 'pan', [(panel, panel ^ 1) for panel in range(...  8.77 us
    ppermute x2, starting transfers between devices, on_device(): message = lax.ppermute(message, ('dom', 'pan'), across(with_ends))  6.77 us
    ppermute x2, waiting for transfers between devices, on_device(): message = lax.ppermute(message, ('dom', 'pan'), across(with_ends))  6.23 us
    pallas_call x3, Pallas kernels, on_device(): pl.pallas_call(functools.partial(right_kernel, near_wanted, panels, block...  5.49 us
    ppermute x1, waiting for transfers between devices, on_device(): far_cols = lax.ppermute(coupling_cols, ('dom', 'pan'), across(True))  4.44 us
    ppermute x1, starting transfers between devices, on_device(): near = lax.ppermute(near, 'dom', straight)  2.96 us
    ppermute x1, waiting for transfers between devices, on_device(): near_cols = lax.ppermute(coupling_cols, 'dom', straight)  2.07 us
    ppermute x1, starting transfers between devices, on_device(): near_cols = lax.ppermute(coupling_cols, 'dom', straight)  1.92 us
  transfers between devices with their start and end apart: 6, of which 4 were waited for; matrix products, arithmetic and copies ran while one was open for 0% of the time, Pallas kernels for 13%

profile of v4, /device:TPU:1, one launch (start us, length us, event | category | flops | bytes accessed | tf_op | source)
XLA Modules:
  0.0 45.4 jit_solution(14894467776626086290)
XLA Ops:
  0.0 8.8 %collective-permute-start.1 = (bf16[16,256,256]{2,1,0:T(8,128)(2,1)}, bf16[16,256,256]{2,1,0:T(8,128)(2,1)S(1)}, u32[]{:S(2)}, u32[]{:S(2)}) collective-permute-start(bf16[16,256,256]{2,1,0:T(8,128)(2,1)} %factors.1), channel_id=1, source_target_pairs={{0,1},{1,0},{2,3},{3,2},{4,5},{5,4},{6,7},{7,6},{8,9},{9,8},{10,11... | collective-permute-start | bytes 6291464 | tf_op jit(solution)/shard_map/ppermute | solution.py:173
  9.4 1.9 %collective-permute-start.4 = (s32[1,8]{1,0:T(1,128)}, s32[1,8]{1,0:T(1,128)S(1)}, u32[]{:S(2)}, u32[]{:S(2)}) collective-permute-start(s32[1,8]{1,0:T(1,128)} %cols.5), channel_id=1, source_target_pairs={{0,256},{16,272},{32,288},{48,304},{64,320},{80,336},{96,352},{112... | collective-permute-start | bytes 104 | tf_op jit(solution)/shard_map/ppermute | solution.py:174
  11.4 0.0 copy-start
  11.4 1.6 %copy-done = bf16[16,256,256]{2,1,0:T(8,128)(2,1)S(1)} copy-done((bf16[16,256,256]{2,1,0:T(8,128)(2,1)S(1)}, bf16[16,256,256]{2,1,0:T(8,128)(2,1)}, u32[]{:S(2)}) %copy-start) | copy-done | bytes 2097176
  13.0 0.3 load.1
  13.3 2.1 %collective-permute-done.4.cols = s32[1,8]{1,0:T(1,128)S(1)} collective-permute-done((s32[1,8]{1,0:T(1,128)}, s32[1,8]{1,0:T(1,128)S(1)}, u32[]{:S(2)}, u32[]{:S(2)}) %collective-permute-start.4) | collective-permute-done | bytes 64 | tf_op jit(solution)/shard_map/ppermute | solution.py:174
  15.4 0.0 collective-permute-done.1.mate
  15.4 0.0 copy-start.2
  15.4 0.8 %fill_near.1 = bf16[1808,128]{1,0:T(8,128)(2,1)S(1)} custom-call(s32[1,8]{1,0:T(1,128)S(1)} %collective-permute-done.4.cols, bf16[16,256,256]{2,1,0:T(8,128)(2,1)S(1)} %get-tuple-element.9.own, bf16[16,256,256]{2,1,0:T(8,128)(2,1)S(1)} %collective-permute-done.1.mate), custom_call_target="tpu_custom_call" | custom-call | flops 1 | bytes 1 | tf_op jit(solution)/shard_map/fill_near/pallas_call | solution.py:190
  16.2 0.0 copy-start.1
  16.2 3.0 %collective-permute-start.5 = (bf16[1808,128]{1,0:T(8,128)(2,1)S(1)}, bf16[1808,128]{1,0:T(8,128)(2,1)S(1)}, u32[]{:S(2)}, u32[]{:S(2)}) collective-permute-start(bf16[1808,128]{1,0:T(8,128)(2,1)S(1)} %fill_near.1), channel_id=1, source_target_pairs={{0,256},{16,272},{32,288},{48,304},{64,320},{80,336},{96,352},{112... | collective-permute-start | bytes 1388552 | tf_op jit(solution)/shard_map/ppermute | solution.py:202
  19.2 0.0 copy-done.2
  19.2 1.9 %collective-permute-start = (s32[1,8]{1,0:T(1,128)S(1)}, s32[1,8]{1,0:T(1,128)S(1)}, u32[]{:S(2)}, u32[]{:S(2)}) collective-permute-start(s32[1,8]{1,0:T(1,128)S(1)} %copy-done.2), channel_id=1, source_target_pairs={{0,256},{1,258},{2,257},{3,260},{4,259},{5,262},{6,261},{7,264},{8... | collective-permute-start | bytes 104 | tf_op jit(solution)/shard_map/ppermute | solution.py:175
  21.1 4.4 %collective-permute-done.cols = s32[1,8]{1,0:T(1,128)S(1)} collective-permute-done((s32[1,8]{1,0:T(1,128)S(1)}, s32[1,8]{1,0:T(1,128)S(1)}, u32[]{:S(2)}, u32[]{:S(2)}) %collective-permute-start) | collective-permute-done | bytes 64 | tf_op jit(solution)/shard_map/ppermute | solution.py:175
  25.5 0.8 %fill_far.1 = (bf16[1040,128]{1,0:T(8,128)(2,1)S(1)}, bf16[784,128]{1,0:T(8,128)(2,1)S(1)}) custom-call(s32[1,8]{1,0:T(1,128)S(1)} %collective-permute-done.cols, bf16[16,256,256]{2,1,0:T(8,128)(2,1)S(1)} %get-tuple-element.9.own, bf16[16,256,256]{2,1,0:T(8,128)(2,1)S(1)} %collective-permute-done.1.mate), custom_call_target="tpu_custom_call" | custom-call | flops 1 | bytes 1 | tf_op jit(solution)/shard_map/fill_far/pallas_call | solution.py:190
  26.4 1.9 %collective-permute-start.3 = (bf16[1040,128]{1,0:T(8,128)(2,1)S(1)}, bf16[1040,128]{1,0:T(8,128)(2,1)S(1)}, u32[]{:S(2)}, u32[]{:S(2)}) collective-permute-start(bf16[1040,128]{1,0:T(8,128)(2,1)S(1)} %get-tuple-element.12), channel_id=1, source_target_pairs={{1,258},{2,257},{3,260},{4,259},{5,262},{6,261},{7,264},{8,263},{9... | collective-permute-start | bytes 798728 | tf_op jit(solution)/shard_map/ppermute | solution.py:208
  28.3 4.9 %collective-permute-start.2 = (bf16[784,128]{1,0:T(8,128)(2,1)S(1)}, bf16[784,128]{1,0:T(8,128)(2,1)S(1)}, u32[]{:S(2)}, u32[]{:S(2)}) collective-permute-start(bf16[784,128]{1,0:T(8,128)(2,1)S(1)} %get-tuple-element.10), channel_id=1, source_target_pairs={{0,256},{1,258},{2,257},{3,260},{4,259},{5,262},{6,261},{7,264},{8... | collective-permute-start | bytes 602120 | tf_op jit(solution)/shard_map/ppermute | solution.py:208
  33.2 0.0 copy-done.1
  33.2 0.5 %left.1 = bf16[8,256,256]{2,1,0:T(8,128)(2,1)S(1)} custom-call(bf16[256,256]{1,0:T(8,128)(2,1)S(1)} %get-tuple-element.11.z_row, bf16[1,8,256,256]{3,2,1,0:T(8,128)(2,1)S(1)} %copy-done.1), custom_call_target="tpu_custom_call" | custom-call | flops 1 | bytes 1 | tf_op jit(solution)/shard_map/left/pallas_call | solution.py:212
  33.7 0.0 collective-permute-done.5.message
  33.7 2.3 %right_near.1.rest_0_ = bf16[1,8,256,256]{3,2,1,0:T(8,128)(2,1)} custom-call(s32[1,8]{1,0:T(1,128)S(1)} %copy-done.2, bf16[1808,128]{1,0:T(8,128)(2,1)S(1)} %collective-permute-done.5.message, bf16[8,256,256]{2,1,0:T(8,128)(2,1)S(1)} %left.1, bf16[256,256]{1,0:T(8,128)(2,1)S(1)} %get-tuple-element.11.z_row), custom_call_target="tpu_custom_call" | custom-call | flops 1 | bytes 1 | tf_op jit(solution)/shard_map/right_near/pallas_call | solution.py:224
  36.0 2.2 %collective-permute-done.3.message = bf16[1040,128]{1,0:T(8,128)(2,1)S(1)} collective-permute-done((bf16[1040,128]{1,0:T(8,128)(2,1)S(1)}, bf16[1040,128]{1,0:T(8,128)(2,1)S(1)}, u32[]{:S(2)}, u32[]{:S(2)}) %collective-permute-start.3) | collective-permute-done | bytes 266272 | tf_op jit(solution)/shard_map/ppermute | solution.py:208
  38.2 2.0 %right_far.2.rest_0_ = bf16[1,8,256,256]{3,2,1,0:T(8,128)(2,1)} custom-call(s32[1,8]{1,0:T(1,128)S(1)} %copy-done.2, bf16[1040,128]{1,0:T(8,128)(2,1)S(1)} %collective-permute-done.3.message, bf16[8,256,256]{2,1,0:T(8,128)(2,1)S(1)} %left.1, bf16[256,256]{1,0:T(8,128)(2,1)S(1)} %get-tuple-element.11.z_row, ...), custom_call_target="tpu_custom_call", output_to_operand_aliasing={{}: (4, {})} | custom-call | flops 1 | bytes 1 | tf_op jit(solution)/shard_map/right_far/pallas_call | solution.py:224
  40.2 4.0 %collective-permute-done.2.message = bf16[784,128]{1,0:T(8,128)(2,1)S(1)} collective-permute-done((bf16[784,128]{1,0:T(8,128)(2,1)S(1)}, bf16[784,128]{1,0:T(8,128)(2,1)S(1)}, u32[]{:S(2)}, u32[]{:S(2)}) %collective-permute-start.2) | collective-permute-done | bytes 200736 | tf_op jit(solution)/shard_map/ppermute | solution.py:208
  44.2 1.2 %right_far.3 = bf16[1,8,256,256]{3,2,1,0:T(8,128)(2,1)} custom-call(s32[1,8]{1,0:T(1,128)S(1)} %copy-done.2, bf16[784,128]{1,0:T(8,128)(2,1)S(1)} %collective-permute-done.2.message, bf16[8,256,256]{2,1,0:T(8,128)(2,1)S(1)} %left.1, bf16[256,256]{1,0:T(8,128)(2,1)S(1)} %get-tuple-element.11.z_row, ...), custom_call_target="tpu_custom_call", output_to_operand_aliasing={{}: (4, {})} | custom-call | flops 1 | bytes 1 | tf_op jit(solution)/shard_map/right_far/pallas_call | solution.py:224
Async XLA Ops:
  0.0 15.4 %collective-permute-start.1 = (bf16[16,256,256]{2,1,0:T(8,128)(2,1)}, bf16[16,256,256]{2,1,0:T(8,128)(2,1)S(1)}, u32[]{:S(2)}, u32[]{:S(2)}) collective-permute-start(bf16[16,256,256]{2,1,0:T(8,128)(2,1)} %factors.1), channel_id=1, source_target_pairs={{0,1},{1,0},{2,3},{3,2},{4,5},{5,4},{6,7},{7,6},{8,9},{9,8},{10,11... | collective-permute-start | bytes 6291464 | tf_op jit(solution)/shard_map/ppermute | solution.py:173
  9.4 5.9 %collective-permute-start.4 = (s32[1,8]{1,0:T(1,128)}, s32[1,8]{1,0:T(1,128)S(1)}, u32[]{:S(2)}, u32[]{:S(2)}) collective-permute-start(s32[1,8]{1,0:T(1,128)} %cols.5), channel_id=1, source_target_pairs={{0,256},{16,272},{32,288},{48,304},{64,320},{80,336},{96,352},{112... | collective-permute-start | bytes 104 | tf_op jit(solution)/shard_map/ppermute | solution.py:174
  11.4 1.6 %copy-start = (bf16[16,256,256]{2,1,0:T(8,128)(2,1)S(1)}, bf16[16,256,256]{2,1,0:T(8,128)(2,1)}, u32[]{:S(2)}) copy-start(bf16[16,256,256]{2,1,0:T(8,128)(2,1)} %factors.1) | copy-start | bytes 6291460
  15.4 3.8 %copy-start.2 = (s32[1,8]{1,0:T(1,128)S(1)}, s32[1,8]{1,0:T(1,128)}, u32[]{:S(2)}) copy-start(s32[1,8]{1,0:T(1,128)} %cols.5) | copy-start | bytes 100
  16.2 17.0 %copy-start.1 = (bf16[1,8,256,256]{3,2,1,0:T(8,128)(2,1)S(1)}, bf16[1,8,256,256]{3,2,1,0:T(8,128)(2,1)}, u32[]{:S(2)}) copy-start(bf16[1,8,256,256]{3,2,1,0:T(8,128)(2,1)} %tiles.1) | copy-start | bytes 3145732
  16.2 17.5 %collective-permute-start.5 = (bf16[1808,128]{1,0:T(8,128)(2,1)S(1)}, bf16[1808,128]{1,0:T(8,128)(2,1)S(1)}, u32[]{:S(2)}, u32[]{:S(2)}) collective-permute-start(bf16[1808,128]{1,0:T(8,128)(2,1)S(1)} %fill_near.1), channel_id=1, source_target_pairs={{0,256},{16,272},{32,288},{48,304},{64,320},{80,336},{96,352},{112... | collective-permute-start | bytes 1388552 | tf_op jit(solution)/shard_map/ppermute | solution.py:202
  19.2 6.4 %collective-permute-start = (s32[1,8]{1,0:T(1,128)S(1)}, s32[1,8]{1,0:T(1,128)S(1)}, u32[]{:S(2)}, u32[]{:S(2)}) collective-permute-start(s32[1,8]{1,0:T(1,128)S(1)} %copy-done.2), channel_id=1, source_target_pairs={{0,256},{1,258},{2,257},{3,260},{4,259},{5,262},{6,261},{7,264},{8... | collective-permute-start | bytes 104 | tf_op jit(solution)/shard_map/ppermute | solution.py:175
  26.4 11.8 %collective-permute-start.3 = (bf16[1040,128]{1,0:T(8,128)(2,1)S(1)}, bf16[1040,128]{1,0:T(8,128)(2,1)S(1)}, u32[]{:S(2)}, u32[]{:S(2)}) collective-permute-start(bf16[1040,128]{1,0:T(8,128)(2,1)S(1)} %get-tuple-element.12), channel_id=1, source_target_pairs={{1,258},{2,257},{3,260},{4,259},{5,262},{6,261},{7,264},{8,263},{9... | collective-permute-start | bytes 798728 | tf_op jit(solution)/shard_map/ppermute | solution.py:208
  28.3 15.9 %collective-permute-start.2 = (bf16[784,128]{1,0:T(8,128)(2,1)S(1)}, bf16[784,128]{1,0:T(8,128)(2,1)S(1)}, u32[]{:S(2)}, u32[]{:S(2)}) collective-permute-start(bf16[784,128]{1,0:T(8,128)(2,1)S(1)} %get-tuple-element.10), channel_id=1, source_target_pairs={{0,256},{1,258},{2,257},{3,260},{4,259},{5,262},{6,261},{7,264},{8... | collective-permute-start | bytes 602120 | tf_op jit(solution)/shard_map/ppermute | solution.py:208

commit v5 on v3

--- a/solution.py
+++ b/solution.py
@@ -7,7 +7,7 @@
 from jax.experimental.pallas import tpu as pltpu
 from jax.sharding import PartitionSpec as P
 
-NEAR, FAR, LAST = 5, 4, 3
+NEAR, FAR, LAST = 5, 5, 3
 IN_NEAR, IN_FAR, IN_LAST = range(3)
 
 
@@ -185,7 +185,7 @@
             pltpu.make_async_copy(results.at[slot], out.at[0, 0], sems.at[slot]).wait()
 
 
-RIGHT_COST = (2 * 10**9,) * 3
+RIGHT_COST = (4*10**9,) * 3
 LEFT_COST = 1
 TINY = pl.CostEstimate(flops=1, bytes_accessed=1, transcendentals=0)
 VMEM = pl.BlockSpec(memory_space=pltpu.VMEM)
@@ -221,7 +221,6 @@
     ]
 
     far_cols = lax.ppermute(coupling_cols, ("dom", "pan"), across)
-    near_cols = lax.ppermute(coupling_cols, "dom", straight)
 
     own, z_row = pl.pallas_call(
         load_kernel,
@@ -247,9 +246,10 @@
         )(*operands)
 
     far, relay = fill(far_kernel, (FAR, slots - FAR), far_cols, own)
-    far, relay, near_cols, given = lax.optimization_barrier((far, relay, near_cols, factor_tiles))
+    far, relay, given, cols = lax.optimization_barrier((far, relay, factor_tiles, coupling_cols))
     far = lax.ppermute(far, ("dom", "pan"), across)
     mate = lax.ppermute(given, "pan", [(panel, panel ^ 1) for panel in range(panels)])
+    near_cols = lax.ppermute(cols, "dom", straight)
     relay = lax.ppermute(relay, ("dom", "pan"), beside)
     (near,) = fill(near_kernel, (NEAR,), near_cols, own, mate)
     near = lax.ppermute(near, "dom", straight)

time: 42.5 us -> 41.4 us (0.974)
  the two profiles are of different devices: /device:TPU:200 before, /device:TPU:1 now
where the time goes in v5:
time: 41.4 us; the launch traced here: 41.1 us
  starting transfers between devices  25.8 us (62%)
  Pallas kernels  10.5 us (25%)
  waiting for transfers between devices  3.93 us (9%)
  between operations  0.81 us (2%)
    pallas_call x3, Pallas kernels, on_device(): pl.pallas_call(functools.partial(right_kernel, wanted, blocks), out_shape...  6.02 us
    ppermute x1, starting transfers between devices, on_device(): far_cols = lax.ppermute(coupling_cols, ('dom', 'pan'), across)  5.77 us
    ppermute x1, starting transfers between devices, on_device(): last = lax.ppermute(last, 'dom', straight)  4.58 us
    ppermute x1, starting transfers between devices, on_device(): relay = lax.ppermute(relay, ('dom', 'pan'), beside)  4.34 us
    ppermute x1, starting transfers between devices, on_device(): lax.ppermute(given, 'pan', [(panel, panel ^ 1) for panel in range(panels)])  3.67 us
    ppermute x1, waiting for transfers between devices, on_device(): near = lax.ppermute(near, 'dom', straight)  3.61 us
    ppermute x1, starting transfers between devices, on_device(): far = lax.ppermute(far, ('dom', 'pan'), across)  2.79 us
    ppermute x1, starting transfers between devices, on_device(): near_cols = lax.ppermute(cols, 'dom', straight)  2.41 us
  transfers between devices with their start and end apart: 7, of which 2 were waited for; matrix products, arithmetic and copies ran while one was open for 0% of the time, Pallas kernels for 19%

profile of v5, /device:TPU:1, one launch (start us, length us, event | category | flops | bytes accessed | tf_op | source)
XLA Modules:
  0.0 41.1 jit_solution(5941074330049465008)
XLA Ops:
  0.0 5.8 %collective-permute-start = (s32[1,8]{1,0:T(1,128)}, s32[1,8]{1,0:T(1,128)S(1)}, u32[]{:S(2)}, u32[]{:S(2)}) collective-permute-start(s32[1,8]{1,0:T(1,128)} %cols.5), channel_id=1, source_target_pairs={{1,258},{2,257},{3,260},{4,259},{5,262},{6,261},{7,264},{8,263},{9... | collective-permute-start | bytes 104 | tf_op jit(solution)/shard_map/ppermute | solution.py:223
  6.4 0.0 copy-start
  6.4 1.7 %load.1 = (bf16[16,256,256]{2,1,0:T(8,128)(2,1)S(1)}, bf16[256,256]{1,0:T(8,128)(2,1)S(1)}) custom-call(s32[1]{0:T(128)S(6)} %copy.9.block, bf16[16,256,256]{2,1,0:T(8,128)(2,1)} %factors.1), custom_call_target="tpu_custom_call" | custom-call | flops 1 | bytes 1 | tf_op jit(solution)/shard_map/load/pallas_call | solution.py:225
  8.1 0.0 collective-permute-done.cols
  8.1 0.0 copy-start.1
  8.2 0.8 %far_kernel.1 = (bf16[1296,128]{1,0:T(8,128)(2,1)S(1)}, bf16[528,128]{1,0:T(8,128)(2,1)S(1)}) custom-call(s32[1,8]{1,0:T(1,128)S(1)} %collective-permute-done.cols, bf16[16,256,256]{2,1,0:T(8,128)(2,1)S(1)} %get-tuple-element.13.own), custom_call_target="tpu_custom_call" | custom-call | flops 1 | bytes 1 | tf_op jit(solution)/shard_map/far_kernel/pallas_call | solution.py:237
  8.9 3.7 %collective-permute-start.2 = (bf16[16,256,256]{2,1,0:T(8,128)(2,1)}, bf16[16,256,256]{2,1,0:T(8,128)(2,1)S(1)}, u32[]{:S(2)}, u32[]{:S(2)}) collective-permute-start(bf16[16,256,256]{2,1,0:T(8,128)(2,1)} %factors.1), channel_id=1, source_target_pairs={{0,1},{1,0},{2,3},{3,2},{4,5},{5,4},{6,7},{7,6},{8,9},{9,8},{10,11... | collective-permute-start | bytes 6291464 | tf_op jit(solution)/shard_map/ppermute | solution.py:251
  12.6 2.8 %collective-permute-start.6 = (bf16[1296,128]{1,0:T(8,128)(2,1)S(1)}, bf16[1296,128]{1,0:T(8,128)(2,1)S(1)}, u32[]{:S(2)}, u32[]{:S(2)}) collective-permute-start(bf16[1296,128]{1,0:T(8,128)(2,1)S(1)} %get-tuple-element.20), channel_id=1, source_target_pairs={{1,258},{2,257},{3,260},{4,259},{5,262},{6,261},{7,264},{8,263},{9... | collective-permute-start | bytes 995336 | tf_op jit(solution)/shard_map/ppermute | solution.py:250
  15.4 0.0 copy-done
  15.4 0.5 %left.1 = bf16[8,256,256]{2,1,0:T(8,128)(2,1)S(1)} custom-call(bf16[256,256]{1,0:T(8,128)(2,1)S(1)} %get-tuple-element.19.z_row, bf16[1,8,256,256]{3,2,1,0:T(8,128)(2,1)S(1)} %copy-done), custom_call_target="tpu_custom_call" | custom-call | flops 1 | bytes 1 | tf_op jit(solution)/shard_map/left/pallas_call | solution.py:260
  15.9 0.0 copy-done.1
  15.9 2.4 %collective-permute-start.1 = (s32[1,8]{1,0:T(1,128)S(1)}, s32[1,8]{1,0:T(1,128)S(1)}, u32[]{:S(2)}, u32[]{:S(2)}) collective-permute-start(s32[1,8]{1,0:T(1,128)S(1)} %copy-done.1), channel_id=1, source_target_pairs={{0,256},{16,272},{32,288},{48,304},{64,320},{80,336},{96,352},{112... | collective-permute-start | bytes 104 | tf_op jit(solution)/shard_map/ppermute | solution.py:252
  18.3 4.3 %collective-permute-start.3 = (bf16[528,128]{1,0:T(8,128)(2,1)S(1)}, bf16[528,128]{1,0:T(8,128)(2,1)S(1)}, u32[]{:S(2)}, u32[]{:S(2)}) collective-permute-start(bf16[528,128]{1,0:T(8,128)(2,1)S(1)} %get-tuple-element.18), channel_id=1, source_target_pairs={{1,2},{2,1},{3,4},{4,3},{5,6},{6,5},{7,8},{8,7},{9,10},{10,9},{11,... | collective-permute-start | bytes 405512 | tf_op jit(solution)/shard_map/ppermute | solution.py:253
  22.7 0.0 collective-permute-done.1.cols
  22.7 0.0 collective-permute-done.2.mate
  22.7 0.8 %near_kernel.1 = bf16[1296,128]{1,0:T(8,128)(2,1)S(1)} custom-call(s32[1,8]{1,0:T(1,128)S(1)} %collective-permute-done.1.cols, bf16[16,256,256]{2,1,0:T(8,128)(2,1)S(1)} %get-tuple-element.13.own, bf16[16,256,256]{2,1,0:T(8,128)(2,1)S(1)} %collective-permute-done.2.mate), custom_call_target="tpu_custom_call" | custom-call | flops 1 | bytes 1 | tf_op jit(solution)/shard_map/near_kernel/pallas_call | solution.py:237
  23.5 2.2 %collective-permute-start.5 = (bf16[1296,128]{1,0:T(8,128)(2,1)S(1)}, bf16[1296,128]{1,0:T(8,128)(2,1)S(1)}, u32[]{:S(2)}, u32[]{:S(2)}) collective-permute-start(bf16[1296,128]{1,0:T(8,128)(2,1)S(1)} %near_kernel.1), channel_id=1, source_target_pairs={{0,256},{16,272},{32,288},{48,304},{64,320},{80,336},{96,352},{112... | collective-permute-start | bytes 995336 | tf_op jit(solution)/shard_map/ppermute | solution.py:255
  25.8 0.0 collective-permute-done.6.received
  25.8 2.0 %right_far.1.rest_0_ = bf16[1,8,256,256]{3,2,1,0:T(8,128)(2,1)} custom-call(s32[1,8]{1,0:T(1,128)S(1)} %copy-done.1, bf16[1296,128]{1,0:T(8,128)(2,1)S(1)} %collective-permute-done.6.received, bf16[8,256,256]{2,1,0:T(8,128)(2,1)S(1)} %left.1, bf16[256,256]{1,0:T(8,128)(2,1)S(1)} %get-tuple-element.19.z_row), custom_call_target="tpu_custom_call" | custom-call | flops 4000000000 | bytes 1 | tf_op jit(solution)/shard_map/right_far/pallas_call | solution.py:272
  27.8 0.0 collective-permute-done.3.relay
  27.8 0.8 %last_kernel.1 = bf16[784,128]{1,0:T(8,128)(2,1)S(1)} custom-call(s32[1,8]{1,0:T(1,128)S(1)} %collective-permute-done.1.cols, bf16[16,256,256]{2,1,0:T(8,128)(2,1)S(1)} %get-tuple-element.13.own, bf16[16,256,256]{2,1,0:T(8,128)(2,1)S(1)} %collective-permute-done.2.mate, bf16[528,128]{1,0:T(8,128)(2,1)S(1)} %collective-permute-done.3.relay), custom_call_target="tpu_custom_call" | custom-call | flops 1 | bytes 1 | tf_op jit(solution)/shard_map/last_kernel/pallas_call | solution.py:237
  28.6 4.6 %collective-permute-start.4 = (bf16[784,128]{1,0:T(8,128)(2,1)S(1)}, bf16[784,128]{1,0:T(8,128)(2,1)S(1)}, u32[]{:S(2)}, u32[]{:S(2)}) collective-permute-start(bf16[784,128]{1,0:T(8,128)(2,1)S(1)} %last_kernel.1), channel_id=1, source_target_pairs={{0,256},{16,272},{32,288},{48,304},{64,320},{80,336},{96,352},{112... | collective-permute-start | bytes 602120 | tf_op jit(solution)/shard_map/ppermute | solution.py:257
  33.2 3.6 %collective-permute-done.5.received = bf16[1296,128]{1,0:T(8,128)(2,1)S(1)} collective-permute-done((bf16[1296,128]{1,0:T(8,128)(2,1)S(1)}, bf16[1296,128]{1,0:T(8,128)(2,1)S(1)}, u32[]{:S(2)}, u32[]{:S(2)}) %collective-permute-start.5) | collective-permute-done | bytes 331808 | tf_op jit(solution)/shard_map/ppermute | solution.py:255
  36.8 2.2 %right_near.1.rest_0_ = bf16[1,8,256,256]{3,2,1,0:T(8,128)(2,1)} custom-call(s32[1,8]{1,0:T(1,128)S(1)} %copy-done.1, bf16[1296,128]{1,0:T(8,128)(2,1)S(1)} %collective-permute-done.5.received, bf16[8,256,256]{2,1,0:T(8,128)(2,1)S(1)} %left.1, bf16[256,256]{1,0:T(8,128)(2,1)S(1)} %get-tuple-element.19.z_row, ...), custom_call_target="tpu_custom_call", output_to_operand_aliasing={{}: (4, {})} | custom-call | flops 4000000000 | bytes 1 | tf_op jit(solution)/shard_map/right_near/pallas_call | solution.py:272
  39.0 0.3 collective-permute-done.4.received
  39.3 1.8 %right_last.1 = bf16[1,8,256,256]{3,2,1,0:T(8,128)(2,1)} custom-call(s32[1,8]{1,0:T(1,128)S(1)} %copy-done.1, bf16[784,128]{1,0:T(8,128)(2,1)S(1)} %collective-permute-done.4.received, bf16[8,256,256]{2,1,0:T(8,128)(2,1)S(1)} %left.1, bf16[256,256]{1,0:T(8,128)(2,1)S(1)} %get-tuple-element.19.z_row, ...), custom_call_target="tpu_custom_call", output_to_operand_aliasing={{}: (4, {})} | custom-call | flops 4000000000 | bytes 1 | tf_op jit(solution)/shard_map/right_last/pallas_call | solution.py:272
Async XLA Ops:
  0.0 8.1 %collective-permute-start = (s32[1,8]{1,0:T(1,128)}, s32[1,8]{1,0:T(1,128)S(1)}, u32[]{:S(2)}, u32[]{:S(2)}) collective-permute-start(s32[1,8]{1,0:T(1,128)} %cols.5), channel_id=1, source_target_pairs={{1,258},{2,257},{3,260},{4,259},{5,262},{6,261},{7,264},{8,263},{9... | collective-permute-start | bytes 104 | tf_op jit(solution)/shard_map/ppermute | solution.py:223
  6.4 9.0 %copy-start = (bf16[1,8,256,256]{3,2,1,0:T(8,128)(2,1)S(1)}, bf16[1,8,256,256]{3,2,1,0:T(8,128)(2,1)}, u32[]{:S(2)}) copy-start(bf16[1,8,256,256]{3,2,1,0:T(8,128)(2,1)} %tiles.1) | copy-start | bytes 3145732
  8.1 7.8 %copy-start.1 = (s32[1,8]{1,0:T(1,128)S(1)}, s32[1,8]{1,0:T(1,128)}, u32[]{:S(2)}) copy-start(s32[1,8]{1,0:T(1,128)} %cols.5) | copy-start | bytes 100
  8.9 13.8 %collective-permute-start.2 = (bf16[16,256,256]{2,1,0:T(8,128)(2,1)}, bf16[16,256,256]{2,1,0:T(8,128)(2,1)S(1)}, u32[]{:S(2)}, u32[]{:S(2)}) collective-permute-start(bf16[16,256,256]{2,1,0:T(8,128)(2,1)} %factors.1), channel_id=1, source_target_pairs={{0,1},{1,0},{2,3},{3,2},{4,5},{5,4},{6,7},{7,6},{8,9},{9,8},{10,11... | collective-permute-start | bytes 6291464 | tf_op jit(solution)/shard_map/ppermute | solution.py:251
  12.6 13.1 %collective-permute-start.6 = (bf16[1296,128]{1,0:T(8,128)(2,1)S(1)}, bf16[1296,128]{1,0:T(8,128)(2,1)S(1)}, u32[]{:S(2)}, u32[]{:S(2)}) collective-permute-start(bf16[1296,128]{1,0:T(8,128)(2,1)S(1)} %get-tuple-element.20), channel_id=1, source_target_pairs={{1,258},{2,257},{3,260},{4,259},{5,262},{6,261},{7,264},{8,263},{9... | collective-permute-start | bytes 995336 | tf_op jit(solution)/shard_map/ppermute | solution.py:250
  15.9 6.8 %collective-permute-start.1 = (s32[1,8]{1,0:T(1,128)S(1)}, s32[1,8]{1,0:T(1,128)S(1)}, u32[]{:S(2)}, u32[]{:S(2)}) collective-permute-start(s32[1,8]{1,0:T(1,128)S(1)} %copy-done.1), channel_id=1, source_target_pairs={{0,256},{16,272},{32,288},{48,304},{64,320},{80,336},{96,352},{112... | collective-permute-start | bytes 104 | tf_op jit(solution)/shard_map/ppermute | solution.py:252
  18.3 9.5 %collective-permute-start.3 = (bf16[528,128]{1,0:T(8,128)(2,1)S(1)}, bf16[528,128]{1,0:T(8,128)(2,1)S(1)}, u32[]{:S(2)}, u32[]{:S(2)}) collective-permute-start(bf16[528,128]{1,0:T(8,128)(2,1)S(1)} %get-tuple-element.18), channel_id=1, source_target_pairs={{1,2},{2,1},{3,4},{4,3},{5,6},{6,5},{7,8},{8,7},{9,10},{10,9},{11,... | collective-permute-start | bytes 405512 | tf_op jit(solution)/shard_map/ppermute | solution.py:253
  23.5 13.3 %collective-permute-start.5 = (bf16[1296,128]{1,0:T(8,128)(2,1)S(1)}, bf16[1296,128]{1,0:T(8,128)(2,1)S(1)}, u32[]{:S(2)}, u32[]{:S(2)}) collective-permute-start(bf16[1296,128]{1,0:T(8,128)(2,1)S(1)} %near_kernel.1), channel_id=1, source_target_pairs={{0,256},{16,272},{32,288},{48,304},{64,320},{80,336},{96,352},{112... | collective-permute-start | bytes 995336 | tf_op jit(solution)/shard_map/ppermute | solution.py:255
  28.6 10.7 %collective-permute-start.4 = (bf16[784,128]{1,0:T(8,128)(2,1)S(1)}, bf16[784,128]{1,0:T(8,128)(2,1)S(1)}, u32[]{:S(2)}, u32[]{:S(2)}) collective-permute-start(bf16[784,128]{1,0:T(8,128)(2,1)S(1)} %last_kernel.1), channel_id=1, source_target_pairs={{0,256},{16,272},{32,288},{48,304},{64,320},{80,336},{96,352},{112... | collective-permute-start | bytes 602120 | tf_op jit(solution)/shard_map/ppermute | solution.py:257

commit v6 on v5

--- a/solution.py
+++ b/solution.py
@@ -7,8 +7,8 @@
 from jax.experimental.pallas import tpu as pltpu
 from jax.sharding import PartitionSpec as P
 
-NEAR, FAR, LAST = 5, 5, 3
-IN_NEAR, IN_FAR, IN_LAST = range(3)
+NEAR, FAR, LAST = 5, 5, 2
+IN_NEAR, IN_FAR, IN_LAST, IN_EXTRA = range(4)
 
 
 def other_panel(panel, panels):
@@ -24,8 +24,9 @@
         used = jnp.where(near, near_used, far_used)
         room = jnp.where(near, NEAR, FAR)
         direct = used < room
-        message = jnp.where(direct, jnp.where(near, IN_NEAR, IN_FAR), IN_LAST)
-        put(k, col, message, jnp.where(direct, used, used - room))
+        over = used - room
+        message = jnp.where(direct, jnp.where(near, IN_NEAR, IN_FAR), jnp.where(over < LAST, IN_LAST, IN_EXTRA))
+        put(k, col, message, jnp.where(direct, used, jnp.where(over < LAST, over, 0)))
         near_used = near_used + near.astype(jnp.int32)
         far_used = far_used + 1 - near.astype(jnp.int32)
 
@@ -111,18 +112,19 @@
         out[size * width :, :] = found.astype(jnp.bfloat16)
 
 
-def last_kernel(cols, own, mate, relay, out, source):
+def last_kernel(cols, own, mate, relay, out, extra_out, source):
     blocks, width, _ = own.shape
     half = width // 2
     relayed = relay.shape[0] // width
     me = lax.axis_index("pan")
-    for slot in range(LAST):
+    for slot in range(LAST + 1):
         source[slot] = jnp.int32(0)
 
     def put(k, col, message, slot):
         local = lax.rem(col, blocks) + jnp.where(lax.div(col, blocks) == me, 0, blocks)
         near = lax.div(col, 2 * blocks) == lax.div(me, 2)
-        source[jnp.where(message == IN_LAST, slot, LAST)] = jnp.where(near, local, 2 * blocks)
+        place = jnp.where(message == IN_LAST, slot, jnp.where(message == IN_EXTRA, LAST, LAST + 1))
+        source[place] = jnp.where(near, local, 2 * blocks)
 
     slots_of(cols, me, blocks, put)
     line = lax.broadcasted_iota(jnp.int32, (16, half), 0)
@@ -135,9 +137,13 @@
         out[base : base + width, :] = jnp.where(theirs, relay[base : base + width, :], out[base : base + width, :])
         found = jnp.where((line == slot) & theirs, relay[relayed * width :, :].astype(jnp.float32), found)
     out[LAST * width :, :] = found.astype(jnp.bfloat16)
-
-
-def right_kernel(wanted, blocks, cols, received, left, z_row, *rest):
+    found = jnp.zeros((16, half), jnp.float32)
+    found = write_slot(extra_out, 0, found, chosen(source[LAST], own, mate), width)
+    extra_out[width:, :] = found.astype(jnp.bfloat16)
+
+
+def right_kernel(wanted, sizes, blocks, cols, left, z_row, *rest):
+    received = rest[: len(wanted)]
     out, results, places, sems = rest[-4:]
     slots, width, _ = results.shape
     half = width // 2
@@ -146,30 +152,34 @@
         places[slot] = jnp.int32(-1)
 
     def put(k, col, message, slot):
-        places[jnp.where(message == wanted, slot, slots)] = jnp.int32(k)
+        place = jnp.int32(slots)
+        for i, kind in enumerate(wanted):
+            place = jnp.where(message == kind, slot + sum(sizes[:i]), place)
+        places[place] = jnp.int32(k)
 
     slots_of(cols, me, blocks, put)
 
     rows, lanes = iotas(half)
-    diagonals = received[slots * width :, :].astype(jnp.float32)
-    for slot in range(slots):
-        k = places[slot]
-        base = slot * width
-        triangle = received[base : base + half, :].astype(jnp.float32)
-        upper = jnp.where(rows <= lanes, triangle, 0.0).astype(jnp.bfloat16)
-        lower = jnp.where(rows < lanes, triangle.T, jnp.where(rows == lanes, diagonals[slot : slot + 1, :], 0.0))
-        lower = lower.astype(jnp.bfloat16)
-        corner = received[base + half : base + width, :]
-        z_col = jnp.concatenate(
-            [
-                jnp.concatenate([upper, corner], axis=1),
-                jnp.concatenate([jnp.zeros_like(lower), lower], axis=1),
-            ],
-            axis=0,
-        )
-        inner = jnp.dot(left[jnp.maximum(k, 0)], z_col, preferred_element_type=jnp.float32)
-        product = jnp.dot(z_row[...], inner.astype(jnp.bfloat16), preferred_element_type=jnp.float32)
-        results[slot] = (-0.5 * product).astype(jnp.bfloat16)
+    for i, size in enumerate(sizes):
+        diagonals = received[i][size * width :, :].astype(jnp.float32)
+        for slot in range(size):
+            base = slot * width
+            triangle = received[i][base : base + half, :].astype(jnp.float32)
+            upper = jnp.where(rows <= lanes, triangle, 0.0).astype(jnp.bfloat16)
+            lower = jnp.where(rows < lanes, triangle.T, jnp.where(rows == lanes, diagonals[slot : slot + 1, :], 0.0))
+            lower = lower.astype(jnp.bfloat16)
+            corner = received[i][base + half : base + width, :]
+            z_col = jnp.concatenate(
+                [
+                    jnp.concatenate([upper, corner], axis=1),
+                    jnp.concatenate([jnp.zeros_like(lower), lower], axis=1),
+                ],
+                axis=0,
+            )
+            place = sum(sizes[:i]) + slot
+            inner = jnp.dot(left[jnp.maximum(places[place], 0)], z_col, preferred_element_type=jnp.float32)
+            product = jnp.dot(z_row[...], inner.astype(jnp.bfloat16), preferred_element_type=jnp.float32)
+            results[place] = (-0.5 * product).astype(jnp.bfloat16)
 
     for slot in range(slots):
         k = places[slot]
@@ -213,6 +223,7 @@
         for panel in range(panels)
         if panel not in ends
     ]
+    at_ends = [(flat(dom, panel), flat(dom ^ (doms // 2), panel)) for dom in range(doms) for panel in ends]
     beside = [
         (flat(dom, panel), flat(dom, other_panel(panel, panels)))
         for dom in range(doms)
@@ -253,9 +264,14 @@
     relay = lax.ppermute(relay, ("dom", "pan"), beside)
     (near,) = fill(near_kernel, (NEAR,), near_cols, own, mate)
     near = lax.ppermute(near, "dom", straight)
-    (last,) = fill(last_kernel, (LAST,), near_cols, own, mate, relay)
+    last, extra = fill(last_kernel, (LAST, 1), near_cols, own, mate, relay)
     last = lax.ppermute(last, "dom", straight)
-    messages = [(IN_FAR, FAR, far), (IN_NEAR, NEAR, near), (IN_LAST, LAST, last)]
+    extra = lax.ppermute(extra, ("dom", "pan"), at_ends)
+    steps = [
+        ((IN_FAR,), (FAR,), (far,)),
+        ((IN_NEAR,), (NEAR,), (near,)),
+        ((IN_LAST, IN_EXTRA), (LAST, 1), (last, extra)),
+    ]
 
     left = pl.pallas_call(
         left_kernel,
@@ -268,22 +284,24 @@
     )(z_row, coupling_tiles)
 
     out = None
-    for wanted, size, message in messages:
+    for i, (wanted, sizes, received) in enumerate(steps):
+        operands = [coupling_cols, left, z_row, *received]
+        total = sum(sizes)
         out = pl.pallas_call(
-            functools.partial(right_kernel, wanted, blocks),
+            functools.partial(right_kernel, wanted, sizes, blocks),
             out_shape=bf16(*coupling_tiles.shape),
-            in_specs=[SMEM, VMEM, VMEM, VMEM] + ([] if out is None else [HBM]),
+            in_specs=[SMEM] + [VMEM] * (len(operands) - 1) + ([] if out is None else [HBM]),
             out_specs=HBM,
             scratch_shapes=[
-                pltpu.VMEM((size, width, width), jnp.bfloat16),
-                pltpu.SMEM((size + 1,), jnp.int32),
-                pltpu.SemaphoreType.DMA((size,)),
+                pltpu.VMEM((total, width, width), jnp.bfloat16),
+                pltpu.SMEM((total + 1,), jnp.int32),
+                pltpu.SemaphoreType.DMA((total,)),
             ],
-            input_output_aliases={} if out is None else {4: 0},
+            input_output_aliases={} if out is None else {len(operands): 0},
             compiler_params=limit,
-            cost_estimate=pl.CostEstimate(flops=RIGHT_COST[wanted], bytes_accessed=1, transcendentals=0),
-            name=("right_near", "right_far", "right_last")[wanted],
-        )(coupling_cols, message, left, z_row, *(() if out is None else (out,)))
+            cost_estimate=pl.CostEstimate(flops=RIGHT_COST[i], bytes_accessed=1, transcendentals=0),
+            name=f"right_{i}",
+        )(*operands, *(() if out is None else (out,)))
     return out
 
 

time: 41.4 us -> 40.8 us (0.986)
  waiting for transfers between devices: 3.93 us -> 2.72 us
  starting transfers between devices: 25.8 us -> 26.4 us
    ppermute x1, waiting for transfers between devices: 3.61 us -> 2.7 us  [on_device(): near = lax.ppermute(near, 'dom', straight)]
    ppermute x0 -> x1, starting transfers between devices: none -> 0.67 us  [on_device(): extra = lax.ppermute(extra, ('dom', 'pan'), at_ends)]
  transfers between devices with their start and end apart: 7 -> 8, of which waited for: 2 -> 1; matrix products, arithmetic and copies ran while one was open for 0% -> 0% of each run, Pallas kernels for 19% -> 20%
where the time goes in v6:
time: 40.8 us; the launch traced here: 40.5 us
  starting transfers between devices  26.4 us (65%)
  Pallas kernels  10.5 us (26%)
  waiting for transfers between devices  2.72 us (7%)
  between operations  0.84 us (2%)
    pallas_call x3, Pallas kernels, on_device(): pl.pallas_call(functools.partial(right_kernel, wanted, sizes, blocks), ou...  6.03 us
    ppermute x1, starting transfers between devices, on_device(): far_cols = lax.ppermute(coupling_cols, ('dom', 'pan'), across)  5.77 us
    ppermute x1, starting transfers between devices, on_device(): last = lax.ppermute(last, 'dom', straight)  4.5 us
    ppermute x1, starting transfers between devices, on_device(): relay = lax.ppermute(relay, ('dom', 'pan'), beside)  4.34 us
    ppermute x1, starting transfers between devices, on_device(): lax.ppermute(given, 'pan', [(panel, panel ^ 1) for panel in range(panels)])  3.67 us
    ppermute x1, starting transfers between devices, on_device(): far = lax.ppermute(far, ('dom', 'pan'), across)  2.79 us
    ppermute x1, waiting for transfers between devices, on_device(): near = lax.ppermute(near, 'dom', straight)  2.7 us
    ppermute x1, starting transfers between devices, on_device(): near_cols = lax.ppermute(cols, 'dom', straight)  2.41 us
  transfers between devices with their start and end apart: 8, of which 1 were waited for; matrix products, arithmetic and copies ran while one was open for 0% of the time, Pallas kernels for 20%

profile of v6, /device:TPU:1, one launch (start us, length us, event | category | flops | bytes accessed | tf_op | source)
XLA Modules:
  0.0 40.5 jit_solution(5097411158041094781)
XLA Ops:
  0.0 5.8 %collective-permute-start = (s32[1,8]{1,0:T(1,128)}, s32[1,8]{1,0:T(1,128)S(1)}, u32[]{:S(2)}, u32[]{:S(2)}) collective-permute-start(s32[1,8]{1,0:T(1,128)} %cols.5), channel_id=1, source_target_pairs={{1,258},{2,257},{3,260},{4,259},{5,262},{6,261},{7,264},{8,263},{9... | collective-permute-start | bytes 104 | tf_op jit(solution)/shard_map/ppermute | solution.py:234
  6.4 0.0 copy-start
  6.4 1.7 %load.1 = (bf16[16,256,256]{2,1,0:T(8,128)(2,1)S(1)}, bf16[256,256]{1,0:T(8,128)(2,1)S(1)}) custom-call(s32[1]{0:T(128)S(6)} %copy.9.block, bf16[16,256,256]{2,1,0:T(8,128)(2,1)} %factors.1), custom_call_target="tpu_custom_call" | custom-call | flops 1 | bytes 1 | tf_op jit(solution)/shard_map/load/pallas_call | solution.py:236
  8.1 0.0 collective-permute-done.cols
  8.1 0.0 copy-start.1
  8.2 0.8 %far_kernel.1 = (bf16[1296,128]{1,0:T(8,128)(2,1)S(1)}, bf16[528,128]{1,0:T(8,128)(2,1)S(1)}) custom-call(s32[1,8]{1,0:T(1,128)S(1)} %collective-permute-done.cols, bf16[16,256,256]{2,1,0:T(8,128)(2,1)S(1)} %get-tuple-element.16.own), custom_call_target="tpu_custom_call" | custom-call | flops 1 | bytes 1 | tf_op jit(solution)/shard_map/far_kernel/pallas_call | solution.py:248
  9.0 3.7 %collective-permute-start.2 = (bf16[16,256,256]{2,1,0:T(8,128)(2,1)}, bf16[16,256,256]{2,1,0:T(8,128)(2,1)S(1)}, u32[]{:S(2)}, u32[]{:S(2)}) collective-permute-start(bf16[16,256,256]{2,1,0:T(8,128)(2,1)} %factors.1), channel_id=1, source_target_pairs={{0,1},{1,0},{2,3},{3,2},{4,5},{5,4},{6,7},{7,6},{8,9},{9,8},{10,11... | collective-permute-start | bytes 6291464 | tf_op jit(solution)/shard_map/ppermute | solution.py:262
  12.6 2.8 %collective-permute-start.7 = (bf16[1296,128]{1,0:T(8,128)(2,1)S(1)}, bf16[1296,128]{1,0:T(8,128)(2,1)S(1)}, u32[]{:S(2)}, u32[]{:S(2)}) collective-permute-start(bf16[1296,128]{1,0:T(8,128)(2,1)S(1)} %get-tuple-element.24), channel_id=1, source_target_pairs={{1,258},{2,257},{3,260},{4,259},{5,262},{6,261},{7,264},{8,263},{9... | collective-permute-start | bytes 995336 | tf_op jit(solution)/shard_map/ppermute | solution.py:261
  15.4 0.0 copy-done
  15.4 0.5 %left.1 = bf16[8,256,256]{2,1,0:T(8,128)(2,1)S(1)} custom-call(bf16[256,256]{1,0:T(8,128)(2,1)S(1)} %get-tuple-element.15.z_row, bf16[1,8,256,256]{3,2,1,0:T(8,128)(2,1)S(1)} %copy-done), custom_call_target="tpu_custom_call" | custom-call | flops 1 | bytes 1 | tf_op jit(solution)/shard_map/left/pallas_call | solution.py:276
  15.9 0.0 copy-done.1
  15.9 2.4 %collective-permute-start.1 = (s32[1,8]{1,0:T(1,128)S(1)}, s32[1,8]{1,0:T(1,128)S(1)}, u32[]{:S(2)}, u32[]{:S(2)}) collective-permute-start(s32[1,8]{1,0:T(1,128)S(1)} %copy-done.1), channel_id=1, source_target_pairs={{0,256},{16,272},{32,288},{48,304},{64,320},{80,336},{96,352},{112... | collective-permute-start | bytes 104 | tf_op jit(solution)/shard_map/ppermute | solution.py:263
  18.3 4.3 %collective-permute-start.3 = (bf16[528,128]{1,0:T(8,128)(2,1)S(1)}, bf16[528,128]{1,0:T(8,128)(2,1)S(1)}, u32[]{:S(2)}, u32[]{:S(2)}) collective-permute-start(bf16[528,128]{1,0:T(8,128)(2,1)S(1)} %get-tuple-element.21), channel_id=1, source_target_pairs={{1,2},{2,1},{3,4},{4,3},{5,6},{6,5},{7,8},{8,7},{9,10},{10,9},{11,... | collective-permute-start | bytes 405512 | tf_op jit(solution)/shard_map/ppermute | solution.py:264
  22.7 0.0 collective-permute-done.1.cols
  22.7 0.0 collective-permute-done.2.mate
  22.7 0.8 %near_kernel.1 = bf16[1296,128]{1,0:T(8,128)(2,1)S(1)} custom-call(s32[1,8]{1,0:T(1,128)S(1)} %collective-permute-done.1.cols, bf16[16,256,256]{2,1,0:T(8,128)(2,1)S(1)} %get-tuple-element.16.own, bf16[16,256,256]{2,1,0:T(8,128)(2,1)S(1)} %collective-permute-done.2.mate), custom_call_target="tpu_custom_call" | custom-call | flops 1 | bytes 1 | tf_op jit(solution)/shard_map/near_kernel/pallas_call | solution.py:248
  23.5 2.2 %collective-permute-start.6 = (bf16[1296,128]{1,0:T(8,128)(2,1)S(1)}, bf16[1296,128]{1,0:T(8,128)(2,1)S(1)}, u32[]{:S(2)}, u32[]{:S(2)}) collective-permute-start(bf16[1296,128]{1,0:T(8,128)(2,1)S(1)} %near_kernel.1), channel_id=1, source_target_pairs={{0,256},{16,272},{32,288},{48,304},{64,320},{80,336},{96,352},{112... | collective-permute-start | bytes 995336 | tf_op jit(solution)/shard_map/ppermute | solution.py:266
  25.8 0.0 collective-permute-done.7.rest_0_
  25.8 2.2 %right_0.1.rest_1_ = bf16[1,8,256,256]{3,2,1,0:T(8,128)(2,1)} custom-call(s32[1,8]{1,0:T(1,128)S(1)} %copy-done.1, bf16[8,256,256]{2,1,0:T(8,128)(2,1)S(1)} %left.1, bf16[256,256]{1,0:T(8,128)(2,1)S(1)} %get-tuple-element.15.z_row, bf16[1296,128]{1,0:T(8,128)(2,1)S(1)} %collective-permute-done.7.rest_0_), custom_call_target="tpu_custom_call" | custom-call | flops 4000000000 | bytes 1 | tf_op jit(solution)/shard_map/right_0/pallas_call | solution.py:290
  27.9 0.0 collective-permute-done.3.relay
  28.0 0.8 %last_kernel.1 = (bf16[528,128]{1,0:T(8,128)(2,1)S(1)}, bf16[272,128]{1,0:T(8,128)(2,1)S(1)}) custom-call(s32[1,8]{1,0:T(1,128)S(1)} %collective-permute-done.1.cols, bf16[16,256,256]{2,1,0:T(8,128)(2,1)S(1)} %get-tuple-element.16.own, bf16[16,256,256]{2,1,0:T(8,128)(2,1)S(1)} %collective-permute-done.2.mate, bf16[528,128]{1,0:T(8,128)(2,1)S(1)} %collective-permute-done.3.relay), custom_call_target="tpu_custom_call" | custom-call | flops 1 | bytes 1 | tf_op jit(solution)/shard_map/last_kernel/pallas_call | solution.py:248
  28.7 4.5 %collective-permute-start.4 = (bf16[528,128]{1,0:T(8,128)(2,1)S(1)}, bf16[528,128]{1,0:T(8,128)(2,1)S(1)}, u32[]{:S(2)}, u32[]{:S(2)}) collective-permute-start(bf16[528,128]{1,0:T(8,128)(2,1)S(1)} %get-tuple-element.22), channel_id=1, source_target_pairs={{0,256},{16,272},{32,288},{48,304},{64,320},{80,336},{96,352},{112... | collective-permute-start | bytes 405512 | tf_op jit(solution)/shard_map/ppermute | solution.py:268
  33.2 0.7 %collective-permute-start.5 = (bf16[272,128]{1,0:T(8,128)(2,1)S(1)}, bf16[272,128]{1,0:T(8,128)(2,1)S(1)}, u32[]{:S(2)}, u32[]{:S(2)}) collective-permute-start(bf16[272,128]{1,0:T(8,128)(2,1)S(1)} %get-tuple-element.23), channel_id=1, source_target_pairs={{0,256},{15,271},{16,272},{31,287},{32,288},{47,303},{48,304},{63,... | collective-permute-start | bytes 208904 | tf_op jit(solution)/shard_map/ppermute | solution.py:269
  33.9 2.7 %collective-permute-done.6.rest_0_ = bf16[1296,128]{1,0:T(8,128)(2,1)S(1)} collective-permute-done((bf16[1296,128]{1,0:T(8,128)(2,1)S(1)}, bf16[1296,128]{1,0:T(8,128)(2,1)S(1)}, u32[]{:S(2)}, u32[]{:S(2)}) %collective-permute-start.6) | collective-permute-done | bytes 331808 | tf_op jit(solution)/shard_map/ppermute | solution.py:266
  36.6 2.0 %right_1.1.rest_2_ = bf16[1,8,256,256]{3,2,1,0:T(8,128)(2,1)} custom-call(s32[1,8]{1,0:T(1,128)S(1)} %copy-done.1, bf16[8,256,256]{2,1,0:T(8,128)(2,1)S(1)} %left.1, bf16[256,256]{1,0:T(8,128)(2,1)S(1)} %get-tuple-element.15.z_row, bf16[1296,128]{1,0:T(8,128)(2,1)S(1)} %collective-permute-done.6.rest_0_, ...), custom_call_target="tpu_custom_call", output_to_operand_aliasing={{}: (4, {})} | custom-call | flops 4000000000 | bytes 1 | tf_op jit(solution)/shard_map/right_1/pallas_call | solution.py:290
  38.6 0.0 collective-permute-done.5.rest_1_
  38.7 0.0 collective-permute-done.4.rest_0_
  38.7 1.8 %right_2.1 = bf16[1,8,256,256]{3,2,1,0:T(8,128)(2,1)} custom-call(s32[1,8]{1,0:T(1,128)S(1)} %copy-done.1, bf16[8,256,256]{2,1,0:T(8,128)(2,1)S(1)} %left.1, bf16[256,256]{1,0:T(8,128)(2,1)S(1)} %get-tuple-element.15.z_row, bf16[528,128]{1,0:T(8,128)(2,1)S(1)} %collective-permute-done.4.rest_0_, ...), custom_call_target="tpu_custom_call", output_to_operand_aliasing={{}: (5, {})} | custom-call | flops 4000000000 | bytes 1 | tf_op jit(solution)/shard_map/right_2/pallas_call | solution.py:290
Async XLA Ops:
  0.0 8.1 %collective-permute-start = (s32[1,8]{1,0:T(1,128)}, s32[1,8]{1,0:T(1,128)S(1)}, u32[]{:S(2)}, u32[]{:S(2)}) collective-permute-start(s32[1,8]{1,0:T(1,128)} %cols.5), channel_id=1, source_target_pairs={{1,258},{2,257},{3,260},{4,259},{5,262},{6,261},{7,264},{8,263},{9... | collective-permute-start | bytes 104 | tf_op jit(solution)/shard_map/ppermute | solution.py:234
  6.4 9.0 %copy-start = (bf16[1,8,256,256]{3,2,1,0:T(8,128)(2,1)S(1)}, bf16[1,8,256,256]{3,2,1,0:T(8,128)(2,1)}, u32[]{:S(2)}) copy-start(bf16[1,8,256,256]{3,2,1,0:T(8,128)(2,1)} %tiles.1) | copy-start | bytes 3145732
  8.1 7.8 %copy-start.1 = (s32[1,8]{1,0:T(1,128)S(1)}, s32[1,8]{1,0:T(1,128)}, u32[]{:S(2)}) copy-start(s32[1,8]{1,0:T(1,128)} %cols.5) | copy-start | bytes 100
  9.0 13.8 %collective-permute-start.2 = (bf16[16,256,256]{2,1,0:T(8,128)(2,1)}, bf16[16,256,256]{2,1,0:T(8,128)(2,1)S(1)}, u32[]{:S(2)}, u32[]{:S(2)}) collective-permute-start(bf16[16,256,256]{2,1,0:T(8,128)(2,1)} %factors.1), channel_id=1, source_target_pairs={{0,1},{1,0},{2,3},{3,2},{4,5},{5,4},{6,7},{7,6},{8,9},{9,8},{10,11... | collective-permute-start | bytes 6291464 | tf_op jit(solution)/shard_map/ppermute | solution.py:262
  12.6 13.1 %collective-permute-start.7 = (bf16[1296,128]{1,0:T(8,128)(2,1)S(1)}, bf16[1296,128]{1,0:T(8,128)(2,1)S(1)}, u32[]{:S(2)}, u32[]{:S(2)}) collective-permute-start(bf16[1296,128]{1,0:T(8,128)(2,1)S(1)} %get-tuple-element.24), channel_id=1, source_target_pairs={{1,258},{2,257},{3,260},{4,259},{5,262},{6,261},{7,264},{8,263},{9... | collective-permute-start | bytes 995336 | tf_op jit(solution)/shard_map/ppermute | solution.py:261
  15.9 6.8 %collective-permute-start.1 = (s32[1,8]{1,0:T(1,128)S(1)}, s32[1,8]{1,0:T(1,128)S(1)}, u32[]{:S(2)}, u32[]{:S(2)}) collective-permute-start(s32[1,8]{1,0:T(1,128)S(1)} %copy-done.1), channel_id=1, source_target_pairs={{0,256},{16,272},{32,288},{48,304},{64,320},{80,336},{96,352},{112... | collective-permute-start | bytes 104 | tf_op jit(solution)/shard_map/ppermute | solution.py:263
  18.3 9.6 %collective-permute-start.3 = (bf16[528,128]{1,0:T(8,128)(2,1)S(1)}, bf16[528,128]{1,0:T(8,128)(2,1)S(1)}, u32[]{:S(2)}, u32[]{:S(2)}) collective-permute-start(bf16[528,128]{1,0:T(8,128)(2,1)S(1)} %get-tuple-element.21), channel_id=1, source_target_pairs={{1,2},{2,1},{3,4},{4,3},{5,6},{6,5},{7,8},{8,7},{9,10},{10,9},{11,... | collective-permute-start | bytes 405512 | tf_op jit(solution)/shard_map/ppermute | solution.py:264
  23.5 13.1 %collective-permute-start.6 = (bf16[1296,128]{1,0:T(8,128)(2,1)S(1)}, bf16[1296,128]{1,0:T(8,128)(2,1)S(1)}, u32[]{:S(2)}, u32[]{:S(2)}) collective-permute-start(bf16[1296,128]{1,0:T(8,128)(2,1)S(1)} %near_kernel.1), channel_id=1, source_target_pairs={{0,256},{16,272},{32,288},{48,304},{64,320},{80,336},{96,352},{112... | collective-permute-start | bytes 995336 | tf_op jit(solution)/shard_map/ppermute | solution.py:266
  28.7 9.9 %collective-permute-start.4 = (bf16[528,128]{1,0:T(8,128)(2,1)S(1)}, bf16[528,128]{1,0:T(8,128)(2,1)S(1)}, u32[]{:S(2)}, u32[]{:S(2)}) collective-permute-start(bf16[528,128]{1,0:T(8,128)(2,1)S(1)} %get-tuple-element.22), channel_id=1, source_target_pairs={{0,256},{16,272},{32,288},{48,304},{64,320},{80,336},{96,352},{112... | collective-permute-start | bytes 405512 | tf_op jit(solution)/shard_map/ppermute | solution.py:268
  33.2 5.4 %collective-permute-start.5 = (bf16[272,128]{1,0:T(8,128)(2,1)S(1)}, bf16[272,128]{1,0:T(8,128)(2,1)S(1)}, u32[]{:S(2)}, u32[]{:S(2)}) collective-permute-start(bf16[272,128]{1,0:T(8,128)(2,1)S(1)} %get-tuple-element.23), channel_id=1, source_target_pairs={{0,256},{15,271},{16,272},{31,287},{32,288},{47,303},{48,304},{63,... | collective-permute-start | bytes 208904 | tf_op jit(solution)/shard_map/ppermute | solution.py:269

commit v7 on v6

--- a/solution.py
+++ b/solution.py
@@ -46,12 +46,6 @@
     copy.wait()
 
 
-def left_kernel(z_row, tiles, left):
-    turned = z_row[...].astype(jnp.float32).T.astype(jnp.bfloat16)
-    for k in range(tiles.shape[1]):
-        left[k] = jnp.dot(turned, tiles[0, k], preferred_element_type=jnp.float32).astype(jnp.bfloat16)
-
-
 def write_slot(out, slot, found, tile_part, width):
     half = width // 2
     rows, lanes = iotas(half)
@@ -140,6 +134,14 @@
     found = jnp.zeros((16, half), jnp.float32)
     found = write_slot(extra_out, 0, found, chosen(source[LAST], own, mate), width)
     extra_out[width:, :] = found.astype(jnp.bfloat16)
+
+
+def first_right_kernel(wanted, sizes, blocks, cols, tiles, z_row, *rest):
+    received, (out, left), scratch = rest[: len(wanted)], rest[len(wanted) : -3], rest[-3:]
+    turned = z_row[...].astype(jnp.float32).T.astype(jnp.bfloat16)
+    for k in range(tiles.shape[1]):
+        left[k] = jnp.dot(turned, tiles[0, k], preferred_element_type=jnp.float32).astype(jnp.bfloat16)
+    right_kernel(wanted, sizes, blocks, cols, left, z_row, *received, out, *scratch)
 
 
 def right_kernel(wanted, sizes, blocks, cols, left, z_row, *rest):
@@ -181,12 +183,9 @@
             product = jnp.dot(z_row[...], inner.astype(jnp.bfloat16), preferred_element_type=jnp.float32)
             results[place] = (-0.5 * product).astype(jnp.bfloat16)
 
-    for slot in range(slots):
-        k = places[slot]
-
-        @pl.when(k >= 0)
-        def _():
-            pltpu.make_async_copy(results.at[slot], out.at[0, k], sems.at[slot]).start()
+            @pl.when(places[place] >= 0)
+            def _():
+                pltpu.make_async_copy(results.at[place], out.at[0, places[place]], sems.at[place]).start()
 
     for slot in range(slots):
 
@@ -195,8 +194,8 @@
             pltpu.make_async_copy(results.at[slot], out.at[0, 0], sems.at[slot]).wait()
 
 
-RIGHT_COST = (4*10**9,) * 3
-LEFT_COST = 1
+FILL_COST = {far_kernel: 4 * 10**10}
+RIGHT_COST = (4 * 10**9,) * 3
 TINY = pl.CostEstimate(flops=1, bytes_accessed=1, transcendentals=0)
 VMEM = pl.BlockSpec(memory_space=pltpu.VMEM)
 SMEM = pl.BlockSpec(memory_space=pltpu.SMEM)
@@ -252,14 +251,14 @@
             out_specs=(VMEM,) * len(sizes),
             scratch_shapes=[pltpu.SMEM((sum(sizes) + 1,), jnp.int32)],
             compiler_params=limit,
-            cost_estimate=TINY,
+            cost_estimate=pl.CostEstimate(flops=FILL_COST.get(kernel, 1), bytes_accessed=1, transcendentals=0),
             name=kernel.__name__,
         )(*operands)
 
+    mate = lax.ppermute(factor_tiles, "pan", [(panel, panel ^ 1) for panel in range(panels)])
     far, relay = fill(far_kernel, (FAR, slots - FAR), far_cols, own)
-    far, relay, given, cols = lax.optimization_barrier((far, relay, factor_tiles, coupling_cols))
+    far, relay, cols = lax.optimization_barrier((far, relay, coupling_cols))
     far = lax.ppermute(far, ("dom", "pan"), across)
-    mate = lax.ppermute(given, "pan", [(panel, panel ^ 1) for panel in range(panels)])
     near_cols = lax.ppermute(cols, "dom", straight)
     relay = lax.ppermute(relay, ("dom", "pan"), beside)
     (near,) = fill(near_kernel, (NEAR,), near_cols, own, mate)
@@ -273,35 +272,29 @@
         ((IN_LAST, IN_EXTRA), (LAST, 1), (last, extra)),
     ]
 
-    left = pl.pallas_call(
-        left_kernel,
-        out_shape=bf16(count, width, width),
-        in_specs=[VMEM, VMEM],
-        out_specs=VMEM,
-        compiler_params=limit,
-        cost_estimate=pl.CostEstimate(flops=LEFT_COST, bytes_accessed=1, transcendentals=0),
-        name="left",
-    )(z_row, coupling_tiles)
-
-    out = None
+    out = left = None
     for i, (wanted, sizes, received) in enumerate(steps):
-        operands = [coupling_cols, left, z_row, *received]
+        begins = out is None
         total = sum(sizes)
-        out = pl.pallas_call(
-            functools.partial(right_kernel, wanted, sizes, blocks),
-            out_shape=bf16(*coupling_tiles.shape),
-            in_specs=[SMEM] + [VMEM] * (len(operands) - 1) + ([] if out is None else [HBM]),
-            out_specs=HBM,
+        operands = [coupling_cols, coupling_tiles if begins else left, z_row, *received]
+        results = pl.pallas_call(
+            functools.partial(first_right_kernel if begins else right_kernel, wanted, sizes, blocks),
+            out_shape=(bf16(*coupling_tiles.shape),) + ((bf16(count, width, width),) if begins else ()),
+            in_specs=[SMEM] + [VMEM] * (len(operands) - 1) + ([] if begins else [HBM]),
+            out_specs=(HBM, VMEM) if begins else (HBM,),
             scratch_shapes=[
                 pltpu.VMEM((total, width, width), jnp.bfloat16),
                 pltpu.SMEM((total + 1,), jnp.int32),
                 pltpu.SemaphoreType.DMA((total,)),
             ],
-            input_output_aliases={} if out is None else {len(operands): 0},
+            input_output_aliases={} if begins else {len(operands): 0},
             compiler_params=limit,
             cost_estimate=pl.CostEstimate(flops=RIGHT_COST[i], bytes_accessed=1, transcendentals=0),
             name=f"right_{i}",
-        )(*operands, *(() if out is None else (out,)))
+        )(*operands, *(() if begins else (out,)))
+        out = results[0]
+        if begins:
+            left = results[1]
     return out
 
 

time: 40.8 us -> 39.6 us (0.971)
  Pallas kernels: 10.5 us -> 8.52 us
  local copies, waits for them, and re-layouts: 0.01 us -> 1.6 us
  waiting for transfers between devices: 2.72 us -> 1.77 us
    unnamed x4 -> x6, local copies, waits for them, and re-layouts: 0.01 us -> 1.6 us
    pallas_call x1, Pallas kernels: 1.7 us -> 0.33 us  [on_device(): pl.pallas_call(load_kernel, out_shape=(bf16(blocks, width, width), bf16(w...]
    ppermute x1, waiting for transfers between devices: 2.7 us -> 1.75 us  [on_device(): near = lax.ppermute(near, 'dom', straight)]
    ppermute x1, starting transfers between devices: 2.41 us -> 3.27 us  [on_device(): near_cols = lax.ppermute(cols, 'dom', straight)]
    ppermute x1, starting transfers between devices: 2.79 us -> 2.05 us  [on_device(): far = lax.ppermute(far, ('dom', 'pan'), across)]
    pallas_call x4 -> x3, Pallas kernels: 6.5 us -> 5.86 us  [on_device(): pl.pallas_call(functools.partial(first_right_kernel if begins else right_...]
  transfers between devices with their start and end apart: 8 -> 8, of which waited for: 1 -> 1; matrix products, arithmetic and copies ran while one was open for 0% -> 0% of each run, Pallas kernels for 20% -> 17%
where the time goes in v7:
time: 39.6 us; the launch traced here: 39.3 us
  starting transfers between devices  26.6 us (67%)
  Pallas kernels  8.52 us (22%)
  waiting for transfers between devices  1.77 us (4%)
  local copies, waits for them, and re-layouts  1.6 us (4%)
  between operations  0.84 us (2%)
    pallas_call x3, Pallas kernels, on_device(): pl.pallas_call(functools.partial(first_right_kernel if begins else right_...  5.86 us
    ppermute x1, starting transfers between devices, on_device(): far_cols = lax.ppermute(coupling_cols, ('dom', 'pan'), across)  5.77 us
    ppermute x1, starting transfers between devices, on_device(): last = lax.ppermute(last, 'dom', straight)  4.54 us
    ppermute x1, starting transfers between devices, on_device(): relay = lax.ppermute(relay, ('dom', 'pan'), beside)  4.34 us
    ppermute x1, starting transfers between devices, on_device(): lax.ppermute(factor_tiles, 'pan', [(panel, panel ^ 1) for panel in range(...  3.67 us
    ppermute x1, starting transfers between devices, on_device(): near_cols = lax.ppermute(cols, 'dom', straight)  3.27 us
    pallas_call x3, Pallas kernels, fill(): pl.pallas_call(kernel, out_shape=tuple((bf16(size * width + 16, half) for...  2.34 us
    ppermute x1, starting transfers between devices, on_device(): near = lax.ppermute(near, 'dom', straight)  2.25 us
  transfers between devices with their start and end apart: 8, of which 1 were waited for; matrix products, arithmetic and copies ran while one was open for 0% of the time, Pallas kernels for 17%

profile of v7, /device:TPU:1, one launch (start us, length us, event | category | flops | bytes accessed | tf_op | source)
XLA Modules:
  0.0 39.3 jit_solution(3357735333184887783)
XLA Ops:
  0.0 5.8 %collective-permute-start = (s32[1,8]{1,0:T(1,128)}, s32[1,8]{1,0:T(1,128)S(1)}, u32[]{:S(2)}, u32[]{:S(2)}) collective-permute-start(s32[1,8]{1,0:T(1,128)} %cols.5), channel_id=1, source_target_pairs={{1,258},{2,257},{3,260},{4,259},{5,262},{6,261},{7,264},{8,263},{9... | collective-permute-start | bytes 104 | tf_op jit(solution)/shard_map/ppermute | solution.py:233
  6.4 3.7 %collective-permute-start.3 = (bf16[16,256,256]{2,1,0:T(8,128)(2,1)}, bf16[16,256,256]{2,1,0:T(8,128)(2,1)S(1)}, u32[]{:S(2)}, u32[]{:S(2)}) collective-permute-start(bf16[16,256,256]{2,1,0:T(8,128)(2,1)} %factors.1), channel_id=1, source_target_pairs={{0,1},{1,0},{2,3},{3,2},{4,5},{5,4},{6,7},{7,6},{8,9},{9,8},{10,11... | collective-permute-start | bytes 6291464 | tf_op jit(solution)/shard_map/ppermute | solution.py:258
  10.1 0.0 copy-start
  10.1 1.6 %copy-done = bf16[16,256,256]{2,1,0:T(8,128)(2,1)S(1)} copy-done((bf16[16,256,256]{2,1,0:T(8,128)(2,1)S(1)}, bf16[16,256,256]{2,1,0:T(8,128)(2,1)}, u32[]{:S(2)}) %copy-start) | copy-done | bytes 2097176
  11.7 0.3 load.1
  12.0 0.0 collective-permute-done.cols
  12.0 0.0 copy-start.2
  12.0 0.8 %far_kernel.1 = (bf16[1296,128]{1,0:T(8,128)(2,1)S(1)}, bf16[528,128]{1,0:T(8,128)(2,1)S(1)}) custom-call(s32[1,8]{1,0:T(1,128)S(1)} %collective-permute-done.cols, bf16[16,256,256]{2,1,0:T(8,128)(2,1)S(1)} %get-tuple-element.17.own), custom_call_target="tpu_custom_call" | custom-call | flops 40000000000 | bytes 1 | tf_op jit(solution)/shard_map/far_kernel/pallas_call | solution.py:247
  12.8 0.0 copy-start.1
  12.9 2.1 %collective-permute-start.1 = (bf16[1296,128]{1,0:T(8,128)(2,1)S(1)}, bf16[1296,128]{1,0:T(8,128)(2,1)S(1)}, u32[]{:S(2)}, u32[]{:S(2)}) collective-permute-start(bf16[1296,128]{1,0:T(8,128)(2,1)S(1)} %get-tuple-element.20), channel_id=1, source_target_pairs={{1,258},{2,257},{3,260},{4,259},{5,262},{6,261},{7,264},{8,263},{9... | collective-permute-start | bytes 995336 | tf_op jit(solution)/shard_map/ppermute | solution.py:261
  14.9 0.0 copy-done.2
  14.9 3.3 %collective-permute-start.2 = (s32[1,8]{1,0:T(1,128)S(1)}, s32[1,8]{1,0:T(1,128)S(1)}, u32[]{:S(2)}, u32[]{:S(2)}) collective-permute-start(s32[1,8]{1,0:T(1,128)S(1)} %copy-done.2), channel_id=1, source_target_pairs={{0,256},{16,272},{32,288},{48,304},{64,320},{80,336},{96,352},{112... | collective-permute-start | bytes 104 | tf_op jit(solution)/shard_map/ppermute | solution.py:262
  18.2 4.3 %collective-permute-start.4 = (bf16[528,128]{1,0:T(8,128)(2,1)S(1)}, bf16[528,128]{1,0:T(8,128)(2,1)S(1)}, u32[]{:S(2)}, u32[]{:S(2)}) collective-permute-start(bf16[528,128]{1,0:T(8,128)(2,1)S(1)} %get-tuple-element.23), channel_id=1, source_target_pairs={{1,2},{2,1},{3,4},{4,3},{5,6},{6,5},{7,8},{8,7},{9,10},{10,9},{11,... | collective-permute-start | bytes 405512 | tf_op jit(solution)/shard_map/ppermute | solution.py:263
  22.6 0.0 collective-permute-done.2.cols
  22.6 0.0 collective-permute-done.3.mate
  22.6 0.8 %near_kernel.1 = bf16[1296,128]{1,0:T(8,128)(2,1)S(1)} custom-call(s32[1,8]{1,0:T(1,128)S(1)} %collective-permute-done.2.cols, bf16[16,256,256]{2,1,0:T(8,128)(2,1)S(1)} %get-tuple-element.17.own, bf16[16,256,256]{2,1,0:T(8,128)(2,1)S(1)} %collective-permute-done.3.mate), custom_call_target="tpu_custom_call" | custom-call | flops 1 | bytes 1 | tf_op jit(solution)/shard_map/near_kernel/pallas_call | solution.py:247
  23.4 2.2 %collective-permute-start.7 = (bf16[1296,128]{1,0:T(8,128)(2,1)S(1)}, bf16[1296,128]{1,0:T(8,128)(2,1)S(1)}, u32[]{:S(2)}, u32[]{:S(2)}) collective-permute-start(bf16[1296,128]{1,0:T(8,128)(2,1)S(1)} %near_kernel.1), channel_id=1, source_target_pairs={{0,256},{16,272},{32,288},{48,304},{64,320},{80,336},{96,352},{112... | collective-permute-start | bytes 995336 | tf_op jit(solution)/shard_map/ppermute | solution.py:265
  25.6 0.0 collective-permute-done.1.rest_0_
  25.6 0.0 copy-done.1
  25.6 2.2 %right_0.1 = (bf16[1,8,256,256]{3,2,1,0:T(8,128)(2,1)}, bf16[8,256,256]{2,1,0:T(8,128)(2,1)S(1)}) custom-call(s32[1,8]{1,0:T(1,128)S(1)} %copy-done.2, bf16[1,8,256,256]{3,2,1,0:T(8,128)(2,1)S(1)} %copy-done.1, bf16[256,256]{1,0:T(8,128)(2,1)S(1)} %get-tuple-element.16.z_row, bf16[1296,128]{1,0:T(8,128)(2,1)S(1)} %collective-permute-done.1.rest_0_), custom_call_target="tpu_custom_call" | custom-call | flops 4000000000 | bytes 1 | tf_op jit(solution)/shard_map/right_0/pallas_call | solution.py:280
  27.8 0.0 collective-permute-done.4.relay
  27.8 0.8 %last_kernel.1 = (bf16[528,128]{1,0:T(8,128)(2,1)S(1)}, bf16[272,128]{1,0:T(8,128)(2,1)S(1)}) custom-call(s32[1,8]{1,0:T(1,128)S(1)} %collective-permute-done.2.cols, bf16[16,256,256]{2,1,0:T(8,128)(2,1)S(1)} %get-tuple-element.17.own, bf16[16,256,256]{2,1,0:T(8,128)(2,1)S(1)} %collective-permute-done.3.mate, bf16[528,128]{1,0:T(8,128)(2,1)S(1)} %collective-permute-done.4.relay), custom_call_target="tpu_custom_call" | custom-call | flops 1 | bytes 1 | tf_op jit(solution)/shard_map/last_kernel/pallas_call | solution.py:247
  28.6 0.7 %collective-permute-start.6 = (bf16[272,128]{1,0:T(8,128)(2,1)S(1)}, bf16[272,128]{1,0:T(8,128)(2,1)S(1)}, u32[]{:S(2)}, u32[]{:S(2)}) collective-permute-start(bf16[272,128]{1,0:T(8,128)(2,1)S(1)} %get-tuple-element.25), channel_id=1, source_target_pairs={{0,256},{15,271},{16,272},{31,287},{32,288},{47,303},{48,304},{63,... | collective-permute-start | bytes 208904 | tf_op jit(solution)/shard_map/ppermute | solution.py:268
  29.3 4.5 %collective-permute-start.5 = (bf16[528,128]{1,0:T(8,128)(2,1)S(1)}, bf16[528,128]{1,0:T(8,128)(2,1)S(1)}, u32[]{:S(2)}, u32[]{:S(2)}) collective-permute-start(bf16[528,128]{1,0:T(8,128)(2,1)S(1)} %get-tuple-element.24), channel_id=1, source_target_pairs={{0,256},{16,272},{32,288},{48,304},{64,320},{80,336},{96,352},{112... | collective-permute-start | bytes 405512 | tf_op jit(solution)/shard_map/ppermute | solution.py:267
  33.8 1.7 %collective-permute-done.7.rest_0_ = bf16[1296,128]{1,0:T(8,128)(2,1)S(1)} collective-permute-done((bf16[1296,128]{1,0:T(8,128)(2,1)S(1)}, bf16[1296,128]{1,0:T(8,128)(2,1)S(1)}, u32[]{:S(2)}, u32[]{:S(2)}) %collective-permute-start.7) | collective-permute-done | bytes 331808 | tf_op jit(solution)/shard_map/ppermute | solution.py:265
  35.6 2.0 %right_1.1.rest_2_ = bf16[1,8,256,256]{3,2,1,0:T(8,128)(2,1)} custom-call(s32[1,8]{1,0:T(1,128)S(1)} %copy-done.2, bf16[8,256,256]{2,1,0:T(8,128)(2,1)S(1)} %get-tuple-element.21.left, bf16[256,256]{1,0:T(8,128)(2,1)S(1)} %get-tuple-element.16.z_row, bf16[1296,128]{1,0:T(8,128)(2,1)S(1)} %collective-permute-done.7.rest_0_, ...), custom_call_target="tpu_custom_call", output_to_operand_aliasing={{}: (4, {})} | custom-call | flops 4000000000 | bytes 1 | tf_op jit(solution)/shard_map/right_1/pallas_call | solution.py:280
  37.6 0.0 collective-permute-done.6.rest_1_
  37.6 0.0 collective-permute-done.5.rest_0_
  37.6 1.7 %right_2.1 = bf16[1,8,256,256]{3,2,1,0:T(8,128)(2,1)} custom-call(s32[1,8]{1,0:T(1,128)S(1)} %copy-done.2, bf16[8,256,256]{2,1,0:T(8,128)(2,1)S(1)} %get-tuple-element.21.left, bf16[256,256]{1,0:T(8,128)(2,1)S(1)} %get-tuple-element.16.z_row, bf16[528,128]{1,0:T(8,128)(2,1)S(1)} %collective-permute-done.5.rest_0_, ...), custom_call_target="tpu_custom_call", output_to_operand_aliasing={{}: (5, {})} | custom-call | flops 4000000000 | bytes 1 | tf_op jit(solution)/shard_map/right_2/pallas_call | solution.py:280
Async XLA Ops:
  0.0 12.0 %collective-permute-start = (s32[1,8]{1,0:T(1,128)}, s32[1,8]{1,0:T(1,128)S(1)}, u32[]{:S(2)}, u32[]{:S(2)}) collective-permute-start(s32[1,8]{1,0:T(1,128)} %cols.5), channel_id=1, source_target_pairs={{1,258},{2,257},{3,260},{4,259},{5,262},{6,261},{7,264},{8,263},{9... | collective-permute-start | bytes 104 | tf_op jit(solution)/shard_map/ppermute | solution.py:233
  6.4 16.1 %collective-permute-start.3 = (bf16[16,256,256]{2,1,0:T(8,128)(2,1)}, bf16[16,256,256]{2,1,0:T(8,128)(2,1)S(1)}, u32[]{:S(2)}, u32[]{:S(2)}) collective-permute-start(bf16[16,256,256]{2,1,0:T(8,128)(2,1)} %factors.1), channel_id=1, source_target_pairs={{0,1},{1,0},{2,3},{3,2},{4,5},{5,4},{6,7},{7,6},{8,9},{9,8},{10,11... | collective-permute-start | bytes 6291464 | tf_op jit(solution)/shard_map/ppermute | solution.py:258
  10.1 1.6 %copy-start = (bf16[16,256,256]{2,1,0:T(8,128)(2,1)S(1)}, bf16[16,256,256]{2,1,0:T(8,128)(2,1)}, u32[]{:S(2)}) copy-start(bf16[16,256,256]{2,1,0:T(8,128)(2,1)} %factors.1) | copy-start | bytes 6291460
  12.0 2.9 %copy-start.2 = (s32[1,8]{1,0:T(1,128)S(1)}, s32[1,8]{1,0:T(1,128)}, u32[]{:S(2)}) copy-start(s32[1,8]{1,0:T(1,128)} %cols.5) | copy-start | bytes 100
  12.8 12.8 %copy-start.1 = (bf16[1,8,256,256]{3,2,1,0:T(8,128)(2,1)S(1)}, bf16[1,8,256,256]{3,2,1,0:T(8,128)(2,1)}, u32[]{:S(2)}) copy-start(bf16[1,8,256,256]{3,2,1,0:T(8,128)(2,1)} %tiles.1) | copy-start | bytes 3145732
  12.9 12.8 %collective-permute-start.1 = (bf16[1296,128]{1,0:T(8,128)(2,1)S(1)}, bf16[1296,128]{1,0:T(8,128)(2,1)S(1)}, u32[]{:S(2)}, u32[]{:S(2)}) collective-permute-start(bf16[1296,128]{1,0:T(8,128)(2,1)S(1)} %get-tuple-element.20), channel_id=1, source_target_pairs={{1,258},{2,257},{3,260},{4,259},{5,262},{6,261},{7,264},{8,263},{9... | collective-permute-start | bytes 995336 | tf_op jit(solution)/shard_map/ppermute | solution.py:261
  14.9 7.6 %collective-permute-start.2 = (s32[1,8]{1,0:T(1,128)S(1)}, s32[1,8]{1,0:T(1,128)S(1)}, u32[]{:S(2)}, u32[]{:S(2)}) collective-permute-start(s32[1,8]{1,0:T(1,128)S(1)} %copy-done.2), channel_id=1, source_target_pairs={{0,256},{16,272},{32,288},{48,304},{64,320},{80,336},{96,352},{112... | collective-permute-start | bytes 104 | tf_op jit(solution)/shard_map/ppermute | solution.py:262
  18.2 9.6 %collective-permute-start.4 = (bf16[528,128]{1,0:T(8,128)(2,1)S(1)}, bf16[528,128]{1,0:T(8,128)(2,1)S(1)}, u32[]{:S(2)}, u32[]{:S(2)}) collective-permute-start(bf16[528,128]{1,0:T(8,128)(2,1)S(1)} %get-tuple-element.23), channel_id=1, source_target_pairs={{1,2},{2,1},{3,4},{4,3},{5,6},{6,5},{7,8},{8,7},{9,10},{10,9},{11,... | collective-permute-start | bytes 405512 | tf_op jit(solution)/shard_map/ppermute | solution.py:263
  23.4 12.2 %collective-permute-start.7 = (bf16[1296,128]{1,0:T(8,128)(2,1)S(1)}, bf16[1296,128]{1,0:T(8,128)(2,1)S(1)}, u32[]{:S(2)}, u32[]{:S(2)}) collective-permute-start(bf16[1296,128]{1,0:T(8,128)(2,1)S(1)} %near_kernel.1), channel_id=1, source_target_pairs={{0,256},{16,272},{32,288},{48,304},{64,320},{80,336},{96,352},{112... | collective-permute-start | bytes 995336 | tf_op jit(solution)/shard_map/ppermute | solution.py:265
  28.6 9.0 %collective-permute-start.6 = (bf16[272,128]{1,0:T(8,128)(2,1)S(1)}, bf16[272,128]{1,0:T(8,128)(2,1)S(1)}, u32[]{:S(2)}, u32[]{:S(2)}) collective-permute-start(bf16[272,128]{1,0:T(8,128)(2,1)S(1)} %get-tuple-element.25), channel_id=1, source_target_pairs={{0,256},{15,271},{16,272},{31,287},{32,288},{47,303},{48,304},{63,... | collective-permute-start | bytes 208904 | tf_op jit(solution)/shard_map/ppermute | solution.py:268
  29.3 8.3 %collective-permute-start.5 = (bf16[528,128]{1,0:T(8,128)(2,1)S(1)}, bf16[528,128]{1,0:T(8,128)(2,1)S(1)}, u32[]{:S(2)}, u32[]{:S(2)}) collective-permute-start(bf16[528,128]{1,0:T(8,128)(2,1)S(1)} %get-tuple-element.24), channel_id=1, source_target_pairs={{0,256},{16,272},{32,288},{48,304},{64,320},{80,336},{96,352},{112... | collective-permute-start | bytes 405512 | tf_op jit(solution)/shard_map/ppermute | solution.py:267

commit v8 on v7

--- a/solution.py
+++ b/solution.py
@@ -241,7 +241,7 @@
         compiler_params=limit,
         cost_estimate=TINY,
         name="load",
-    )(row_blocks, factor_tiles)
+    )(row_blocks, pltpu.with_memory_space_constraint(factor_tiles, pltpu.HBM))
 
     def fill(kernel, sizes, *operands):
         return pl.pallas_call(
@@ -256,8 +256,8 @@
         )(*operands)
 
     mate = lax.ppermute(factor_tiles, "pan", [(panel, panel ^ 1) for panel in range(panels)])
+    own, cols = lax.optimization_barrier((own, coupling_cols))
     far, relay = fill(far_kernel, (FAR, slots - FAR), far_cols, own)
-    far, relay, cols = lax.optimization_barrier((far, relay, coupling_cols))
     far = lax.ppermute(far, ("dom", "pan"), across)
     near_cols = lax.ppermute(cols, "dom", straight)
     relay = lax.ppermute(relay, ("dom", "pan"), beside)

time: 39.6 us -> 39.1 us (0.987)
  the two profiles are of different devices: /device:TPU:1 before, /device:TPU:2 now
where the time goes in v8:
time: 39.1 us; the launch traced here: 38.7 us
  starting transfers between devices  24.4 us (62%)
  Pallas kernels  9.36 us (24%)
  waiting for transfers between devices  4.11 us (11%)
  between operations  0.82 us (2%)
    ppermute x1, starting transfers between devices, on_device(): near_cols = lax.ppermute(cols, 'dom', straight)  6.12 us
    pallas_call x3, Pallas kernels, on_device(): pl.pallas_call(functools.partial(first_right_kernel if begins else right_...  5.41 us
    ppermute x1, starting transfers between devices, on_device(): near = lax.ppermute(near, 'dom', straight)  4.84 us
    ppermute x1, starting transfers between devices, on_device(): lax.ppermute(factor_tiles, 'pan', [(panel, panel ^ 1) for panel in range(...  3.6 us
    ppermute x1, waiting for transfers between devices, on_device(): near = lax.ppermute(near, 'dom', straight)  2.99 us
    ppermute x1, starting transfers between devices, on_device(): far_cols = lax.ppermute(coupling_cols, ('dom', 'pan'), across)  2.83 us
    ppermute x1, starting transfers between devices, on_device(): last = lax.ppermute(last, 'dom', straight)  2.37 us
    pallas_call x3, Pallas kernels, fill(): pl.pallas_call(kernel, out_shape=tuple((bf16(size * width + 16, half) for...  2.34 us
  transfers between devices with their start and end apart: 8, of which 2 were waited for; matrix products, arithmetic and copies ran while one was open for 0% of the time, Pallas kernels for 21%

profile of v8, /device:TPU:2, one launch (start us, length us, event | category | flops | bytes accessed | tf_op | source)
XLA Modules:
  0.0 38.7 jit_solution(610392015653497583)
XLA Ops:
  0.0 2.8 %collective-permute-start = (s32[1,8]{1,0:T(1,128)}, s32[1,8]{1,0:T(1,128)S(1)}, u32[]{:S(2)}, u32[]{:S(2)}) collective-permute-start(s32[1,8]{1,0:T(1,128)} %cols.5), channel_id=1, source_target_pairs={{1,258},{2,257},{3,260},{4,259},{5,262},{6,261},{7,264},{8,263},{9... | collective-permute-start | bytes 104 | tf_op jit(solution)/shard_map/ppermute | solution.py:233
  3.5 3.6 %collective-permute-start.3 = (bf16[16,256,256]{2,1,0:T(8,128)(2,1)}, bf16[16,256,256]{2,1,0:T(8,128)(2,1)S(1)}, u32[]{:S(2)}, u32[]{:S(2)}) collective-permute-start(bf16[16,256,256]{2,1,0:T(8,128)(2,1)} %factors.1), channel_id=1, source_target_pairs={{0,1},{1,0},{2,3},{3,2},{4,5},{5,4},{6,7},{7,6},{8,9},{9,8},{10,11... | collective-permute-start | bytes 6291464 | tf_op jit(solution)/shard_map/ppermute | solution.py:258
  7.1 1.6 %load.1 = (bf16[16,256,256]{2,1,0:T(8,128)(2,1)S(1)}, bf16[256,256]{1,0:T(8,128)(2,1)S(1)}) custom-call(s32[1]{0:T(128)S(6)} %copy.9.block, bf16[16,256,256]{2,1,0:T(8,128)(2,1)} %factors.1), custom_call_target="tpu_custom_call" | custom-call | flops 1 | bytes 1 | tf_op jit(solution)/shard_map/load/pallas_call | solution.py:235
  8.7 0.0 copy-start.1
  8.7 0.0 collective-permute-done.cols
  8.7 0.8 %far_kernel.1 = (bf16[1296,128]{1,0:T(8,128)(2,1)S(1)}, bf16[528,128]{1,0:T(8,128)(2,1)S(1)}) custom-call(s32[1,8]{1,0:T(1,128)S(1)} %collective-permute-done.cols, bf16[16,256,256]{2,1,0:T(8,128)(2,1)S(1)} %get-tuple-element.17.own), custom_call_target="tpu_custom_call" | custom-call | flops 40000000000 | bytes 1 | tf_op jit(solution)/shard_map/far_kernel/pallas_call | solution.py:247
  9.5 1.9 %collective-permute-start.1 = (bf16[1296,128]{1,0:T(8,128)(2,1)S(1)}, bf16[1296,128]{1,0:T(8,128)(2,1)S(1)}, u32[]{:S(2)}, u32[]{:S(2)}) collective-permute-start(bf16[1296,128]{1,0:T(8,128)(2,1)S(1)} %get-tuple-element.18), channel_id=1, source_target_pairs={{1,258},{2,257},{3,260},{4,259},{5,262},{6,261},{7,264},{8,263},{9... | collective-permute-start | bytes 995336 | tf_op jit(solution)/shard_map/ppermute | solution.py:261
  11.4 0.0 copy-done.1
  11.5 6.1 %collective-permute-start.2 = (s32[1,8]{1,0:T(1,128)S(1)}, s32[1,8]{1,0:T(1,128)S(1)}, u32[]{:S(2)}, u32[]{:S(2)}) collective-permute-start(s32[1,8]{1,0:T(1,128)S(1)} %copy-done.1), channel_id=1, source_target_pairs={{0,256},{16,272},{32,288},{48,304},{64,320},{80,336},{96,352},{112... | collective-permute-start | bytes 104 | tf_op jit(solution)/shard_map/ppermute | solution.py:262
  17.6 0.0 copy-start
  17.6 2.1 %collective-permute-start.4 = (bf16[528,128]{1,0:T(8,128)(2,1)S(1)}, bf16[528,128]{1,0:T(8,128)(2,1)S(1)}, u32[]{:S(2)}, u32[]{:S(2)}) collective-permute-start(bf16[528,128]{1,0:T(8,128)(2,1)S(1)} %get-tuple-element.21), channel_id=1, source_target_pairs={{1,2},{2,1},{3,4},{4,3},{5,6},{6,5},{7,8},{8,7},{9,10},{10,9},{11,... | collective-permute-start | bytes 405512 | tf_op jit(solution)/shard_map/ppermute | solution.py:263
  19.7 0.0 collective-permute-done.2.cols
  19.7 0.0 collective-permute-done.3.mate
  19.7 0.8 %near_kernel.1 = bf16[1296,128]{1,0:T(8,128)(2,1)S(1)} custom-call(s32[1,8]{1,0:T(1,128)S(1)} %collective-permute-done.2.cols, bf16[16,256,256]{2,1,0:T(8,128)(2,1)S(1)} %get-tuple-element.17.own, bf16[16,256,256]{2,1,0:T(8,128)(2,1)S(1)} %collective-permute-done.3.mate), custom_call_target="tpu_custom_call" | custom-call | flops 1 | bytes 1 | tf_op jit(solution)/shard_map/near_kernel/pallas_call | solution.py:247
  20.5 4.8 %collective-permute-start.7 = (bf16[1296,128]{1,0:T(8,128)(2,1)S(1)}, bf16[1296,128]{1,0:T(8,128)(2,1)S(1)}, u32[]{:S(2)}, u32[]{:S(2)}) collective-permute-start(bf16[1296,128]{1,0:T(8,128)(2,1)S(1)} %near_kernel.1), channel_id=1, source_target_pairs={{0,256},{16,272},{32,288},{48,304},{64,320},{80,336},{96,352},{112... | collective-permute-start | bytes 995336 | tf_op jit(solution)/shard_map/ppermute | solution.py:265
  25.3 0.0 collective-permute-done.1.rest_0_
  25.3 0.0 copy-done
  25.3 2.3 %right_0.1 = (bf16[1,8,256,256]{3,2,1,0:T(8,128)(2,1)}, bf16[8,256,256]{2,1,0:T(8,128)(2,1)S(1)}) custom-call(s32[1,8]{1,0:T(1,128)S(1)} %copy-done.1, bf16[1,8,256,256]{3,2,1,0:T(8,128)(2,1)S(1)} %copy-done, bf16[256,256]{1,0:T(8,128)(2,1)S(1)} %get-tuple-element.15.z_row, bf16[1296,128]{1,0:T(8,128)(2,1)S(1)} %collective-permute-done.1.rest_0_), custom_call_target="tpu_custom_call" | custom-call | flops 4000000000 | bytes 1 | tf_op jit(solution)/shard_map/right_0/pallas_call | solution.py:280
  27.7 0.0 collective-permute-done.4.relay
  27.7 0.8 %last_kernel.1 = (bf16[528,128]{1,0:T(8,128)(2,1)S(1)}, bf16[272,128]{1,0:T(8,128)(2,1)S(1)}) custom-call(s32[1,8]{1,0:T(1,128)S(1)} %collective-permute-done.2.cols, bf16[16,256,256]{2,1,0:T(8,128)(2,1)S(1)} %get-tuple-element.17.own, bf16[16,256,256]{2,1,0:T(8,128)(2,1)S(1)} %collective-permute-done.3.mate, bf16[528,128]{1,0:T(8,128)(2,1)S(1)} %collective-permute-done.4.relay), custom_call_target="tpu_custom_call" | custom-call | flops 1 | bytes 1 | tf_op jit(solution)/shard_map/last_kernel/pallas_call | solution.py:247
  28.4 0.7 %collective-permute-start.6 = (bf16[272,128]{1,0:T(8,128)(2,1)S(1)}, bf16[272,128]{1,0:T(8,128)(2,1)S(1)}, u32[]{:S(2)}, u32[]{:S(2)}) collective-permute-start(bf16[272,128]{1,0:T(8,128)(2,1)S(1)} %get-tuple-element.23), channel_id=1, source_target_pairs={{0,256},{15,271},{16,272},{31,287},{32,288},{47,303},{48,304},{63,... | collective-permute-start | bytes 208904 | tf_op jit(solution)/shard_map/ppermute | solution.py:268
  29.1 2.4 %collective-permute-start.5 = (bf16[528,128]{1,0:T(8,128)(2,1)S(1)}, bf16[528,128]{1,0:T(8,128)(2,1)S(1)}, u32[]{:S(2)}, u32[]{:S(2)}) collective-permute-start(bf16[528,128]{1,0:T(8,128)(2,1)S(1)} %get-tuple-element.22), channel_id=1, source_target_pairs={{0,256},{16,272},{32,288},{48,304},{64,320},{80,336},{96,352},{112... | collective-permute-start | bytes 405512 | tf_op jit(solution)/shard_map/ppermute | solution.py:267
  31.5 3.0 %collective-permute-done.7.rest_0_ = bf16[1296,128]{1,0:T(8,128)(2,1)S(1)} collective-permute-done((bf16[1296,128]{1,0:T(8,128)(2,1)S(1)}, bf16[1296,128]{1,0:T(8,128)(2,1)S(1)}, u32[]{:S(2)}, u32[]{:S(2)}) %collective-permute-start.7) | collective-permute-done | bytes 331808 | tf_op jit(solution)/shard_map/ppermute | solution.py:265
  34.5 1.9 %right_1.1.rest_2_ = bf16[1,8,256,256]{3,2,1,0:T(8,128)(2,1)} custom-call(s32[1,8]{1,0:T(1,128)S(1)} %copy-done.1, bf16[8,256,256]{2,1,0:T(8,128)(2,1)S(1)} %get-tuple-element.19.left, bf16[256,256]{1,0:T(8,128)(2,1)S(1)} %get-tuple-element.15.z_row, bf16[1296,128]{1,0:T(8,128)(2,1)S(1)} %collective-permute-done.7.rest_0_, ...), custom_call_target="tpu_custom_call", output_to_operand_aliasing={{}: (4, {})} | custom-call | flops 4000000000 | bytes 1 | tf_op jit(solution)/shard_map/right_1/pallas_call | solution.py:280
  36.4 0.0 collective-permute-done.6.rest_1_
  36.4 1.1 %collective-permute-done.5.rest_0_ = bf16[528,128]{1,0:T(8,128)(2,1)S(1)} collective-permute-done((bf16[528,128]{1,0:T(8,128)(2,1)S(1)}, bf16[528,128]{1,0:T(8,128)(2,1)S(1)}, u32[]{:S(2)}, u32[]{:S(2)}) %collective-permute-start.5) | collective-permute-done | bytes 135200 | tf_op jit(solution)/shard_map/ppermute | solution.py:267
  37.5 1.2 %right_2.1 = bf16[1,8,256,256]{3,2,1,0:T(8,128)(2,1)} custom-call(s32[1,8]{1,0:T(1,128)S(1)} %copy-done.1, bf16[8,256,256]{2,1,0:T(8,128)(2,1)S(1)} %get-tuple-element.19.left, bf16[256,256]{1,0:T(8,128)(2,1)S(1)} %get-tuple-element.15.z_row, bf16[528,128]{1,0:T(8,128)(2,1)S(1)} %collective-permute-done.5.rest_0_, ...), custom_call_target="tpu_custom_call", output_to_operand_aliasing={{}: (5, {})} | custom-call | flops 4000000000 | bytes 1 | tf_op jit(solution)/shard_map/right_2/pallas_call | solution.py:280
Async XLA Ops:
  0.0 8.7 %collective-permute-start = (s32[1,8]{1,0:T(1,128)}, s32[1,8]{1,0:T(1,128)S(1)}, u32[]{:S(2)}, u32[]{:S(2)}) collective-permute-start(s32[1,8]{1,0:T(1,128)} %cols.5), channel_id=1, source_target_pairs={{1,258},{2,257},{3,260},{4,259},{5,262},{6,261},{7,264},{8,263},{9... | collective-permute-start | bytes 104 | tf_op jit(solution)/shard_map/ppermute | solution.py:233
  3.5 16.2 %collective-permute-start.3 = (bf16[16,256,256]{2,1,0:T(8,128)(2,1)}, bf16[16,256,256]{2,1,0:T(8,128)(2,1)S(1)}, u32[]{:S(2)}, u32[]{:S(2)}) collective-permute-start(bf16[16,256,256]{2,1,0:T(8,128)(2,1)} %factors.1), channel_id=1, source_target_pairs={{0,1},{1,0},{2,3},{3,2},{4,5},{5,4},{6,7},{7,6},{8,9},{9,8},{10,11... | collective-permute-start | bytes 6291464 | tf_op jit(solution)/shard_map/ppermute | solution.py:258
  8.7 2.7 %copy-start.1 = (s32[1,8]{1,0:T(1,128)S(1)}, s32[1,8]{1,0:T(1,128)}, u32[]{:S(2)}) copy-start(s32[1,8]{1,0:T(1,128)} %cols.5) | copy-start | bytes 100
  9.5 15.8 %collective-permute-start.1 = (bf16[1296,128]{1,0:T(8,128)(2,1)S(1)}, bf16[1296,128]{1,0:T(8,128)(2,1)S(1)}, u32[]{:S(2)}, u32[]{:S(2)}) collective-permute-start(bf16[1296,128]{1,0:T(8,128)(2,1)S(1)} %get-tuple-element.18), channel_id=1, source_target_pairs={{1,258},{2,257},{3,260},{4,259},{5,262},{6,261},{7,264},{8,263},{9... | collective-permute-start | bytes 995336 | tf_op jit(solution)/shard_map/ppermute | solution.py:261
  11.5 8.2 %collective-permute-start.2 = (s32[1,8]{1,0:T(1,128)S(1)}, s32[1,8]{1,0:T(1,128)S(1)}, u32[]{:S(2)}, u32[]{:S(2)}) collective-permute-start(s32[1,8]{1,0:T(1,128)S(1)} %copy-done.1), channel_id=1, source_target_pairs={{0,256},{16,272},{32,288},{48,304},{64,320},{80,336},{96,352},{112... | collective-permute-start | bytes 104 | tf_op jit(solution)/shard_map/ppermute | solution.py:262
  17.6 7.8 %copy-start = (bf16[1,8,256,256]{3,2,1,0:T(8,128)(2,1)S(1)}, bf16[1,8,256,256]{3,2,1,0:T(8,128)(2,1)}, u32[]{:S(2)}) copy-start(bf16[1,8,256,256]{3,2,1,0:T(8,128)(2,1)} %tiles.1) | copy-start | bytes 3145732
  17.6 10.1 %collective-permute-start.4 = (bf16[528,128]{1,0:T(8,128)(2,1)S(1)}, bf16[528,128]{1,0:T(8,128)(2,1)S(1)}, u32[]{:S(2)}, u32[]{:S(2)}) collective-permute-start(bf16[528,128]{1,0:T(8,128)(2,1)S(1)} %get-tuple-element.21), channel_id=1, source_target_pairs={{1,2},{2,1},{3,4},{4,3},{5,6},{6,5},{7,8},{8,7},{9,10},{10,9},{11,... | collective-permute-start | bytes 405512 | tf_op jit(solution)/shard_map/ppermute | solution.py:263
  20.5 14.0 %collective-permute-start.7 = (bf16[1296,128]{1,0:T(8,128)(2,1)S(1)}, bf16[1296,128]{1,0:T(8,128)(2,1)S(1)}, u32[]{:S(2)}, u32[]{:S(2)}) collective-permute-start(bf16[1296,128]{1,0:T(8,128)(2,1)S(1)} %near_kernel.1), channel_id=1, source_target_pairs={{0,256},{16,272},{32,288},{48,304},{64,320},{80,336},{96,352},{112... | collective-permute-start | bytes 995336 | tf_op jit(solution)/shard_map/ppermute | solution.py:265
  28.4 8.0 %collective-permute-start.6 = (bf16[272,128]{1,0:T(8,128)(2,1)S(1)}, bf16[272,128]{1,0:T(8,128)(2,1)S(1)}, u32[]{:S(2)}, u32[]{:S(2)}) collective-permute-start(bf16[272,128]{1,0:T(8,128)(2,1)S(1)} %get-tuple-element.23), channel_id=1, source_target_pairs={{0,256},{15,271},{16,272},{31,287},{32,288},{47,303},{48,304},{63,... | collective-permute-start | bytes 208904 | tf_op jit(solution)/shard_map/ppermute | solution.py:268
  29.1 8.4 %collective-permute-start.5 = (bf16[528,128]{1,0:T(8,128)(2,1)S(1)}, bf16[528,128]{1,0:T(8,128)(2,1)S(1)}, u32[]{:S(2)}, u32[]{:S(2)}) collective-permute-start(bf16[528,128]{1,0:T(8,128)(2,1)S(1)} %get-tuple-element.22), channel_id=1, source_target_pairs={{0,256},{16,272},{32,288},{48,304},{64,320},{80,336},{96,352},{112... | collective-permute-start | bytes 405512 | tf_op jit(solution)/shard_map/ppermute | solution.py:267
